TPU v7x, 32 devices: a whole 2x2x4 slice. The times are simulated.
32 devices in a mesh: lon: 8 (over z, y), lat: 4 (over x, core).
Axes of the slice: x: 2, y: 2, z: 4, core: 2. Of those that a mesh axis runs over, the one named last changes fastest.
Arguments:
- height: float32 [1024, 128, 512], P(None, 'lon', 'lat'), may hold values from -1 to 1
- land_sea: int32 [128, 512], P('lon', 'lat'), may hold values 0 or 1
- patterns: bfloat16 [512, 2, 128, 512], P(None, None, 'lon', 'lat'), may hold values from -0.0234375 to 0.0234375
Outputs:
- covariance: float32 [8, 512, 512], P('lon', 'lat')
All inputs are finite; a program needn't handle non-finite values. No bound on the sum of `land_sea` on one device may be relied on, other than what follows from the above.
Results may differ from a plain program's by a relative error of at most 0.0003.
The roundings to bfloat16 on the way count: a program that leaves them out, or rounds other values in their place, can miss the bound.
Values sent between devices are 32-bit elements; how exact they have to be, the bound alone decides.
No kernel may reach another device: no remote copies, remote signals or barrier semaphores. Data moves between devices by JAX's collectives and lax.ppermute only.
A program may use at most 128 MiB of HBM per device.

v0:
```python
import math

import jax
import jax.numpy as jnp
from jax import lax
from jax.sharding import PartitionSpec as P

LAG_DEV = 1


GRAVITY = 9.81
ROTATION = 7.2921e-05
EARTH_RADIUS = 6371000.0
LAT_SOUTH = 20.0
LAT_SPAN = 45.0
LON_STEP = 1.0 / 12.0


def padded_2(shard, sides, width):
    for axis, dim in sides:
        devices, length = (lax.axis_size(axis), shard.shape[dim])
        up = [(i, (i + 1) % devices) for i in range(devices - 1)]
        down = [(j, i) for i, j in up]
        last = lax.slice_in_dim(shard, length - width, length, axis=dim)
        initial = lax.slice_in_dim(shard, 0, width, axis=dim)
        before = lax.ppermute(last, axis, up)
        after = lax.ppermute(initial, axis, down)
        shard = jnp.concatenate([before, shard, after], axis=dim)
    return shard


def stencil_coefs(rows_index, total_rows):
    degrees = LAT_SOUTH + LAT_SPAN * (rows_index.astype(jnp.float32) + 0.5) / total_rows
    radians = degrees * (math.pi / 180.0)
    coriolis = 2.0 * ROTATION * jnp.sin(radians)
    north_step = EARTH_RADIUS * (LAT_SPAN / total_rows) * (math.pi / 180.0)
    east_step = EARTH_RADIUS * jnp.cos(radians) * (LON_STEP * math.pi / 180.0)
    return (-GRAVITY / (coriolis * 2.0 * north_step), GRAVITY / (coriolis * 2.0 * east_step))


def velocities(padded, coef_east, coef_north, ocean):
    lat_diff = padded[:, 1:-1, 2:] - padded[:, 1:-1, :-2]
    lon_diff = padded[:, 2:, 1:-1] - padded[:, :-2, 1:-1]
    return (coef_east * lat_diff * ocean, coef_north * lon_diff * ocean)


def on_device(height, land_sea, patterns):
    days, lon_cells, lat_cells = height.shape
    lat_devices = lax.axis_size("lat")
    lon_devices = lax.axis_size("lon")
    total_rows = lat_cells * lat_devices
    lat_place = lax.axis_index("lat")
    lon_place = lax.axis_index("lon")
    rows_index = lat_place * lat_cells + jnp.arange(lat_cells, dtype=jnp.int32)
    coef_east, coef_north = stencil_coefs(rows_index, total_rows)
    ocean = land_sea.astype(jnp.float32)
    padded = padded_2(height, (("lon", 1), ("lat", 2)), 1)
    east_vel, north_vel = velocities(padded, coef_east, coef_north, ocean)
    local_energy = jnp.sum(east_vel * east_vel + north_vel * north_vel)
    stacked = (
        jnp.stack([east_vel, north_vel], axis=1)
        .astype(jnp.bfloat16)
        .reshape(days, 2 * lon_cells * lat_cells)
    )
    mode_count = patterns.shape[0]
    owned = mode_count // lat_devices
    flat_patterns = patterns.reshape(mode_count, 2 * lon_cells * lat_cells)
    energy = lax.psum(local_energy, ("lon", "lat"))
    totals = lax.psum(
        lax.dot_general(
            flat_patterns, stacked, (((1,), (1,)), ((), ())), preferred_element_type=jnp.float32
        ),
        ("lon", "lat"),
    )
    cell_total = 2.0 * days * lon_cells * lon_devices * total_rows
    centered = totals - jnp.mean(totals, axis=1, keepdims=True)
    normed = centered / jnp.sqrt(energy / cell_total + 1e-06)
    my_rows = lax.dynamic_slice_in_dim(normed, lat_place * owned, owned, 0)
    padded_rows = jnp.concatenate([my_rows, jnp.zeros_like(my_rows)], axis=1)
    lag = lon_place * LAG_DEV + 0
    shifted = lax.dynamic_slice_in_dim(padded_rows, lag, days, 1)
    product = lax.dot_general(
        shifted,
        normed,
        (((1,), (1,)), ((), ())),
        precision=lax.Precision.HIGHEST,
        preferred_element_type=jnp.float32,
    )
    results = [product / (days - lag).astype(jnp.float32)]
    return jnp.stack(results, axis=0)


def solution(mesh):
    placed = (P(None, "lon", "lat"), P("lon", "lat"), P(None, None, "lon", "lat"))
    return jax.shard_map(
        on_device, mesh=mesh, in_specs=placed, out_specs=P("lon", "lat", None), check_vma=False
    )
```

profile of v0, /device:TPU:0, one launch (start us, length us, event | category | flops | bytes accessed | tf_op | source)
XLA Modules:
  0.0 259.3 jit_solution(2457111199029538386)
XLA Ops:
  6.5 0.0 copy-start.2
  6.5 0.0 all-reduce.3.cloned.1.call-start
  6.5 6.1 %copy.10 = f32[1024,16,128]{2,0,1:T(8,128)S(1)} copy(f32[1024,16,128]{2,1,0:T(8,128)} %param.3) | data formatting | bytes 16777216 | tf_op args[0]
  12.6 0.0 copy-start.1
  12.6 3.3 %copy-done.1 = f32[1024,16,128]{2,0,1:T(8,128)} copy-done((f32[1024,16,128]{2,0,1:T(8,128)}, f32[1024,16,128]{2,0,1:T(8,128)S(1)}, u32[]{:S(2)}) %copy-start.1) | copy-done | bytes 8388632
  15.9 0.1 fusion.23
  16.0 4.9 %collective-permute-start = (f32[1024,1,128]{2,0,1:T(8,128)S(1)}, f32[1024,1,128]{2,0,1:T(8,128)S(1)}, u32[]{:S(2)}, u32[]{:S(2)}) collective-permute-start(f32[1024,1,128]{2,0,1:T(8,128)S(1)} %get-tuple-element.11), channel_id=1, source_target_pairs={{0,4},{4,8},{8,12},{12,16},{16,20},{20,24},{24,28},{1,5},{5,9},{9,... | collective-permute-start | bytes 1572872 | tf_op jit(solution)/shard_map/ppermute | solution.py:26
  20.9 1.3 collective-permute-start.1
  22.2 0.0 copy-done.2
  22.2 21.0 %collective-permute-done = f32[1024,1,128]{2,0,1:T(8,128)S(1)} collective-permute-done((f32[1024,1,128]{2,0,1:T(8,128)S(1)}, f32[1024,1,128]{2,0,1:T(8,128)S(1)}, u32[]{:S(2)}, u32[]{:S(2)}) %collective-permute-start) | collective-permute-done | bytes 524320 | tf_op jit(solution)/shard_map/ppermute | solution.py:26
  43.3 5.8 %constant_dynamic-update-slice_fusion.1 = f32[1024,18,128]{2,0,1:T(8,128)S(1)} fusion(f32[1024,18,128]{2,0,1:T(8,128)S(1)} %constant_dynamic-update-slice_fusion.2, f32[1024,16,128]{2,1,0:T(8,128)} %param.3), kind=kLoop, calls=%fused_computation.24 | loop fusion | bytes 16777216
  49.1 0.0 collective-permute-done.1
  49.2 0.0 copy-start
  49.2 8.4 %fusion.22 = (f32[1024,18,1]{2,0,1:T(8,128)}, f32[1024,18,1]{2,0,1:T(8,128)}) fusion(f32[1024,18,128]{2,0,1:T(8,128)S(1)} %constant_dynamic-update-slice_fusion), kind=kLoop, calls=%fused_computation.35 | loop fusion | bytes 294912 | tf_op jit(solution)/shard_map/slice | solution.py:25
  57.6 0.9 copy-done
  58.5 5.6 %copy.13 = f32[1024,18,1]{0,2,1:T(1,128)S(1)} copy(f32[1024,18,1]{2,0,1:T(8,128)} %get-tuple-element.8) | data formatting | bytes 147456 | tf_op jit(solution)/shard_map/slice | solution.py:25
  64.1 1.3 collective-permute-start.2
  65.4 5.6 %copy.15 = f32[1024,18,1]{0,2,1:T(1,128)S(1)} copy(f32[1024,18,1]{2,0,1:T(8,128)} %get-tuple-element.9) | data formatting | bytes 147456 | tf_op jit(solution)/shard_map/slice | solution.py:24
  71.0 3.2 %collective-permute-start.3 = (f32[1024,18,1]{0,2,1:T(1,128)S(1)}, f32[1024,18,1]{0,2,1:T(1,128)S(1)}, u32[]{:S(2)}, u32[]{:S(2)}) collective-permute-start(f32[1024,18,1]{0,2,1:T(1,128)S(1)} %copy.15), channel_id=1, source_target_pairs={{0,1},{1,2},{2,3},{4,5},{5,6},{6,7},{8,9},{9,10},{10,11},{12,13},{... | collective-permute-start | bytes 221192 | tf_op jit(solution)/shard_map/ppermute | solution.py:26
  74.2 0.1 multiply_divide_fusion
  74.3 0.0 collective-permute-done.2
  74.3 5.1 %copy.14 = f32[1024,18,1]{2,0,1:T(8,128)} copy(f32[1024,18,1]{0,2,1:T(1,128)S(1)} %collective-permute-done.2) | data formatting | bytes 147456 | tf_op jit(solution)/shard_map/ppermute | solution.py:27
  79.4 0.0 collective-permute-done.3
  79.4 5.2 %copy.16 = f32[1024,18,1]{2,0,1:T(8,128)} copy(f32[1024,18,1]{0,2,1:T(1,128)S(1)} %collective-permute-done.3) | data formatting | bytes 147456 | tf_op jit(solution)/shard_map/ppermute | solution.py:26
  84.5 18.3 %add_reduce_fusion = (f32[]{:T(128)}, bf16[1024,16,128]{2,0,1:T(8,128)(2,1)S(1)}, bf16[1024,1,16,128]{3,0,2,1:T(8,128)(2,1)S(1)}) fusion(f32[16,128]{1,0:T(8,128)S(1)} %convert_element_type.18, f32[1024,16,128]{2,0,1:T(8,128)} %copy-done.1, f32[1024,1,128]{2,0,1:T(8,128)S(1)} %collective-permute-done, f32[1024,1,128]{2,0,1:T(8,128)S(1)} %collective-permute-done.1, ...), kind=kLoop, calls=%fused_computation.14 | loop fusion | flops 33554432 | bytes 27419652 | tf_op jit(solution)/shard_map/reduce_sum | solution.py:59
  102.8 8.1 %fusion.11 = f32[512,1024]{0,1:T(8,128)} fusion(bf16[512,2,16,128]{3,2,1,0:T(8,128)(2,1)} %param.5, bf16[1024,1,16,128]{3,0,2,1:T(8,128)(2,1)S(1)} %get-tuple-element.7, bf16[1024,1,16,128]{3,0,2,1:T(8,128)(2,1)S(1)} %bitcast.14), kind=kOutput, calls=%fused_computation.19 | convolution fusion | flops 4299161600 | bytes 14680064 | tf_op jit(solution)/shard_map/dot_general | solution.py:70
  110.9 0.0 all-reduce.3.cloned.1.call-update
  111.0 42.0 %psum.15 = f32[]{:T(128)} all-reduce(f32[]{:T(128)} %get-tuple-element.5), channel_id=1, replica_groups=mesh['lon'=8,'lat'=4] {'lon','lat'}, use_global_device_ids=true, to_apply=%region_3.0 | all-reduce | flops 1 | bytes 8 | tf_op jit(solution)/shard_map/psum | solution.py:68
  153.6 92.9 %all-reduce.3.cloned.1.call-done = f32[512,1024]{0,1:T(8,128)} async-done(((f32[512,1024]{0,1:T(8,128)}), f32[512,1024]{0,1:T(8,128)}) %all-reduce.3.cloned.1.call-update) | async-done | bytes 2097168 | tf_op jit(solution)/shard_map/psum | solution.py:69
  246.5 1.8 reduce_sum.18
  248.3 1.9 subtract_divide_fusion
  250.2 0.1 constant_dynamic-slice_fusion
  250.3 2.2 fusion.16
  (4 shorter events, 0.1 us)
Async XLA Ops:
  6.5 15.7 %copy-start.2 = (s32[16,128]{1,0:T(8,128)S(1)}, s32[16,128]{1,0:T(8,128)}, u32[]{:S(2)}) copy-start(s32[16,128]{1,0:T(8,128)} %param.4) | copy-start | bytes 24580
  6.5 240.0 %all-reduce.3.cloned.1.call-start = ((), (), s32[]{:S(2)}) async-start(), calls=%async_computation | async-start | bytes 4194304 | tf_op jit(solution)/shard_map/psum | solution.py:69
  12.6 3.3 %copy-start.1 = (f32[1024,16,128]{2,0,1:T(8,128)}, f32[1024,16,128]{2,0,1:T(8,128)S(1)}, u32[]{:S(2)}) copy-start(f32[1024,16,128]{2,0,1:T(8,128)S(1)} %copy.10) | copy-start | bytes 25165828
  16.0 27.3 %collective-permute-start = (f32[1024,1,128]{2,0,1:T(8,128)S(1)}, f32[1024,1,128]{2,0,1:T(8,128)S(1)}, u32[]{:S(2)}, u32[]{:S(2)}) collective-permute-start(f32[1024,1,128]{2,0,1:T(8,128)S(1)} %get-tuple-element.11), channel_id=1, source_target_pairs={{0,4},{4,8},{8,12},{12,16},{16,20},{20,24},{24,28},{1,5},{5,9},{9,... | collective-permute-start | bytes 1572872 | tf_op jit(solution)/shard_map/ppermute | solution.py:26
  20.9 28.2 %collective-permute-start.1 = (f32[1024,1,128]{2,0,1:T(8,128)S(1)}, f32[1024,1,128]{2,0,1:T(8,128)S(1)}, u32[]{:S(2)}, u32[]{:S(2)}) collective-permute-start(f32[1024,1,128]{2,0,1:T(8,128)S(1)} %get-tuple-element.10), channel_id=1, source_target_pairs={{4,0},{8,4},{12,8},{16,12},{20,16},{24,20},{28,24},{5,1},{9,5},{13... | collective-permute-start | bytes 1572872 | tf_op jit(solution)/shard_map/ppermute | solution.py:27
  49.2 9.3 %copy-start = (f32[1024,18,128]{2,0,1:T(8,128)}, f32[1024,18,128]{2,0,1:T(8,128)S(1)}, u32[]{:S(2)}) copy-start(f32[1024,18,128]{2,0,1:T(8,128)S(1)} %constant_dynamic-update-slice_fusion) | copy-start | bytes 28311556
  64.1 10.2 %collective-permute-start.2 = (f32[1024,18,1]{0,2,1:T(1,128)S(1)}, f32[1024,18,1]{0,2,1:T(1,128)S(1)}, u32[]{:S(2)}, u32[]{:S(2)}) collective-permute-start(f32[1024,18,1]{0,2,1:T(1,128)S(1)} %copy.13), channel_id=1, source_target_pairs={{1,0},{2,1},{3,2},{5,4},{6,5},{7,6},{9,8},{10,9},{11,10},{13,12},{... | collective-permute-start | bytes 221192 | tf_op jit(solution)/shard_map/ppermute | solution.py:27
  71.0 8.4 %collective-permute-start.3 = (f32[1024,18,1]{0,2,1:T(1,128)S(1)}, f32[1024,18,1]{0,2,1:T(1,128)S(1)}, u32[]{:S(2)}, u32[]{:S(2)}) collective-permute-start(f32[1024,18,1]{0,2,1:T(1,128)S(1)} %copy.15), channel_id=1, source_target_pairs={{0,1},{1,2},{2,3},{4,5},{5,6},{6,7},{8,9},{9,10},{10,11},{12,13},{... | collective-permute-start | bytes 221192 | tf_op jit(solution)/shard_map/ppermute | solution.py:26
Sparse Core Ops, SparseCore 0:
  111.1 135.3 all-reduce.2
where the time goes:
time: 260 us; the launch traced here: 259 us
  waiting for transfers between devices  114 us (44%)
  local copies, waits for them, and re-layouts  46.1 us (18%)
  blocking collectives  42 us (16%)
  other arithmetic  22 us (8%)
  between operations  14.2 us (5%)
  starting transfers between devices  10.7 us (4%)
  matrix products  10.3 us (4%)
    psum x1, waiting for transfers between devices, on_device(): lax.psum(lax.dot_general(flat_patterns, stacked, (((1,), (1,)), ((), ()))...  92.9 us
    psum x1, blocking collectives, on_device(): energy = lax.psum(local_energy, ('lon', 'lat'))  42 us
    ppermute x2, waiting for transfers between devices, padded_2(): before = lax.ppermute(last, axis, up)  21 us
    reduce_sum x1, other arithmetic, on_device(): local_energy = jnp.sum(east_vel * east_vel + north_vel * north_vel)  18.3 us
    unnamed x9, local copies, waits for them, and re-layouts  16.1 us
    slice x3, local copies, waits for them, and re-layouts, padded_2(): initial = lax.slice_in_dim(shard, 0, width, axis=dim)  14.1 us
    ppermute x2, starting transfers between devices, padded_2(): before = lax.ppermute(last, axis, up)  8.12 us
    dot_general x1, matrix products, on_device(): lax.dot_general(flat_patterns, stacked, (((1,), (1,)), ((), ())), preferr...  8.1 us
  transfers between devices with their start and end apart: 5, of which 2 were waited for; matrix products, arithmetic and copies ran while one was open for 6% of the time, Pallas kernels for 0%

commit v1 on v0

v1 whole, which is shorter than its diff:
```python
import functools
import math

import jax
import jax.numpy as jnp
from jax import lax
from jax.experimental import pallas as pl
from jax.experimental.pallas import tpu as pltpu
from jax.sharding import PartitionSpec as P

GRAVITY = 9.81
ROTATION = 7.2921e-05
EARTH_RADIUS = 6371000.0
LAT_SOUTH = 20.0
LAT_SPAN = 45.0
LON_STEP = 1.0 / 12.0

F32 = jnp.float32
BF16 = jnp.bfloat16
BOTH = ("lon", "lat")
LANES = 128
TILE = 8
DAY_BLOCK = 256
SPLIT = 8
VMEM = pl.BlockSpec(memory_space=pltpu.VMEM)
SMEM = pl.BlockSpec(memory_space=pltpu.SMEM)
ANY = pl.BlockSpec(memory_space=pl.ANY)
NT = (((1,), (1,)), ((), ()))
NN = (((1,), (0,)), ((), ()))


def like(*shape, dtype=F32):
    return jax.ShapeDtypeStruct(shape, dtype)


def params(mib=48):
    return pltpu.CompilerParams(vmem_limit_bytes=mib << 20)


def stencil_coefs(rows_index, total_rows):
    degrees = LAT_SOUTH + LAT_SPAN * (rows_index.astype(F32) + 0.5) / total_rows
    radians = degrees * (math.pi / 180.0)
    coriolis = 2.0 * ROTATION * jnp.sin(radians)
    north_step = EARTH_RADIUS * (LAT_SPAN / total_rows) * (math.pi / 180.0)
    east_step = EARTH_RADIUS * jnp.cos(radians) * (LON_STEP * math.pi / 180.0)
    return (-GRAVITY / (coriolis * 2.0 * north_step), GRAVITY / (coriolis * 2.0 * east_step))


def edge_rows_kernel(chunks, height, *refs):
    outs, sems = refs[:-1], refs[-1]
    last = height.shape[1] - 1
    copies = []
    for at, (start, size) in enumerate(chunks):
        for side, row in enumerate((0, last)):
            copies.append(
                pltpu.make_async_copy(
                    height.at[pl.ds(start, size), row, :], outs[2 * at + side], sems.at[2 * at + side]
                )
            )
    for copy in copies:
        copy.start()
    for copy in copies:
        copy.wait()


def edge_rows(height, chunks):
    lanes = height.shape[2]
    shapes = [like(size, lanes) for _, size in chunks for _ in range(2)]
    return pl.pallas_call(
        functools.partial(edge_rows_kernel, chunks),
        out_shape=shapes,
        in_specs=[ANY],
        out_specs=[VMEM] * len(shapes),
        scratch_shapes=[pltpu.SemaphoreType.DMA((len(shapes),))],
    )(height)


def interior_kernel(
    order, height, coefs, patterns,
    totals, energy, near_rows, edge_cols, row_patterns, col_patterns,
    flat, velocity,
):
    cells, lanes = coefs.shape[1:]
    days = height.shape[0] // cells
    modes = patterns.shape[0]
    north_at = cells * lanes
    block = modes // SPLIT
    group_days = lanes // 4
    size = 16 * cells
    step = pl.program_id(0)
    to, source = (lax.broadcasted_iota(jnp.int32, (size, size), dim) for dim in (0, 1))
    swap = ((to // 16 == source % cells) & (to % 16 == source // cells)).astype(BF16)

    @pl.when(step == 0)
    def _():
        energy[...] = jnp.zeros_like(energy)

        @pl.loop(0, modes // 16, unroll=8)
        def _(group):
            at = group * 16
            source_row = order[at // block] * block + at % block
            both = jnp.concatenate(
                [
                    patterns[pl.ds(source_row, 16), side].reshape(size, lanes)
                    for side in range(2)
                ],
                axis=1,
            )
            moved = lax.dot_general(swap, both, NN, preferred_element_type=F32).astype(BF16)
            here = pl.ds(pl.multiple_of(at, 16), 16)
            for cell in range(cells):
                rows = slice(cell * 16, cell * 16 + 16)
                flat[here, cell * lanes : (cell + 1) * lanes] = moved[rows, :lanes]
                north = moved[rows, lanes:]
                if cell == 0:
                    row_patterns[here, :lanes] = north
                elif cell == cells - 1:
                    row_patterns[here, lanes:] = north
                else:
                    place = north_at + (cell - 1) * lanes
                    flat[here, place : place + lanes] = north

        width = 2 * cells
        place, column = (lax.broadcasted_iota(jnp.int32, (cells * lanes, width), d) for d in (0, 1))
        wanted = (column % cells) * lanes + (column // cells) * (lanes - 1)
        pick = (place == wanted).astype(BF16)
        col_patterns[...] = lax.dot_general(
            flat[:, :north_at], pick, NN, preferred_element_type=F32
        ).astype(BF16)

    lane = lax.broadcasted_iota(jnp.int32, (TILE, lanes), 1)
    row = lax.broadcasted_iota(jnp.int32, (TILE, lanes), 0)
    inner = (lane > 0) & (lane < lanes - 1)
    east_coefs = [jnp.where(inner, coefs[0, at : at + TILE, :], 0.0) for at in (0, TILE)]
    north_coefs = [coefs[1, 1 : 1 + TILE, :], jnp.where(row < 2, 0.0, coefs[1, 7 : 7 + TILE, :])]

    def some_days(group, gathered):
        gathered = list(gathered)
        total = jnp.zeros((TILE, lanes), F32)
        easts, norths = [], []
        for day in range(16):
            base = pl.multiple_of((group * 16 + day) * cells, cells)
            halves = [height[pl.ds(base + at, TILE), :] for at in (0, TILE)]
            inside = [height[pl.ds(base + at, TILE), :] for at in (2, 6)]
            diffs = [inside[0] - halves[0], halves[1] - inside[1]]
            for side in range(2):
                plane = halves[side]
                east = pltpu.roll(plane, lanes - 1, 1) - pltpu.roll(plane, 1, 1)
                east = east * east_coefs[side]
                north = diffs[side] * north_coefs[side]
                total = total + east * east + north * north
                easts.append(east)
                norths.append(north)
                place = (group % 2) * 16 + day
                turn = pltpu.roll(plane, 4 * place + 2, 1)
                gathered[side] = jnp.where(lane // 4 == place, turn, gathered[side])
        both = jnp.concatenate(
            [jnp.concatenate(easts).astype(BF16), jnp.concatenate(norths).astype(BF16)], axis=1
        )
        moved = lax.dot_general(swap, both, NN, preferred_element_type=F32).astype(BF16)
        here = pl.ds(pl.multiple_of(group * 16, 16), 16)
        for cell in range(cells):
            rows = slice(cell * 16, cell * 16 + 16)
            velocity[here, cell * lanes : (cell + 1) * lanes] = moved[rows, :lanes]
            if cell < TILE or cell > TILE + 1:
                place = north_at + (cell if cell < TILE else cell - 2) * lanes
                velocity[here, place : place + lanes] = moved[rows, lanes:]
        return gathered, total

    def two_groups(pair, carry):
        zero = jnp.zeros((TILE, lanes), F32)
        gathered, first = some_days(pair * 2, [zero, zero])
        gathered, second = some_days(pair * 2 + 1, gathered)
        energy[...] += first + second
        here = pl.ds(pl.multiple_of(pair * lanes, lanes), lanes)
        for side in range(2):
            edge_cols[side * TILE : (side + 1) * TILE, here] = gathered[side]
        return carry

    lax.fori_loop(0, days // group_days, two_groups, 0, unroll=4)
    for side, cell in enumerate((1, cells - 2)):
        near_rows[side] = height[pl.ds(cell, days, stride=cells), :]
    totals[...] = lax.dot_general(flat[...], velocity[...], NT, preferred_element_type=F32)


def interior(order, height, coefs, patterns):
    days, cells, lanes = height.shape
    modes = patterns.shape[0]
    depth = (2 * cells - 2) * lanes
    day = min(DAY_BLOCK, days)
    return pl.pallas_call(
        interior_kernel,
        grid=(days // day,),
        out_shape=[
            like(modes, days),
            like(TILE, lanes),
            like(2, days, lanes),
            like(cells, 4 * days),
            like(modes, 2 * lanes, dtype=BF16),
            like(modes, 2 * cells, dtype=BF16),
        ],
        in_specs=[
            SMEM,
            pl.BlockSpec((day * cells, lanes), lambda s: (s, 0)),
            pl.BlockSpec((2, cells, lanes), lambda s: (0, 0, 0)),
            pl.BlockSpec(
                patterns.shape, lambda s: (0, 0, 0, 0), pipeline_mode=pl.Buffered(1)
            ),
        ],
        out_specs=[
            pl.BlockSpec((modes, day), lambda s: (0, s)),
            pl.BlockSpec((TILE, lanes), lambda s: (0, 0)),
            pl.BlockSpec((2, day, lanes), lambda s: (0, s, 0)),
            pl.BlockSpec((cells, 4 * day), lambda s: (0, s)),
            pl.BlockSpec((modes, 2 * lanes), lambda s: (0, 0)),
            pl.BlockSpec((modes, 2 * cells), lambda s: (0, 0)),
        ],
        scratch_shapes=[
            pltpu.VMEM((modes, depth), BF16),
            pltpu.VMEM((day, depth), BF16),
        ],
        compiler_params=params(),
        cost_estimate=pl.CostEstimate(
            flops=2 * modes * depth * days, bytes_accessed=14 << 20, transcendentals=0
        ),
    )(order, height.reshape(days * cells, lanes), coefs, patterns)


def edge_kernel(
    with_energy, totals, before, after, near_rows, west, east, edge_cols, coefs, row_patterns,
    col_patterns, energy, keep, send,
):
    cells, lanes = coefs.shape[1:]
    days = totals.shape[1]
    low = (near_rows[0] - before[...]) * coefs[1, 0:1, :]
    high = (after[...] - near_rows[1]) * coefs[1, cells - 1 : cells, :]
    rows = jnp.concatenate([low.astype(BF16), high.astype(BF16)], axis=1)
    added = lax.dot_general(row_patterns[...], rows, NT, preferred_element_type=F32)
    four = lax.broadcasted_iota(jnp.int32, (cells, 4 * days), 1) % 4
    left = (edge_cols[...] - pltpu.roll(west[...], 2, 1)) * coefs[0, :, 0:1]
    right = (east[...] - pltpu.roll(edge_cols[...], 2, 1)) * coefs[0, :, lanes - 1 : lanes]
    both = jnp.where(four == 3, left, jnp.where(four == 2, right, 0.0))
    packed = both.astype(BF16)
    wide = 4 * lanes
    packed = jnp.concatenate([packed[:, at : at + wide] for at in range(0, 4 * days, wide)], axis=0)
    place, column = (lax.broadcasted_iota(jnp.int32, (wide, 2 * lanes), d) for d in (0, 1))
    pick = (place == 4 * (column % lanes) + 3 - column // lanes).astype(BF16)
    sides = lax.dot_general(packed, pick, NN, preferred_element_type=F32).astype(BF16)
    cols = jnp.concatenate(
        [
            jnp.concatenate([sides[at : at + cells, :lanes], sides[at : at + cells, lanes:]], axis=0)
            for at in range(0, sides.shape[0], cells)
        ],
        axis=1,
    )
    added = added + lax.dot_general(col_patterns[...], cols, NN, preferred_element_type=F32)
    summed = totals[...] + added
    half = keep.shape[0]
    keep[...] = summed[:half]
    send[:half, :] = summed[half:]
    squares = (low * low + high * high).reshape(-1, TILE, lanes).sum(axis=0)
    across = both * both
    for at in range(0, 4 * days, lanes):
        squares = squares + across[:, at : at + lanes].reshape(-1, TILE, lanes).sum(axis=0)
    send[half:, :] = jnp.zeros((TILE, send.shape[1]), F32)
    if with_energy:
        squares = squares + energy[...]
    send[half:, :lanes] = squares


def edge(chunk, with_energy, totals, before, after, near_rows, west, east, edge_cols, coefs,
         row_patterns, col_patterns, energy):
    start, size = chunk
    at = start // size
    modes = totals.shape[0]
    cells, lanes = coefs.shape[1:]
    half = modes // 2
    whole = lambda a: pl.BlockSpec(a.shape, lambda s: (0,) * a.ndim)
    cols = pl.BlockSpec((cells, 4 * size), lambda s: (0, at))
    return pl.pallas_call(
        functools.partial(edge_kernel, with_energy),
        grid=(1,),
        out_shape=[like(half, size), like(half + TILE, size)],
        in_specs=[
            pl.BlockSpec((modes, size), lambda s: (0, at)),
            whole(before),
            whole(after),
            pl.BlockSpec((2, size, lanes), lambda s: (0, at, 0)),
            cols,
            cols,
            cols,
            whole(coefs),
            whole(row_patterns),
            whole(col_patterns),
            whole(energy),
        ],
        out_specs=[
            pl.BlockSpec((half, size), lambda s: (0, 0)),
            pl.BlockSpec((half + TILE, size), lambda s: (0, 0)),
        ],
        compiler_params=params(),
    )(totals, before, after, near_rows, west, east, edge_cols, coefs, row_patterns, col_patterns,
      energy)


def covariance_kernel(cells_total, chunks, place, order, energy, *refs):
    parts, (out, full, high, low) = refs[:-4], refs[-4:]
    modes, days = full.shape
    block = modes // SPLIT
    per_chunk = len(parts) // len(chunks)
    for at, (start, size) in enumerate(chunks):
        position = 0
        for part in parts[at * per_chunk : (at + 1) * per_chunk]:
            for piece in range(part.shape[0] // block):
                to = pl.ds(pl.multiple_of(order[position] * block, block), block)
                full[to, start : start + size] = part[piece * block : (piece + 1) * block, :]
                position += 1
    centered = full[...] - jnp.sum(full[...], axis=1, keepdims=True) * (1.0 / days)
    full[...] = centered
    upper = centered.astype(BF16)
    high[...] = upper
    low[...] = (centered - upper.astype(F32)).astype(BF16)
    rows = out.shape[1]
    lag = place[1]
    mine = full[pl.ds(pl.multiple_of(place[0] * rows, rows), rows), :]
    mine = pltpu.roll(mine, days - lag, 1)
    day = lax.broadcasted_iota(jnp.int32, mine.shape, 1)
    mine = jnp.where(day < days - lag, mine, 0.0)
    mine_high = mine.astype(BF16)
    mine_low = (mine - mine_high.astype(F32)).astype(BF16)
    dot = lambda a, b: lax.dot_general(a, b, NT, preferred_element_type=F32)
    product = dot(mine_low, high[...]) + dot(mine_high, low[...]) + dot(mine_high, high[...])
    total = jnp.sum(energy[...], axis=(0, 1), keepdims=True)
    spread = total / cells_total + 1e-06
    out[0] = product / (spread * (days - lag).astype(F32))


def covariance(cells_total, chunks, rows, place, order, energy, parts):
    modes = SPLIT * parts[0].shape[0] // 2
    days = sum(size for _, size in chunks)
    return pl.pallas_call(
        functools.partial(covariance_kernel, cells_total, chunks),
        out_shape=like(1, rows, modes),
        in_specs=[SMEM, SMEM] + [VMEM] * (1 + len(parts)),
        out_specs=VMEM,
        scratch_shapes=[
            pltpu.VMEM((modes, days), F32),
            pltpu.VMEM((modes, days), BF16),
            pltpu.VMEM((modes, days), BF16),
        ],
        compiler_params=params(),
    )(place, order, energy, *parts)


def steps_of(devices):
    flips = [(1, 1), (2, 4), (4, 2)] + [(b, b) for b in (8 << i for i in range(30)) if b < devices]
    return [[(i, i ^ flip[i & 1]) for i in range(devices)] for flip in flips]


def block_order(index):
    core, first, second = index & 1, (index >> 1) & 1, (index >> 2) & 1
    order = []
    for position in range(SPLIT):
        near, here, there = position >> 2, (position >> 1) & 1, position & 1
        owner = core ^ near
        a = jnp.where(owner == 0, first ^ here, first ^ there)
        b = jnp.where(owner == 0, second ^ there, second ^ here)
        order.append(owner * 4 + a * 2 + b)
    return jnp.stack(order).astype(jnp.int32)


def reduced(keep, send, steps):
    half = keep.shape[0]
    extra = send[half:]
    for step in range(3):
        got = lax.ppermute(send, BOTH, steps[step])
        half = keep.shape[0]
        quarter = half // 2 if step < 2 else 0
        extra = extra + got[half:]
        send = jnp.concatenate([keep[quarter:] + got[quarter:half], extra], axis=0)
        keep = keep[:quarter] + got[:quarter]
    for step in steps[3:]:
        send = send + lax.ppermute(send, BOTH, step)
    return send


def gathered(own, steps):
    pair = jnp.concatenate([own, lax.ppermute(own, BOTH, steps[2])], axis=0)
    other = lax.ppermute(pair, BOTH, steps[1])
    return [pair, other, lax.ppermute(pair, BOTH, steps[0]), lax.ppermute(other, BOTH, steps[0])]


def on_device(height, land_sea, patterns):
    days, lon_cells, lat_cells = height.shape
    lat_devices = lax.axis_size("lat")
    lon_devices = lax.axis_size("lon")
    total_rows = lat_cells * lat_devices
    lat_place = lax.axis_index("lat")
    lon_place = lax.axis_index("lon")
    mode_count = patterns.shape[0]
    chunks = [(0, days)]
    steps = steps_of(lat_devices * lon_devices)
    up = [(i, i + 1) for i in range(lon_devices - 1)]
    down = [(j, i) for i, j in up]
    right = [(i, i + 1) for i in range(lat_devices - 1)]
    left = [(j, i) for i, j in right]

    edges = edge_rows(height, chunks)
    before = [lax.ppermute(edges[2 * i + 1], "lon", up) for i in range(len(chunks))]
    after = [lax.ppermute(edges[2 * i], "lon", down) for i in range(len(chunks))]

    rows_index = lat_place * lat_cells + jnp.arange(lat_cells, dtype=jnp.int32)
    coef_east, coef_north = stencil_coefs(rows_index, total_rows)
    ocean = land_sea.astype(F32)
    coefs = jnp.stack([coef_east * ocean, coef_north * ocean])
    order = block_order(lon_place * lat_devices + lat_place)
    totals, energy, near_rows, edge_cols, row_patterns, col_patterns = interior(
        order, height, coefs, patterns
    )
    west = lax.ppermute(edge_cols, "lat", right)
    east = lax.ppermute(edge_cols, "lat", left)

    parts = []
    for i, chunk in enumerate(chunks):
        last = i == len(chunks) - 1
        keep, send = edge(
            chunk, last, totals, before[i], after[i], near_rows, west, east, edge_cols, coefs,
            row_patterns, col_patterns, energy,
        )
        own = reduced(keep, send, steps)
        block = mode_count // SPLIT
        if last:
            energy = own[block:, :LANES]
            own = own[:block]
        parts.extend(gathered(own, steps))
    cells_total = 2.0 * days * lon_cells * lon_devices * total_rows
    place = jnp.stack([lat_place, lon_place]).astype(jnp.int32)
    return covariance(
        cells_total, chunks, mode_count // lat_devices, place, order, energy, parts
    )


def solution(mesh):
    placed = (P(None, "lon", "lat"), P("lon", "lat"), P(None, None, "lon", "lat"))
    return jax.shard_map(
        on_device, mesh=mesh, in_specs=placed, out_specs=P("lon", "lat", None), check_vma=False
    )
```

time: 260 us -> 106 us (0.41)
  waiting for transfers between devices: 114 us -> 48.4 us
  local copies, waits for them, and re-layouts: 46.1 us -> 1.45 us
  blocking collectives: 42 us -> 0 us
  Pallas kernels: 0 us -> 27.7 us
  other arithmetic: 22 us -> 0.61 us
  starting transfers between devices: 10.7 us -> 27.3 us
  between operations: 14.2 us -> 0.25 us
  matrix products: 10.3 us -> 0 us
    psum x1 -> x0, waiting for transfers between devices: 92.9 us -> none  [on_device(): lax.psum(lax.dot_general(flat_patterns, stacked, (((1,), (1,)), ((), ()))...]
    psum x1 -> x0, blocking collectives: 42 us -> none  [on_device(): energy = lax.psum(local_energy, ('lon', 'lat'))]
    pallas_call x0 -> x4, Pallas kernels: none -> 27.7 us  [the longest x1 19.7 us: interior(): pl.pallas_call(interior_kernel, grid=(days // day,), out_shape=[like(mode...]
    ppermute x4 -> x13, waiting for transfers between devices: 21 us -> 48.4 us  [the longest x2 17.3 us: reduced(): send = send + lax.ppermute(send, BOTH, step)]
    reduce_sum x2 -> x0, other arithmetic: 20.1 us -> none  [the longest x1 18.3 us: on_device(): local_energy = jnp.sum(east_vel * east_vel + north_vel * north_vel)]
    slice x4 -> x2, local copies, waits for them, and re-layouts: 19.7 us -> 0.02 us  [the longest x1 0.02 us: on_device(): own = own[:block]]
    ppermute x4 -> x13, starting transfers between devices: 10.7 us -> 27.3 us  [the longest x3 8.84 us: reduced(): got = lax.ppermute(send, BOTH, steps[step])]
    unnamed x9 -> x4, local copies, waits for them, and re-layouts: 16.1 us -> 1.33 us
  transfers between devices with their start and end apart: 5 -> 13, of which waited for: 2 -> 9; matrix products, arithmetic and copies ran while one was open for 6% -> 0% of each run, Pallas kernels for 0% -> 19%
where the time goes in v1:
time: 106 us
  waiting for transfers between devices  48.4 us (46%)
  Pallas kernels  27.7 us (26%)
  starting transfers between devices  27.3 us (26%)
  local copies, waits for them, and re-layouts  1.45 us (1%)
    pallas_call x1, Pallas kernels, interior(): pl.pallas_call(interior_kernel, grid=(days // day,), out_shape=[like(mode...  19.7 us
    ppermute x2, waiting for transfers between devices, reduced(): send = send + lax.ppermute(send, BOTH, step)  17.3 us
    ppermute x3, waiting for transfers between devices, reduced(): got = lax.ppermute(send, BOTH, steps[step])  14.5 us
    ppermute x3, starting transfers between devices, reduced(): got = lax.ppermute(send, BOTH, steps[step])  8.84 us
    ppermute x1, waiting for transfers between devices, gathered(): other = lax.ppermute(pair, BOTH, steps[1])  7.72 us
    ppermute x1, waiting for transfers between devices, gathered(): pair = jnp.concatenate([own, lax.ppermute(own, BOTH, steps[2])], axis=0)  5.85 us
    ppermute x2, starting transfers between devices, reduced(): send = send + lax.ppermute(send, BOTH, step)  5.83 us
    ppermute x1, starting transfers between devices, on_device(): lax.ppermute(edges[2 * i + 1], 'lon', up)  4.9 us
  transfers between devices with their start and end apart: 13, of which 9 were waited for; matrix products, arithmetic and copies ran while one was open for 0% of the time, Pallas kernels for 19%

profile of v1, /device:TPU:0, one launch (start us, length us, event | category | flops | bytes accessed | tf_op | source)
XLA Modules:
  0.0 105.7 jit_solution(10795015019632286376)
XLA Ops:
  0.0 0.0 copy-start.1
  0.0 2.2 %shard_map.38 = (f32[1024,128]{1,0:T(8,128)}, f32[1024,128]{1,0:T(8,128)}) custom-call(f32[1024,16,128]{2,1,0:T(8,128)} %height.1), custom_call_target="tpu_custom_call" | custom-call | tf_op jit(solution)/shard_map/pallas_call | solution.py:69
  2.2 4.9 %collective-permute-start = (f32[1024,128]{1,0:T(8,128)}, f32[1024,128]{1,0:T(8,128)S(1)}, u32[]{:S(2)}, u32[]{:S(2)}) collective-permute-start(f32[1024,128]{1,0:T(8,128)} %get-tuple-element.16), channel_id=1, source_target_pairs={{0,4},{4,8},{8,12},{12,16},{16,20},{20,24},{24,28},{1,5},{5,9},{9,... | collective-permute-start | bytes 1572872 | tf_op jit(solution)/shard_map/ppermute | solution.py:409
  7.1 1.3 %collective-permute-start.1 = (f32[1024,128]{1,0:T(8,128)}, f32[1024,128]{1,0:T(8,128)S(1)}, u32[]{:S(2)}, u32[]{:S(2)}) collective-permute-start(f32[1024,128]{1,0:T(8,128)} %get-tuple-element.17), channel_id=1, source_target_pairs={{4,0},{8,4},{12,8},{16,12},{20,16},{24,20},{28,24},{5,1},{9,5},{13... | collective-permute-start | bytes 1572872 | tf_op jit(solution)/shard_map/ppermute | solution.py:410
  8.5 0.1 multiply_divide_fusion
  8.6 0.0 copy-done.1
  8.6 0.1 stack.56.order
  8.7 19.7 %shard_map.37 = (f32[512,1024]{1,0:T(8,128)S(1)}, f32[8,128]{1,0:T(8,128)S(1)}, f32[2,1024,128]{2,1,0:T(8,128)S(1)}, f32[16,4096]{1,0:T(8,128)S(1)}, bf16[512,25...) custom-call(s32[8]{0:T(128)S(1)} %stack.56.order, f32[16384,128]{1,0:T(8,128)} %bitcast.15, ...), custom_call_target="tpu_custom_call" | custom-call | flops 4026531840 | bytes 14680064 | tf_op jit(solution)/shard_map/pallas_call | solution.py:191
  28.4 0.0 copy-start
  28.4 1.3 %copy-done = f32[512,1024]{1,0:T(8,128)} copy-done((f32[512,1024]{1,0:T(8,128)}, f32[512,1024]{1,0:T(8,128)S(1)}, u32[]{:S(2)}) %copy-start) | copy-done | bytes 2097176
  29.7 1.3 %collective-permute-start.3 = (f32[16,4096]{1,0:T(8,128)S(1)}, f32[16,4096]{1,0:T(8,128)S(1)}, u32[]{:S(2)}, u32[]{:S(2)}) collective-permute-start(f32[16,4096]{1,0:T(8,128)S(1)} %get-tuple-element.19.edge_cols), channel_id=1, source_target_pairs={{1,0},{2,1},{3,2},{5,4},{6,5},{7,6},{9,8},{10,9},{11,10},{13,12},{... | collective-permute-start | bytes 786440 | tf_op jit(solution)/shard_map/ppermute | solution.py:421
  31.0 3.0 %collective-permute-start.2 = (f32[16,4096]{1,0:T(8,128)S(1)}, f32[16,4096]{1,0:T(8,128)S(1)}, u32[]{:S(2)}, u32[]{:S(2)}) collective-permute-start(f32[16,4096]{1,0:T(8,128)S(1)} %get-tuple-element.19.edge_cols), channel_id=1, source_target_pairs={{0,1},{1,2},{2,3},{4,5},{5,6},{6,7},{8,9},{9,10},{10,11},{12,13},{... | collective-permute-start | bytes 786440 | tf_op jit(solution)/shard_map/ppermute | solution.py:420
  34.1 0.0 collective-permute-done.3.east
  34.1 1.1 %collective-permute-done.2.west = f32[16,4096]{1,0:T(8,128)S(1)} collective-permute-done((f32[16,4096]{1,0:T(8,128)S(1)}, f32[16,4096]{1,0:T(8,128)S(1)}, u32[]{:S(2)}, u32[]{:S(2)}) %collective-permute-start.2) | collective-permute-done | bytes 262176 | tf_op jit(solution)/shard_map/ppermute | solution.py:420
  35.2 0.0 collective-permute-done.before
  35.2 0.0 collective-permute-done.1.after
  35.2 3.0 %shard_map.39 = (f32[256,1024]{1,0:T(8,128)S(1)}, f32[264,1024]{1,0:T(8,128)S(1)}) custom-call(f32[512,1024]{1,0:T(8,128)} %copy-done, f32[1024,128]{1,0:T(8,128)S(1)} %collective-permute-done.before, f32[1024,128]{1,0:T(8,128)S(1)} %collective-permute-done.1.after, f32[2,1024,128]{2,1,0:T(8,128)S(1)} %get-tuple-element.18.near_rows, ...), custom_call_target="tpu_custom_call" | custom-call | tf_op jit(solution)/shard_map/pallas_call | solution.py:280
  38.2 3.3 %collective-permute-start.4 = (f32[264,1024]{1,0:T(8,128)S(1)}, f32[264,1024]{1,0:T(8,128)S(1)}, u32[]{:S(2)}, u32[]{:S(2)}) collective-permute-start(f32[264,1024]{1,0:T(8,128)S(1)} %get-tuple-element.24), channel_id=1, source_target_pairs={{0,1},{1,0},{2,3},{3,2},{4,5},{5,4},{6,7},{7,6},{8,9},{9,8},{10,11... | collective-permute-start | bytes 3244040 | tf_op jit(solution)/shard_map/ppermute | solution.py:376
  41.5 2.3 %collective-permute-done.4 = f32[264,1024]{1,0:T(8,128)S(1)} collective-permute-done((f32[264,1024]{1,0:T(8,128)S(1)}, f32[264,1024]{1,0:T(8,128)S(1)}, u32[]{:S(2)}, u32[]{:S(2)}) %collective-permute-start.4) | collective-permute-done | bytes 1081376 | tf_op jit(solution)/shard_map/ppermute | solution.py:376
  43.8 0.2 slice_add_fusion.1
  44.1 2.8 %collective-permute-start.5 = (f32[136,1024]{1,0:T(8,128)S(1)}, f32[136,1024]{1,0:T(8,128)S(1)}, u32[]{:S(2)}, u32[]{:S(2)}) collective-permute-start(f32[136,1024]{1,0:T(8,128)S(1)} %pad_maximum_fusion), channel_id=1, source_target_pairs={{0,2},{1,5},{2,0},{3,7},{4,6},{5,1},{6,4},{7,3},{8,10},{9,13},{10,... | collective-permute-start | bytes 1671176 | tf_op jit(solution)/shard_map/ppermute | solution.py:376
  46.9 7.5 %collective-permute-done.5 = f32[136,1024]{1,0:T(8,128)S(1)} collective-permute-done((f32[136,1024]{1,0:T(8,128)S(1)}, f32[136,1024]{1,0:T(8,128)S(1)}, u32[]{:S(2)}, u32[]{:S(2)}) %collective-permute-start.5) | collective-permute-done | bytes 557088 | tf_op jit(solution)/shard_map/ppermute | solution.py:376
  54.5 2.7 %collective-permute-start.6 = (f32[72,1024]{1,0:T(8,128)S(1)}, f32[72,1024]{1,0:T(8,128)S(1)}, u32[]{:S(2)}, u32[]{:S(2)}) collective-permute-start(f32[72,1024]{1,0:T(8,128)S(1)} %pad_maximum_fusion.2), channel_id=1, source_target_pairs={{0,4},{1,3},{2,6},{3,1},{4,0},{5,7},{6,2},{7,5},{8,12},{9,11},{10,... | collective-permute-start | bytes 884744 | tf_op jit(solution)/shard_map/ppermute | solution.py:376
  57.2 4.7 %collective-permute-done.6 = f32[72,1024]{1,0:T(8,128)S(1)} collective-permute-done((f32[72,1024]{1,0:T(8,128)S(1)}, f32[72,1024]{1,0:T(8,128)S(1)}, u32[]{:S(2)}, u32[]{:S(2)}) %collective-permute-start.6) | collective-permute-done | bytes 294944 | tf_op jit(solution)/shard_map/ppermute | solution.py:376
  62.0 3.0 %collective-permute-start.7 = (f32[72,1024]{1,0:T(8,128)S(1)}, f32[72,1024]{1,0:T(8,128)S(1)}, u32[]{:S(2)}, u32[]{:S(2)}) collective-permute-start(f32[72,1024]{1,0:T(8,128)S(1)} %pad_maximum_fusion.3), channel_id=1, source_target_pairs={{0,8},{1,9},{2,10},{3,11},{4,12},{5,13},{6,14},{7,15},{8,0},{9,1},... | collective-permute-start | bytes 884744 | tf_op jit(solution)/shard_map/ppermute | solution.py:383
  65.0 5.9 %collective-permute-done.7 = f32[72,1024]{1,0:T(8,128)S(1)} collective-permute-done((f32[72,1024]{1,0:T(8,128)S(1)}, f32[72,1024]{1,0:T(8,128)S(1)}, u32[]{:S(2)}, u32[]{:S(2)}) %collective-permute-start.7) | collective-permute-done | bytes 294944 | tf_op jit(solution)/shard_map/ppermute | solution.py:383
  70.9 2.8 %collective-permute-start.8 = (f32[72,1024]{1,0:T(8,128)S(1)}, f32[72,1024]{1,0:T(8,128)S(1)}, u32[]{:S(2)}, u32[]{:S(2)}) collective-permute-start(f32[72,1024]{1,0:T(8,128)S(1)} %fusion.1), channel_id=1, source_target_pairs={{0,16},{1,17},{2,18},{3,19},{4,20},{5,21},{6,22},{7,23},{8,24},{9,... | collective-permute-start | bytes 884744 | tf_op jit(solution)/shard_map/ppermute | solution.py:383
  73.7 11.5 %collective-permute-done.8 = f32[72,1024]{1,0:T(8,128)S(1)} collective-permute-done((f32[72,1024]{1,0:T(8,128)S(1)}, f32[72,1024]{1,0:T(8,128)S(1)}, u32[]{:S(2)}, u32[]{:S(2)}) %collective-permute-start.8) | collective-permute-done | bytes 294944 | tf_op jit(solution)/shard_map/ppermute | solution.py:383
  85.2 0.6 collective-permute-start.9
  85.8 5.9 %collective-permute-done.9 = f32[64,1024]{1,0:T(8,128)S(1)} collective-permute-done((f32[64,1024]{1,0:T(8,128)S(1)}, f32[64,1024]{1,0:T(8,128)S(1)}, u32[]{:S(2)}, u32[]{:S(2)}) %collective-permute-start.9) | collective-permute-done | bytes 262176 | tf_op jit(solution)/shard_map/ppermute | solution.py:388
  91.7 1.5 %collective-permute-start.10 = (f32[128,1024]{1,0:T(8,128)S(1)}, f32[128,1024]{1,0:T(8,128)S(1)}, u32[]{:S(2)}, u32[]{:S(2)}) collective-permute-start(f32[128,1024]{1,0:T(8,128)S(1)} %pad_maximum_fusion.1.refs_0_), channel_id=1, source_target_pairs={{0,2},{1,5},{2,0},{3,7},{4,6},{5,1},{6,4},{7,3},{8,10},{9,13},{10,... | collective-permute-start | bytes 1572872 | tf_op jit(solution)/shard_map/ppermute | solution.py:389
  93.2 0.0 collective-permute-start.11
  93.3 7.7 %collective-permute-done.10.refs_1_ = f32[128,1024]{1,0:T(8,128)S(1)} collective-permute-done((f32[128,1024]{1,0:T(8,128)S(1)}, f32[128,1024]{1,0:T(8,128)S(1)}, u32[]{:S(2)}, u32[]{:S(2)}) %collective-permute-start.10) | collective-permute-done | bytes 524320 | tf_op jit(solution)/shard_map/ppermute | solution.py:389
  101.0 0.0 collective-permute-start.12
  101.0 0.1 pad_add_fusion.place
  101.1 0.0 collective-permute-done.11.refs_2_
  101.1 1.8 %collective-permute-done.12.refs_3_ = f32[128,1024]{1,0:T(8,128)S(1)} collective-permute-done((f32[128,1024]{1,0:T(8,128)S(1)}, f32[128,1024]{1,0:T(8,128)S(1)}, u32[]{:S(2)}, u32[]{:S(2)}) %collective-permute-start.12) | collective-permute-done | bytes 524320 | tf_op jit(solution)/shard_map/ppermute | solution.py:390
  102.9 2.9 %shard_map.40 = f32[1,128,512]{2,1,0:T(8,128)} custom-call(s32[2]{0:T(128)S(1)} %pad_add_fusion.place, s32[8]{0:T(128)S(1)} %stack.56.order, f32[8,128]{1,0:T(8,128)S(1)} %slice.70.energy, f32[128,1024]{1,0:T(8,128)S(1)} %pad_maximum_fusion.1.refs_0_, f32[128,1024]{1,0:T(8,128)S(1)} %collective-permute-done.10.refs_1_, ...), custom_call_target="tpu_custom_call" | custom-call | tf_op jit(solution)/shard_map/pallas_call | solution.py:341
  (15 shorter events, 0.3 us)
Async XLA Ops:
  0.0 8.6 %copy-start.1 = (s32[16,128]{1,0:T(8,128)S(1)}, s32[16,128]{1,0:T(8,128)}, u32[]{:S(2)}) copy-start(s32[16,128]{1,0:T(8,128)} %param.4) | copy-start | bytes 24580
  2.2 33.0 %collective-permute-start = (f32[1024,128]{1,0:T(8,128)}, f32[1024,128]{1,0:T(8,128)S(1)}, u32[]{:S(2)}, u32[]{:S(2)}) collective-permute-start(f32[1024,128]{1,0:T(8,128)} %get-tuple-element.16), channel_id=1, source_target_pairs={{0,4},{4,8},{8,12},{12,16},{16,20},{20,24},{24,28},{1,5},{5,9},{9,... | collective-permute-start | bytes 1572872 | tf_op jit(solution)/shard_map/ppermute | solution.py:409
  7.1 28.0 %collective-permute-start.1 = (f32[1024,128]{1,0:T(8,128)}, f32[1024,128]{1,0:T(8,128)S(1)}, u32[]{:S(2)}, u32[]{:S(2)}) collective-permute-start(f32[1024,128]{1,0:T(8,128)} %get-tuple-element.17), channel_id=1, source_target_pairs={{4,0},{8,4},{12,8},{16,12},{20,16},{24,20},{28,24},{5,1},{9,5},{13... | collective-permute-start | bytes 1572872 | tf_op jit(solution)/shard_map/ppermute | solution.py:410
  28.4 1.3 %copy-start = (f32[512,1024]{1,0:T(8,128)}, f32[512,1024]{1,0:T(8,128)S(1)}, u32[]{:S(2)}) copy-start(f32[512,1024]{1,0:T(8,128)S(1)} %get-tuple-element.15.totals) | copy-start | bytes 6291460
  29.7 4.3 %collective-permute-start.3 = (f32[16,4096]{1,0:T(8,128)S(1)}, f32[16,4096]{1,0:T(8,128)S(1)}, u32[]{:S(2)}, u32[]{:S(2)}) collective-permute-start(f32[16,4096]{1,0:T(8,128)S(1)} %get-tuple-element.19.edge_cols), channel_id=1, source_target_pairs={{1,0},{2,1},{3,2},{5,4},{6,5},{7,6},{9,8},{10,9},{11,10},{13,12},{... | collective-permute-start | bytes 786440 | tf_op jit(solution)/shard_map/ppermute | solution.py:421
  31.0 4.2 %collective-permute-start.2 = (f32[16,4096]{1,0:T(8,128)S(1)}, f32[16,4096]{1,0:T(8,128)S(1)}, u32[]{:S(2)}, u32[]{:S(2)}) collective-permute-start(f32[16,4096]{1,0:T(8,128)S(1)} %get-tuple-element.19.edge_cols), channel_id=1, source_target_pairs={{0,1},{1,2},{2,3},{4,5},{5,6},{6,7},{8,9},{9,10},{10,11},{12,13},{... | collective-permute-start | bytes 786440 | tf_op jit(solution)/shard_map/ppermute | solution.py:420
  38.2 5.7 %collective-permute-start.4 = (f32[264,1024]{1,0:T(8,128)S(1)}, f32[264,1024]{1,0:T(8,128)S(1)}, u32[]{:S(2)}, u32[]{:S(2)}) collective-permute-start(f32[264,1024]{1,0:T(8,128)S(1)} %get-tuple-element.24), channel_id=1, source_target_pairs={{0,1},{1,0},{2,3},{3,2},{4,5},{5,4},{6,7},{7,6},{8,9},{9,8},{10,11... | collective-permute-start | bytes 3244040 | tf_op jit(solution)/shard_map/ppermute | solution.py:376
  44.1 10.3 %collective-permute-start.5 = (f32[136,1024]{1,0:T(8,128)S(1)}, f32[136,1024]{1,0:T(8,128)S(1)}, u32[]{:S(2)}, u32[]{:S(2)}) collective-permute-start(f32[136,1024]{1,0:T(8,128)S(1)} %pad_maximum_fusion), channel_id=1, source_target_pairs={{0,2},{1,5},{2,0},{3,7},{4,6},{5,1},{6,4},{7,3},{8,10},{9,13},{10,... | collective-permute-start | bytes 1671176 | tf_op jit(solution)/shard_map/ppermute | solution.py:376
  54.5 7.4 %collective-permute-start.6 = (f32[72,1024]{1,0:T(8,128)S(1)}, f32[72,1024]{1,0:T(8,128)S(1)}, u32[]{:S(2)}, u32[]{:S(2)}) collective-permute-start(f32[72,1024]{1,0:T(8,128)S(1)} %pad_maximum_fusion.2), channel_id=1, source_target_pairs={{0,4},{1,3},{2,6},{3,1},{4,0},{5,7},{6,2},{7,5},{8,12},{9,11},{10,... | collective-permute-start | bytes 884744 | tf_op jit(solution)/shard_map/ppermute | solution.py:376
  62.0 8.9 %collective-permute-start.7 = (f32[72,1024]{1,0:T(8,128)S(1)}, f32[72,1024]{1,0:T(8,128)S(1)}, u32[]{:S(2)}, u32[]{:S(2)}) collective-permute-start(f32[72,1024]{1,0:T(8,128)S(1)} %pad_maximum_fusion.3), channel_id=1, source_target_pairs={{0,8},{1,9},{2,10},{3,11},{4,12},{5,13},{6,14},{7,15},{8,0},{9,1},... | collective-permute-start | bytes 884744 | tf_op jit(solution)/shard_map/ppermute | solution.py:383
  70.9 14.3 %collective-permute-start.8 = (f32[72,1024]{1,0:T(8,128)S(1)}, f32[72,1024]{1,0:T(8,128)S(1)}, u32[]{:S(2)}, u32[]{:S(2)}) collective-permute-start(f32[72,1024]{1,0:T(8,128)S(1)} %fusion.1), channel_id=1, source_target_pairs={{0,16},{1,17},{2,18},{3,19},{4,20},{5,21},{6,22},{7,23},{8,24},{9,... | collective-permute-start | bytes 884744 | tf_op jit(solution)/shard_map/ppermute | solution.py:383
  85.2 6.4 %collective-permute-start.9 = (f32[64,1024]{1,0:T(8,128)S(1)}, f32[64,1024]{1,0:T(8,128)S(1)}, u32[]{:S(2)}, u32[]{:S(2)}) collective-permute-start(f32[64,1024]{1,0:T(8,128)S(1)} %slice.71), channel_id=1, source_target_pairs={{0,4},{1,3},{2,6},{3,1},{4,0},{5,7},{6,2},{7,5},{8,12},{9,11},{10,... | collective-permute-start | bytes 786440 | tf_op jit(solution)/shard_map/ppermute | solution.py:388
  91.7 9.2 %collective-permute-start.10 = (f32[128,1024]{1,0:T(8,128)S(1)}, f32[128,1024]{1,0:T(8,128)S(1)}, u32[]{:S(2)}, u32[]{:S(2)}) collective-permute-start(f32[128,1024]{1,0:T(8,128)S(1)} %pad_maximum_fusion.1.refs_0_), channel_id=1, source_target_pairs={{0,2},{1,5},{2,0},{3,7},{4,6},{5,1},{6,4},{7,3},{8,10},{9,13},{10,... | collective-permute-start | bytes 1572872 | tf_op jit(solution)/shard_map/ppermute | solution.py:389
  93.2 7.8 %collective-permute-start.11 = (f32[128,1024]{1,0:T(8,128)S(1)}, f32[128,1024]{1,0:T(8,128)S(1)}, u32[]{:S(2)}, u32[]{:S(2)}) collective-permute-start(f32[128,1024]{1,0:T(8,128)S(1)} %pad_maximum_fusion.1.refs_0_), channel_id=1, source_target_pairs={{0,1},{1,0},{2,3},{3,2},{4,5},{5,4},{6,7},{7,6},{8,9},{9,8},{10,11... | collective-permute-start | bytes 1572872 | tf_op jit(solution)/shard_map/ppermute | solution.py:390
  101.0 1.9 %collective-permute-start.12 = (f32[128,1024]{1,0:T(8,128)S(1)}, f32[128,1024]{1,0:T(8,128)S(1)}, u32[]{:S(2)}, u32[]{:S(2)}) collective-permute-start(f32[128,1024]{1,0:T(8,128)S(1)} %collective-permute-done.10.refs_1_), channel_id=1, source_target_pairs={{0,1},{1,0},{2,3},{3,2},{4,5},{5,4},{6,7},{7,6},{8,9},{9,8},{10,11... | collective-permute-start | bytes 1572872 | tf_op jit(solution)/shard_map/ppermute | solution.py:390

commit v2 on v1

--- a/solution.py
+++ b/solution.py
@@ -21,7 +21,8 @@
 LANES = 128
 TILE = 8
 DAY_BLOCK = 256
-SPLIT = 8
+SCATTERS = 4
+SPLIT = 2**SCATTERS
 VMEM = pl.BlockSpec(memory_space=pltpu.VMEM)
 SMEM = pl.BlockSpec(memory_space=pltpu.SMEM)
 ANY = pl.BlockSpec(memory_space=pl.ANY)
@@ -33,7 +34,7 @@
     return jax.ShapeDtypeStruct(shape, dtype)
 
 
-def params(mib=48):
+def params(mib=24):
     return pltpu.CompilerParams(vmem_limit_bytes=mib << 20)
 
 
@@ -46,40 +47,32 @@
     return (-GRAVITY / (coriolis * 2.0 * north_step), GRAVITY / (coriolis * 2.0 * east_step))
 
 
-def edge_rows_kernel(chunks, height, *refs):
-    outs, sems = refs[:-1], refs[-1]
-    last = height.shape[1] - 1
-    copies = []
-    for at, (start, size) in enumerate(chunks):
-        for side, row in enumerate((0, last)):
-            copies.append(
-                pltpu.make_async_copy(
-                    height.at[pl.ds(start, size), row, :], outs[2 * at + side], sems.at[2 * at + side]
-                )
-            )
+def edge_rows_kernel(height, first, last, sems):
+    copies = [
+        pltpu.make_async_copy(height.at[:, row, :], to, sems.at[at])
+        for at, (row, to) in enumerate(((0, first), (height.shape[1] - 1, last)))
+    ]
     for copy in copies:
         copy.start()
     for copy in copies:
         copy.wait()
 
 
-def edge_rows(height, chunks):
-    lanes = height.shape[2]
-    shapes = [like(size, lanes) for _, size in chunks for _ in range(2)]
+def edge_rows(height):
+    days, _, lanes = height.shape
     return pl.pallas_call(
-        functools.partial(edge_rows_kernel, chunks),
-        out_shape=shapes,
+        edge_rows_kernel,
+        out_shape=[like(days, lanes)] * 2,
         in_specs=[ANY],
-        out_specs=[VMEM] * len(shapes),
-        scratch_shapes=[pltpu.SemaphoreType.DMA((len(shapes),))],
+        out_specs=[VMEM] * 2,
+        scratch_shapes=[pltpu.SemaphoreType.DMA((2,))],
     )(height)
 
 
-def interior_kernel(
-    order, height, coefs, patterns,
-    totals, energy, near_rows, edge_cols, row_patterns, col_patterns,
-    flat, velocity,
-):
+def interior_kernel(chunks, order, height, coefs, patterns_hbm, *refs):
+    totals, refs = refs[: len(chunks)], refs[len(chunks) :]
+    energy, near_rows, edge_cols, row_patterns, col_patterns, *refs = refs
+    patterns, flat, first, second, sem = refs
     cells, lanes = coefs.shape[1:]
     days = height.shape[0] // cells
     modes = patterns.shape[0]
@@ -91,10 +84,9 @@
     to, source = (lax.broadcasted_iota(jnp.int32, (size, size), dim) for dim in (0, 1))
     swap = ((to // 16 == source % cells) & (to % 16 == source // cells)).astype(BF16)
 
-    @pl.when(step == 0)
-    def _():
-        energy[...] = jnp.zeros_like(energy)
-
+    copy = pltpu.make_async_copy(patterns_hbm, patterns, sem)
+
+    def lay_out_patterns():
         @pl.loop(0, modes // 16, unroll=8)
         def _(group):
             at = group * 16
@@ -134,7 +126,7 @@
     east_coefs = [jnp.where(inner, coefs[0, at : at + TILE, :], 0.0) for at in (0, TILE)]
     north_coefs = [coefs[1, 1 : 1 + TILE, :], jnp.where(row < 2, 0.0, coefs[1, 7 : 7 + TILE, :])]
 
-    def some_days(group, gathered):
+    def some_days(velocity, group, gathered):
         gathered = list(gathered)
         total = jnp.zeros((TILE, lanes), F32)
         easts, norths = [], []
@@ -167,32 +159,63 @@
                 velocity[here, place : place + lanes] = moved[rows, lanes:]
         return gathered, total
 
-    def two_groups(pair, carry):
+    def two_groups(velocity, pair, carry):
         zero = jnp.zeros((TILE, lanes), F32)
-        gathered, first = some_days(pair * 2, [zero, zero])
-        gathered, second = some_days(pair * 2 + 1, gathered)
-        energy[...] += first + second
+        gathered, one = some_days(velocity, pair * 2, [zero, zero])
+        gathered, two = some_days(velocity, pair * 2 + 1, gathered)
+        energy[...] += one + two
         here = pl.ds(pl.multiple_of(pair * lanes, lanes), lanes)
         for side in range(2):
             edge_cols[side * TILE : (side + 1) * TILE, here] = gathered[side]
         return carry
 
-    lax.fori_loop(0, days // group_days, two_groups, 0, unroll=4)
-    for side, cell in enumerate((1, cells - 2)):
-        near_rows[side] = height[pl.ds(cell, days, stride=cells), :]
-    totals[...] = lax.dot_general(flat[...], velocity[...], NT, preferred_element_type=F32)
-
-
-def interior(order, height, coefs, patterns):
+    def work_out(velocity):
+        lax.fori_loop(
+            0, days // group_days, functools.partial(two_groups, velocity), 0, unroll=True
+        )
+        for side, cell in enumerate((1, cells - 2)):
+            near_rows[side] = height[pl.ds(cell, days, stride=cells), :]
+
+    def project(velocity, to):
+        to[...] = lax.dot_general(flat[...], velocity[...], NT, preferred_element_type=F32)
+
+    blocks = (chunks[-1][0] + chunks[-1][1]) // days
+    for at in range(blocks + 1):
+
+        @pl.when(step == at)
+        def _(at=at):
+            now, ago = (first, second) if at % 2 == 0 else (second, first)
+            if at == 0:
+                copy.start()
+                energy[...] = jnp.zeros_like(energy)
+            else:
+                day = (at - 1) * days
+                chunk = max(i for i, (start, _) in enumerate(chunks) if start <= day)
+                project(ago, totals[chunk])
+            if at < blocks:
+                work_out(now)
+            if at == 0:
+                copy.wait()
+                lay_out_patterns()
+
+
+def interior(chunks, order, height, coefs, patterns):
     days, cells, lanes = height.shape
     modes = patterns.shape[0]
     depth = (2 * cells - 2) * lanes
     day = min(DAY_BLOCK, days)
+    blocks = days // day
+    now = lambda s: jnp.minimum(s, blocks - 1)
+
+    def totals_spec(start, size):
+        index = lambda s: (0, jnp.clip(s - 1 - start // day, 0, size // day - 1))
+        return pl.BlockSpec((modes, day), index)
+
     return pl.pallas_call(
-        interior_kernel,
-        grid=(days // day,),
-        out_shape=[
-            like(modes, days),
+        functools.partial(interior_kernel, chunks),
+        grid=(blocks + 1,),
+        out_shape=[like(modes, size) for _, size in chunks]
+        + [
             like(TILE, lanes),
             like(2, days, lanes),
             like(cells, 4 * days),
@@ -201,25 +224,26 @@
         ],
         in_specs=[
             SMEM,
-            pl.BlockSpec((day * cells, lanes), lambda s: (s, 0)),
+            pl.BlockSpec((day * cells, lanes), lambda s: (now(s), 0)),
             pl.BlockSpec((2, cells, lanes), lambda s: (0, 0, 0)),
-            pl.BlockSpec(
-                patterns.shape, lambda s: (0, 0, 0, 0), pipeline_mode=pl.Buffered(1)
-            ),
-        ],
-        out_specs=[
-            pl.BlockSpec((modes, day), lambda s: (0, s)),
+            ANY,
+        ],
+        out_specs=[totals_spec(*chunk) for chunk in chunks]
+        + [
             pl.BlockSpec((TILE, lanes), lambda s: (0, 0)),
-            pl.BlockSpec((2, day, lanes), lambda s: (0, s, 0)),
-            pl.BlockSpec((cells, 4 * day), lambda s: (0, s)),
+            pl.BlockSpec((2, day, lanes), lambda s: (0, now(s), 0)),
+            pl.BlockSpec((cells, 4 * day), lambda s: (0, now(s))),
             pl.BlockSpec((modes, 2 * lanes), lambda s: (0, 0)),
             pl.BlockSpec((modes, 2 * cells), lambda s: (0, 0)),
         ],
         scratch_shapes=[
+            pltpu.VMEM(patterns.shape, BF16),
             pltpu.VMEM((modes, depth), BF16),
             pltpu.VMEM((day, depth), BF16),
-        ],
-        compiler_params=params(),
+            pltpu.VMEM((day, depth), BF16),
+            pltpu.SemaphoreType.DMA,
+        ],
+        compiler_params=params(48),
         cost_estimate=pl.CostEstimate(
             flops=2 * modes * depth * days, bytes_accessed=14 << 20, transcendentals=0
         ),
@@ -227,8 +251,8 @@
 
 
 def edge_kernel(
-    with_energy, totals, before, after, near_rows, west, east, edge_cols, coefs, row_patterns,
-    col_patterns, energy, keep, send,
+    last, place, totals, before, after, near_rows, paired, other, edge_cols, coefs, row_patterns,
+    col_patterns, energy, keep, send, *more,
 ):
     cells, lanes = coefs.shape[1:]
     days = totals.shape[1]
@@ -237,8 +261,11 @@
     rows = jnp.concatenate([low.astype(BF16), high.astype(BF16)], axis=1)
     added = lax.dot_general(row_patterns[...], rows, NT, preferred_element_type=F32)
     four = lax.broadcasted_iota(jnp.int32, (cells, 4 * days), 1) % 4
-    left = (edge_cols[...] - pltpu.roll(west[...], 2, 1)) * coefs[0, :, 0:1]
-    right = (east[...] - pltpu.roll(edge_cols[...], 2, 1)) * coefs[0, :, lanes - 1 : lanes]
+    even = place[0] % 2 == 0
+    west = jnp.where(even, other[...], paired[...])
+    east = jnp.where(even, paired[...], other[...])
+    left = (edge_cols[...] - pltpu.roll(west, 2, 1)) * coefs[0, :, 0:1]
+    right = (east - pltpu.roll(edge_cols[...], 2, 1)) * coefs[0, :, lanes - 1 : lanes]
     both = jnp.where(four == 3, left, jnp.where(four == 2, right, 0.0))
     packed = both.astype(BF16)
     wide = 4 * lanes
@@ -258,17 +285,18 @@
     half = keep.shape[0]
     keep[...] = summed[:half]
     send[:half, :] = summed[half:]
-    squares = (low * low + high * high).reshape(-1, TILE, lanes).sum(axis=0)
+    squares = energy[...] + (low * low + high * high).reshape(-1, TILE, lanes).sum(axis=0)
     across = both * both
     for at in range(0, 4 * days, lanes):
         squares = squares + across[:, at : at + lanes].reshape(-1, TILE, lanes).sum(axis=0)
-    send[half:, :] = jnp.zeros((TILE, send.shape[1]), F32)
-    if with_energy:
-        squares = squares + energy[...]
-    send[half:, :lanes] = squares
-
-
-def edge(chunk, with_energy, totals, before, after, near_rows, west, east, edge_cols, coefs,
+    if last:
+        send[half:, :] = jnp.zeros((TILE, send.shape[1]), F32)
+        send[half:, :lanes] = squares
+    else:
+        more[0][...] = squares
+
+
+def edge(chunk, last, place, totals, before, after, near_rows, paired, other, edge_cols, coefs,
          row_patterns, col_patterns, energy):
     start, size = chunk
     at = start // size
@@ -277,14 +305,18 @@
     half = modes // 2
     whole = lambda a: pl.BlockSpec(a.shape, lambda s: (0,) * a.ndim)
     cols = pl.BlockSpec((cells, 4 * size), lambda s: (0, at))
+    outs = [like(half, size), like(half + TILE * last, size)]
+    if not last:
+        outs.append(like(TILE, lanes))
     return pl.pallas_call(
-        functools.partial(edge_kernel, with_energy),
+        functools.partial(edge_kernel, last),
         grid=(1,),
-        out_shape=[like(half, size), like(half + TILE, size)],
+        out_shape=outs,
         in_specs=[
-            pl.BlockSpec((modes, size), lambda s: (0, at)),
-            whole(before),
-            whole(after),
+            SMEM,
+            whole(totals),
+            pl.BlockSpec((size, lanes), lambda s: (at, 0)),
+            pl.BlockSpec((size, lanes), lambda s: (at, 0)),
             pl.BlockSpec((2, size, lanes), lambda s: (0, at, 0)),
             cols,
             cols,
@@ -294,13 +326,10 @@
             whole(col_patterns),
             whole(energy),
         ],
-        out_specs=[
-            pl.BlockSpec((half, size), lambda s: (0, 0)),
-            pl.BlockSpec((half + TILE, size), lambda s: (0, 0)),
-        ],
+        out_specs=[whole(a) for a in outs],
         compiler_params=params(),
-    )(totals, before, after, near_rows, west, east, edge_cols, coefs, row_patterns, col_patterns,
-      energy)
+    )(place, totals, before, after, near_rows, paired, other, edge_cols, coefs, row_patterns,
+      col_patterns, energy)
 
 
 def covariance_kernel(cells_total, chunks, place, order, energy, *refs):
@@ -336,7 +365,7 @@
 
 
 def covariance(cells_total, chunks, rows, place, order, energy, parts):
-    modes = SPLIT * parts[0].shape[0] // 2
+    modes = 4 * parts[0].shape[0]
     days = sum(size for _, size in chunks)
     return pl.pallas_call(
         functools.partial(covariance_kernel, cells_total, chunks),
@@ -358,36 +387,37 @@
 
 
 def block_order(index):
-    core, first, second = index & 1, (index >> 1) & 1, (index >> 2) & 1
+    core, first, second, third = (index >> bit & 1 for bit in range(SCATTERS))
     order = []
     for position in range(SPLIT):
-        near, here, there = position >> 2, (position >> 1) & 1, position & 1
+        near, here, there, far = (position >> bit & 1 for bit in reversed(range(SCATTERS)))
         owner = core ^ near
         a = jnp.where(owner == 0, first ^ here, first ^ there)
         b = jnp.where(owner == 0, second ^ there, second ^ here)
-        order.append(owner * 4 + a * 2 + b)
+        order.append(owner * 8 + a * 4 + b * 2 + (third ^ far))
     return jnp.stack(order).astype(jnp.int32)
 
 
 def reduced(keep, send, steps):
-    half = keep.shape[0]
-    extra = send[half:]
-    for step in range(3):
+    for step in range(SCATTERS):
         got = lax.ppermute(send, BOTH, steps[step])
         half = keep.shape[0]
-        quarter = half // 2 if step < 2 else 0
-        extra = extra + got[half:]
-        send = jnp.concatenate([keep[quarter:] + got[quarter:half], extra], axis=0)
+        quarter = half // 2 if step < SCATTERS - 1 else 0
+        parts = [keep[quarter:] + got[quarter:half]]
+        if got.shape[0] > half:
+            parts.append(send[-TILE:] + got[half:])
+        send = jnp.concatenate(parts, axis=0)
         keep = keep[:quarter] + got[:quarter]
-    for step in steps[3:]:
+    for step in steps[SCATTERS:]:
         send = send + lax.ppermute(send, BOTH, step)
     return send
 
 
 def gathered(own, steps):
-    pair = jnp.concatenate([own, lax.ppermute(own, BOTH, steps[2])], axis=0)
-    other = lax.ppermute(pair, BOTH, steps[1])
-    return [pair, other, lax.ppermute(pair, BOTH, steps[0]), lax.ppermute(other, BOTH, steps[0])]
+    pair = jnp.concatenate([own, lax.ppermute(own, BOTH, steps[3])], axis=0)
+    four = jnp.concatenate([pair, lax.ppermute(pair, BOTH, steps[2])], axis=0)
+    other = lax.ppermute(four, BOTH, steps[1])
+    return [four, other, lax.ppermute(four, BOTH, steps[0]), lax.ppermute(other, BOTH, steps[0])]
 
 
 def on_device(height, land_sea, patterns):
@@ -398,43 +428,43 @@
     lat_place = lax.axis_index("lat")
     lon_place = lax.axis_index("lon")
     mode_count = patterns.shape[0]
-    chunks = [(0, days)]
+    chunks = [(0, days // 2), (days // 2, days // 2)]
     steps = steps_of(lat_devices * lon_devices)
     up = [(i, i + 1) for i in range(lon_devices - 1)]
     down = [(j, i) for i, j in up]
-    right = [(i, i + 1) for i in range(lat_devices - 1)]
-    left = [(j, i) for i, j in right]
-
-    edges = edge_rows(height, chunks)
-    before = [lax.ppermute(edges[2 * i + 1], "lon", up) for i in range(len(chunks))]
-    after = [lax.ppermute(edges[2 * i], "lon", down) for i in range(len(chunks))]
+
+    first, last = edge_rows(height)
+    before = lax.ppermute(last, "lon", up)
+    after = lax.ppermute(first, "lon", down)
 
     rows_index = lat_place * lat_cells + jnp.arange(lat_cells, dtype=jnp.int32)
     coef_east, coef_north = stencil_coefs(rows_index, total_rows)
     ocean = land_sea.astype(F32)
     coefs = jnp.stack([coef_east * ocean, coef_north * ocean])
+    place = jnp.stack([lat_place, lon_place]).astype(jnp.int32)
     order = block_order(lon_place * lat_devices + lat_place)
-    totals, energy, near_rows, edge_cols, row_patterns, col_patterns = interior(
-        order, height, coefs, patterns
+    *totals, energy, near_rows, edge_cols, row_patterns, col_patterns = interior(
+        chunks, order, height, coefs, patterns
     )
-    west = lax.ppermute(edge_cols, "lat", right)
-    east = lax.ppermute(edge_cols, "lat", left)
+    pairs = [[(i, i ^ 1) for i in range(lat_devices)]]
+    pairs.append([(i, ((i + 1) ^ 1) - 1) for i in range(1, lat_devices - 1)])
+    paired, other = (lax.ppermute(edge_cols, "lat", pair) for pair in pairs)
 
     parts = []
     for i, chunk in enumerate(chunks):
         last = i == len(chunks) - 1
-        keep, send = edge(
-            chunk, last, totals, before[i], after[i], near_rows, west, east, edge_cols, coefs,
-            row_patterns, col_patterns, energy,
+        keep, send, *more = edge(
+            chunk, last, place, totals[i], before, after, near_rows, paired, other, edge_cols,
+            coefs, row_patterns, col_patterns, energy,
         )
         own = reduced(keep, send, steps)
-        block = mode_count // SPLIT
         if last:
-            energy = own[block:, :LANES]
-            own = own[:block]
+            block = mode_count // SPLIT
+            own, energy = own[:block], own[block:, :LANES]
+        else:
+            energy = more[0]
         parts.extend(gathered(own, steps))
     cells_total = 2.0 * days * lon_cells * lon_devices * total_rows
-    place = jnp.stack([lat_place, lon_place]).astype(jnp.int32)
     return covariance(
         cells_total, chunks, mode_count // lat_devices, place, order, energy, parts
     )

time: 106 us -> 88.5 us (0.83)
  waiting for transfers between devices: 48.4 us -> 22.6 us
  starting transfers between devices: 27.3 us -> 41 us
  Pallas kernels: 27.7 us -> 23.6 us
  local copies, waits for them, and re-layouts: 1.45 us -> 0.11 us
    ppermute x2, waiting for transfers between devices: 17.3 us -> 3.13 us  [reduced(): send = send + lax.ppermute(send, BOTH, step)]
    ppermute x3 -> x8, waiting for transfers between devices: 14.5 us -> 5.38 us  [reduced(): got = lax.ppermute(send, BOTH, steps[step])]
    ppermute x3 -> x8, starting transfers between devices: 8.84 us -> 17 us  [reduced(): got = lax.ppermute(send, BOTH, steps[step])]
    ppermute x7 -> x12, starting transfers between devices: 12.6 us -> 18.8 us  [the longest x1 4.9 us: on_device(): before = lax.ppermute(last, 'lon', up)]
    pallas_call x3 -> x4, Pallas kernels: 24.9 us -> 20.8 us  [the longest x1 15.9 us: interior(): pl.pallas_call(functools.partial(interior_kernel, chunks), grid=(blocks +...]
    ppermute x7 -> x12, waiting for transfers between devices: 14.7 us -> 12.6 us  [the longest x2 4.37 us: gathered(): four = jnp.concatenate([pair, lax.ppermute(pair, BOTH, steps[2])], axis=0)]
    unnamed x4 -> x2, local copies, waits for them, and re-layouts: 1.33 us -> 0.01 us
  transfers between devices with their start and end apart: 13 -> 24, of which waited for: 9 -> 12; matrix products, arithmetic and copies ran while one was open for 0% -> 1% of each run, Pallas kernels for 19% -> 18%
where the time goes in v2:
time: 88.5 us; the launch traced here: 88.3 us
  starting transfers between devices  41 us (46%)
  Pallas kernels  23.6 us (27%)
  waiting for transfers between devices  22.6 us (26%)
    ppermute x8, starting transfers between devices, reduced(): got = lax.ppermute(send, BOTH, steps[step])  17 us
    pallas_call x1, Pallas kernels, interior(): pl.pallas_call(functools.partial(interior_kernel, chunks), grid=(blocks +...  15.9 us
    ppermute x8, waiting for transfers between devices, reduced(): got = lax.ppermute(send, BOTH, steps[step])  5.38 us
    ppermute x2, starting transfers between devices, reduced(): send = send + lax.ppermute(send, BOTH, step)  5.29 us
    ppermute x1, starting transfers between devices, on_device(): before = lax.ppermute(last, 'lon', up)  4.9 us
    ppermute x2, starting transfers between devices, gathered(): other = lax.ppermute(four, BOTH, steps[1])  4.56 us
    ppermute x2, waiting for transfers between devices, gathered(): four = jnp.concatenate([pair, lax.ppermute(pair, BOTH, steps[2])], axis=0)  4.37 us
    ppermute x2, waiting for transfers between devices, gathered(): other = lax.ppermute(four, BOTH, steps[1])  3.84 us
  transfers between devices with their start and end apart: 24, of which 12 were waited for; matrix products, arithmetic and copies ran while one was open for 1% of the time, Pallas kernels for 18%

profile of v2, /device:TPU:0, one launch (start us, length us, event | category | flops | bytes accessed | tf_op | source)
XLA Modules:
  0.0 88.3 jit_solution(3118524246488234110)
XLA Ops:
  0.0 0.0 copy-start
  0.0 2.2 %shard_map.38 = (f32[1024,128]{1,0:T(8,128)}, f32[1024,128]{1,0:T(8,128)}) custom-call(f32[1024,16,128]{2,1,0:T(8,128)} %height.1), custom_call_target="tpu_custom_call" | custom-call | tf_op jit(solution)/shard_map/pallas_call | solution.py:63
  2.2 4.9 %collective-permute-start = (f32[1024,128]{1,0:T(8,128)}, f32[1024,128]{1,0:T(8,128)S(1)}, u32[]{:S(2)}, u32[]{:S(2)}) collective-permute-start(f32[1024,128]{1,0:T(8,128)} %get-tuple-element.20), channel_id=1, source_target_pairs={{0,4},{4,8},{8,12},{12,16},{16,20},{20,24},{24,28},{1,5},{5,9},{9,... | collective-permute-start | bytes 1572872 | tf_op jit(solution)/shard_map/ppermute | solution.py:437
  7.2 1.3 %collective-permute-start.1 = (f32[1024,128]{1,0:T(8,128)}, f32[1024,128]{1,0:T(8,128)S(1)}, u32[]{:S(2)}, u32[]{:S(2)}) collective-permute-start(f32[1024,128]{1,0:T(8,128)} %get-tuple-element.21), channel_id=1, source_target_pairs={{4,0},{8,4},{12,8},{16,12},{20,16},{24,20},{28,24},{5,1},{9,5},{13... | collective-permute-start | bytes 1572872 | tf_op jit(solution)/shard_map/ppermute | solution.py:438
  8.5 0.1 multiply_divide_fusion
  8.6 0.0 copy-done
  8.6 0.1 stack.88.order
  8.7 15.9 %shard_map.37 = (f32[512,512]{1,0:T(8,128)S(1)}, f32[512,512]{1,0:T(8,128)S(1)}, f32[8,128]{1,0:T(8,128)S(1)}, f32[2,1024,128]{2,1,0:T(8,128)S(1)}, f32[16,4096]...) custom-call(s32[16]{0:T(128)S(1)} %stack.88.order, f32[16384,128]{1,0:T(8,128)} %bitcast.23, ...), custom_call_target="tpu_custom_call" | custom-call | flops 4026531840 | bytes 14680064 | tf_op jit(solution)/shard_map/pallas_call | solution.py:214
  24.6 0.9 collective-permute-start.3
  25.5 2.9 %collective-permute-start.2 = (f32[16,4096]{1,0:T(8,128)S(1)}, f32[16,4096]{1,0:T(8,128)S(1)}, u32[]{:S(2)}, u32[]{:S(2)}) collective-permute-start(f32[16,4096]{1,0:T(8,128)S(1)} %get-tuple-element.23.edge_cols), channel_id=1, source_target_pairs={{0,1},{1,0},{2,3},{3,2},{4,5},{5,4},{6,7},{7,6},{8,9},{9,8},{10,11... | collective-permute-start | bytes 786440 | tf_op jit(solution)/shard_map/ppermute | solution.py:451
  28.4 0.1 pad_add_fusion.place
  28.5 0.0 collective-permute-done.3.other
  28.5 1.1 %collective-permute-done.2.paired = f32[16,4096]{1,0:T(8,128)S(1)} collective-permute-done((f32[16,4096]{1,0:T(8,128)S(1)}, f32[16,4096]{1,0:T(8,128)S(1)}, u32[]{:S(2)}, u32[]{:S(2)}) %collective-permute-start.2) | collective-permute-done | bytes 262176 | tf_op jit(solution)/shard_map/ppermute | solution.py:451
  29.6 0.3 collective-permute-done.before
  29.8 0.0 collective-permute-done.1.after
  29.8 1.3 %shard_map.39 = (f32[256,512]{1,0:T(8,128)S(1)}, f32[256,512]{1,0:T(8,128)S(1)}, f32[8,128]{1,0:T(8,128)S(1)}) custom-call(s32[2]{0:T(128)S(1)} %pad_add_fusion.place, f32[512,512]{1,0:T(8,128)S(1)} %get-tuple-element.26.totals, f32[1024,128]{1,0:T(8,128)S(1)} %collective-permute-done.before, f32[1024,128]{1,0:T(8,128)S(1)} %collective-permute-done.1.after, ...), custom_call_target="tpu_custom_call" | custom-call | tf_op jit(solution)/shard_map/pallas_call | solution.py:311
  31.2 1.3 %shard_map.40 = (f32[256,512]{1,0:T(8,128)S(1)}, f32[264,512]{1,0:T(8,128)S(1)}) custom-call(s32[2]{0:T(128)S(1)} %pad_add_fusion.place, f32[512,512]{1,0:T(8,128)S(1)} %get-tuple-element.19.totals, f32[1024,128]{1,0:T(8,128)S(1)} %collective-permute-done.before, f32[1024,128]{1,0:T(8,128)S(1)} %collective-permute-done.1.after, ...), custom_call_target="tpu_custom_call" | custom-call | tf_op jit(solution)/shard_map/pallas_call | solution.py:311
  32.5 2.4 %collective-permute-start.4 = (f32[264,512]{1,0:T(8,128)S(1)}, f32[264,512]{1,0:T(8,128)S(1)}, u32[]{:S(2)}, u32[]{:S(2)}) collective-permute-start(f32[264,512]{1,0:T(8,128)S(1)} %get-tuple-element.30), channel_id=1, source_target_pairs={{0,1},{1,0},{2,3},{3,2},{4,5},{5,4},{6,7},{7,6},{8,9},{9,8},{10,11... | collective-permute-start | bytes 1622024 | tf_op jit(solution)/shard_map/ppermute | solution.py:403
  34.9 0.1 collective-permute-start.9
  35.0 1.5 %collective-permute-done.4 = f32[264,512]{1,0:T(8,128)S(1)} collective-permute-done((f32[264,512]{1,0:T(8,128)S(1)}, f32[264,512]{1,0:T(8,128)S(1)}, u32[]{:S(2)}, u32[]{:S(2)}) %collective-permute-start.4) | collective-permute-done | bytes 540704 | tf_op jit(solution)/shard_map/ppermute | solution.py:403
  36.5 0.1 slice_add_fusion.3
  36.6 2.1 %collective-permute-start.5 = (f32[136,512]{1,0:T(8,128)S(1)}, f32[136,512]{1,0:T(8,128)S(1)}, u32[]{:S(2)}, u32[]{:S(2)}) collective-permute-start(f32[136,512]{1,0:T(8,128)S(1)} %pad_maximum_fusion), channel_id=1, source_target_pairs={{0,2},{1,5},{2,0},{3,7},{4,6},{5,1},{6,4},{7,3},{8,10},{9,13},{10,... | collective-permute-start | bytes 835592 | tf_op jit(solution)/shard_map/ppermute | solution.py:403
  38.7 0.0 collective-permute-done.9
  38.7 0.1 slice_add_fusion.1
  38.8 0.6 collective-permute-start.10
  39.4 3.8 %collective-permute-done.5 = f32[136,512]{1,0:T(8,128)S(1)} collective-permute-done((f32[136,512]{1,0:T(8,128)S(1)}, f32[136,512]{1,0:T(8,128)S(1)}, u32[]{:S(2)}, u32[]{:S(2)}) %collective-permute-start.5) | collective-permute-done | bytes 278560 | tf_op jit(solution)/shard_map/ppermute | solution.py:403
  43.3 2.7 %collective-permute-start.6 = (f32[72,512]{1,0:T(8,128)S(1)}, f32[72,512]{1,0:T(8,128)S(1)}, u32[]{:S(2)}, u32[]{:S(2)}) collective-permute-start(f32[72,512]{1,0:T(8,128)S(1)} %pad_maximum_fusion.3), channel_id=1, source_target_pairs={{0,4},{1,3},{2,6},{3,1},{4,0},{5,7},{6,2},{7,5},{8,12},{9,11},{10,... | collective-permute-start | bytes 442376 | tf_op jit(solution)/shard_map/ppermute | solution.py:403
  46.0 0.0 collective-permute-done.10
  46.1 3.2 %collective-permute-start.11 = (f32[64,512]{1,0:T(8,128)S(1)}, f32[64,512]{1,0:T(8,128)S(1)}, u32[]{:S(2)}, u32[]{:S(2)}) collective-permute-start(f32[64,512]{1,0:T(8,128)S(1)} %get-tuple-element.40), channel_id=1, source_target_pairs={{0,4},{1,3},{2,6},{3,1},{4,0},{5,7},{6,2},{7,5},{8,12},{9,11},{10,... | collective-permute-start | bytes 393224 | tf_op jit(solution)/shard_map/ppermute | solution.py:403
  49.3 0.0 collective-permute-done.6
  49.3 2.9 %collective-permute-start.7 = (f32[40,512]{1,0:T(8,128)S(1)}, f32[40,512]{1,0:T(8,128)S(1)}, u32[]{:S(2)}, u32[]{:S(2)}) collective-permute-start(f32[40,512]{1,0:T(8,128)S(1)} %pad_maximum_fusion.6), channel_id=1, source_target_pairs={{0,8},{1,9},{2,10},{3,11},{4,12},{5,13},{6,14},{7,15},{8,0},{9,1},... | collective-permute-start | bytes 245768 | tf_op jit(solution)/shard_map/ppermute | solution.py:403
  52.2 0.0 collective-permute-done.11
  52.2 3.0 %collective-permute-start.12 = (f32[32,512]{1,0:T(8,128)S(1)}, f32[32,512]{1,0:T(8,128)S(1)}, u32[]{:S(2)}, u32[]{:S(2)}) collective-permute-start(f32[32,512]{1,0:T(8,128)S(1)} %slice_add_fusion.8), channel_id=1, source_target_pairs={{0,8},{1,9},{2,10},{3,11},{4,12},{5,13},{6,14},{7,15},{8,0},{9,1},... | collective-permute-start | bytes 196616 | tf_op jit(solution)/shard_map/ppermute | solution.py:403
  55.2 0.0 collective-permute-done.7
  55.3 3.2 %collective-permute-start.8 = (f32[40,512]{1,0:T(8,128)S(1)}, f32[40,512]{1,0:T(8,128)S(1)}, u32[]{:S(2)}, u32[]{:S(2)}) collective-permute-start(f32[40,512]{1,0:T(8,128)S(1)} %pad_maximum_fusion.7), channel_id=1, source_target_pairs={{0,16},{1,17},{2,18},{3,19},{4,20},{5,21},{6,22},{7,23},{8,24},{9,... | collective-permute-start | bytes 245768 | tf_op jit(solution)/shard_map/ppermute | solution.py:412
  58.4 0.0 collective-permute-done.12
  58.5 2.1 %collective-permute-start.13 = (f32[32,512]{1,0:T(8,128)S(1)}, f32[32,512]{1,0:T(8,128)S(1)}, u32[]{:S(2)}, u32[]{:S(2)}) collective-permute-start(f32[32,512]{1,0:T(8,128)S(1)} %fusion), channel_id=1, source_target_pairs={{0,16},{1,17},{2,18},{3,19},{4,20},{5,21},{6,22},{7,23},{8,24},{9,... | collective-permute-start | bytes 196616 | tf_op jit(solution)/shard_map/ppermute | solution.py:412
  60.6 3.1 %collective-permute-done.13 = f32[32,512]{1,0:T(8,128)S(1)} collective-permute-done((f32[32,512]{1,0:T(8,128)S(1)}, f32[32,512]{1,0:T(8,128)S(1)}, u32[]{:S(2)}, u32[]{:S(2)}) %collective-permute-start.13) | collective-permute-done | bytes 65568 | tf_op jit(solution)/shard_map/ppermute | solution.py:412
  63.7 1.8 %collective-permute-start.14 = (f32[32,512]{1,0:T(8,128)S(1)}, f32[32,512]{1,0:T(8,128)S(1)}, u32[]{:S(2)}, u32[]{:S(2)}) collective-permute-start(f32[32,512]{1,0:T(8,128)S(1)} %add.272), channel_id=1, source_target_pairs={{0,8},{1,9},{2,10},{3,11},{4,12},{5,13},{6,14},{7,15},{8,0},{9,1},... | collective-permute-start | bytes 196616 | tf_op jit(solution)/shard_map/ppermute | solution.py:417
  65.5 0.0 collective-permute-done.8
  65.6 0.4 collective-permute-start.19
  65.9 2.1 %collective-permute-done.14 = f32[32,512]{1,0:T(8,128)S(1)} collective-permute-done((f32[32,512]{1,0:T(8,128)S(1)}, f32[32,512]{1,0:T(8,128)S(1)}, u32[]{:S(2)}, u32[]{:S(2)}) %collective-permute-start.14) | collective-permute-done | bytes 65568 | tf_op jit(solution)/shard_map/ppermute | solution.py:417
  68.1 0.9 %collective-permute-start.15 = (f32[64,512]{1,0:T(8,128)S(1)}, f32[64,512]{1,0:T(8,128)S(1)}, u32[]{:S(2)}, u32[]{:S(2)}) collective-permute-start(f32[64,512]{1,0:T(8,128)S(1)} %pad_maximum_fusion.4), channel_id=1, source_target_pairs={{0,4},{1,3},{2,6},{3,1},{4,0},{5,7},{6,2},{7,5},{8,12},{9,11},{10,... | collective-permute-start | bytes 393224 | tf_op jit(solution)/shard_map/ppermute | solution.py:418
  69.0 0.9 %collective-permute-done.19 = f32[32,512]{1,0:T(8,128)S(1)} collective-permute-done((f32[32,512]{1,0:T(8,128)S(1)}, f32[32,512]{1,0:T(8,128)S(1)}, u32[]{:S(2)}, u32[]{:S(2)}) %collective-permute-start.19) | collective-permute-done | bytes 65568 | tf_op jit(solution)/shard_map/ppermute | solution.py:417
  69.9 0.7 collective-permute-start.20
  70.6 3.9 %collective-permute-done.15 = f32[64,512]{1,0:T(8,128)S(1)} collective-permute-done((f32[64,512]{1,0:T(8,128)S(1)}, f32[64,512]{1,0:T(8,128)S(1)}, u32[]{:S(2)}, u32[]{:S(2)}) %collective-permute-start.15) | collective-permute-done | bytes 131104 | tf_op jit(solution)/shard_map/ppermute | solution.py:418
  74.5 2.3 %collective-permute-start.16 = (f32[128,512]{1,0:T(8,128)S(1)}, f32[128,512]{1,0:T(8,128)S(1)}, u32[]{:S(2)}, u32[]{:S(2)}) collective-permute-start(f32[128,512]{1,0:T(8,128)S(1)} %pad_maximum_fusion.1.refs_0_), channel_id=1, source_target_pairs={{0,2},{1,5},{2,0},{3,7},{4,6},{5,1},{6,4},{7,3},{8,10},{9,13},{10,... | collective-permute-start | bytes 786440 | tf_op jit(solution)/shard_map/ppermute | solution.py:419
  76.8 0.5 collective-permute-done.20
  77.3 2.3 %collective-permute-start.21 = (f32[128,512]{1,0:T(8,128)S(1)}, f32[128,512]{1,0:T(8,128)S(1)}, u32[]{:S(2)}, u32[]{:S(2)}) collective-permute-start(f32[128,512]{1,0:T(8,128)S(1)} %pad_maximum_fusion.2.refs_4_), channel_id=1, source_target_pairs={{0,2},{1,5},{2,0},{3,7},{4,6},{5,1},{6,4},{7,3},{8,10},{9,13},{10,... | collective-permute-start | bytes 786440 | tf_op jit(solution)/shard_map/ppermute | solution.py:419
  79.6 0.0 collective-permute-start.17
  79.6 0.5 collective-permute-start.22
  80.1 1.0 %collective-permute-done.16.refs_1_ = f32[128,512]{1,0:T(8,128)S(1)} collective-permute-done((f32[128,512]{1,0:T(8,128)S(1)}, f32[128,512]{1,0:T(8,128)S(1)}, u32[]{:S(2)}, u32[]{:S(2)}) %collective-permute-start.16) | collective-permute-done | bytes 262176 | tf_op jit(solution)/shard_map/ppermute | solution.py:419
  81.1 0.0 collective-permute-start.18
  81.1 2.8 %collective-permute-done.21.refs_5_ = f32[128,512]{1,0:T(8,128)S(1)} collective-permute-done((f32[128,512]{1,0:T(8,128)S(1)}, f32[128,512]{1,0:T(8,128)S(1)}, u32[]{:S(2)}, u32[]{:S(2)}) %collective-permute-start.21) | collective-permute-done | bytes 262176 | tf_op jit(solution)/shard_map/ppermute | solution.py:419
  83.9 0.0 collective-permute-start.23
  83.9 0.0 collective-permute-done.17.refs_2_
  83.9 0.0 collective-permute-done.22.refs_6_
  83.9 0.0 collective-permute-done.18.refs_3_
  84.0 1.5 %collective-permute-done.23.refs_7_ = f32[128,512]{1,0:T(8,128)S(1)} collective-permute-done((f32[128,512]{1,0:T(8,128)S(1)}, f32[128,512]{1,0:T(8,128)S(1)}, u32[]{:S(2)}, u32[]{:S(2)}) %collective-permute-start.23) | collective-permute-done | bytes 262176 | tf_op jit(solution)/shard_map/ppermute | solution.py:420
  85.5 2.9 %shard_map.41 = f32[1,128,512]{2,1,0:T(8,128)} custom-call(s32[2]{0:T(128)S(1)} %pad_add_fusion.place, s32[16]{0:T(128)S(1)} %stack.88.order, f32[8,128]{1,0:T(8,128)S(1)} %slice.143.energy, f32[128,512]{1,0:T(8,128)S(1)} %pad_maximum_fusion.1.refs_0_, f32[128,512]{1,0:T(8,128)S(1)} %collective-permute-done.16.refs_1_, ...), custom_call_target="tpu_custom_call" | custom-call | tf_op jit(solution)/shard_map/pallas_call | solution.py:370
  (24 shorter events, 0.3 us)
Async XLA Ops:
  0.0 8.6 %copy-start = (s32[16,128]{1,0:T(8,128)S(1)}, s32[16,128]{1,0:T(8,128)}, u32[]{:S(2)}) copy-start(s32[16,128]{1,0:T(8,128)} %param.4) | copy-start | bytes 24580
  2.2 27.6 %collective-permute-start = (f32[1024,128]{1,0:T(8,128)}, f32[1024,128]{1,0:T(8,128)S(1)}, u32[]{:S(2)}, u32[]{:S(2)}) collective-permute-start(f32[1024,128]{1,0:T(8,128)} %get-tuple-element.20), channel_id=1, source_target_pairs={{0,4},{4,8},{8,12},{12,16},{16,20},{20,24},{24,28},{1,5},{5,9},{9,... | collective-permute-start | bytes 1572872 | tf_op jit(solution)/shard_map/ppermute | solution.py:437
  7.2 22.7 %collective-permute-start.1 = (f32[1024,128]{1,0:T(8,128)}, f32[1024,128]{1,0:T(8,128)S(1)}, u32[]{:S(2)}, u32[]{:S(2)}) collective-permute-start(f32[1024,128]{1,0:T(8,128)} %get-tuple-element.21), channel_id=1, source_target_pairs={{4,0},{8,4},{12,8},{16,12},{20,16},{24,20},{28,24},{5,1},{9,5},{13... | collective-permute-start | bytes 1572872 | tf_op jit(solution)/shard_map/ppermute | solution.py:438
  24.6 3.9 %collective-permute-start.3 = (f32[16,4096]{1,0:T(8,128)S(1)}, f32[16,4096]{1,0:T(8,128)S(1)}, u32[]{:S(2)}, u32[]{:S(2)}) collective-permute-start(f32[16,4096]{1,0:T(8,128)S(1)} %get-tuple-element.23.edge_cols), channel_id=1, source_target_pairs={{1,2},{2,1},{5,6},{6,5},{9,10},{10,9},{13,14},{14,13},{17,18},{18,... | collective-permute-start | bytes 786440 | tf_op jit(solution)/shard_map/ppermute | solution.py:451
  25.5 4.1 %collective-permute-start.2 = (f32[16,4096]{1,0:T(8,128)S(1)}, f32[16,4096]{1,0:T(8,128)S(1)}, u32[]{:S(2)}, u32[]{:S(2)}) collective-permute-start(f32[16,4096]{1,0:T(8,128)S(1)} %get-tuple-element.23.edge_cols), channel_id=1, source_target_pairs={{0,1},{1,0},{2,3},{3,2},{4,5},{5,4},{6,7},{7,6},{8,9},{9,8},{10,11... | collective-permute-start | bytes 786440 | tf_op jit(solution)/shard_map/ppermute | solution.py:451
  32.5 4.0 %collective-permute-start.4 = (f32[264,512]{1,0:T(8,128)S(1)}, f32[264,512]{1,0:T(8,128)S(1)}, u32[]{:S(2)}, u32[]{:S(2)}) collective-permute-start(f32[264,512]{1,0:T(8,128)S(1)} %get-tuple-element.30), channel_id=1, source_target_pairs={{0,1},{1,0},{2,3},{3,2},{4,5},{5,4},{6,7},{7,6},{8,9},{9,8},{10,11... | collective-permute-start | bytes 1622024 | tf_op jit(solution)/shard_map/ppermute | solution.py:403
  34.9 3.7 %collective-permute-start.9 = (f32[256,512]{1,0:T(8,128)S(1)}, f32[256,512]{1,0:T(8,128)S(1)}, u32[]{:S(2)}, u32[]{:S(2)}) collective-permute-start(f32[256,512]{1,0:T(8,128)S(1)} %get-tuple-element.32), channel_id=1, source_target_pairs={{0,1},{1,0},{2,3},{3,2},{4,5},{5,4},{6,7},{7,6},{8,9},{9,8},{10,11... | collective-permute-start | bytes 1572872 | tf_op jit(solution)/shard_map/ppermute | solution.py:403
  36.6 6.6 %collective-permute-start.5 = (f32[136,512]{1,0:T(8,128)S(1)}, f32[136,512]{1,0:T(8,128)S(1)}, u32[]{:S(2)}, u32[]{:S(2)}) collective-permute-start(f32[136,512]{1,0:T(8,128)S(1)} %pad_maximum_fusion), channel_id=1, source_target_pairs={{0,2},{1,5},{2,0},{3,7},{4,6},{5,1},{6,4},{7,3},{8,10},{9,13},{10,... | collective-permute-start | bytes 835592 | tf_op jit(solution)/shard_map/ppermute | solution.py:403
  38.8 7.3 %collective-permute-start.10 = (f32[128,512]{1,0:T(8,128)S(1)}, f32[128,512]{1,0:T(8,128)S(1)}, u32[]{:S(2)}, u32[]{:S(2)}) collective-permute-start(f32[128,512]{1,0:T(8,128)S(1)} %get-tuple-element.36), channel_id=1, source_target_pairs={{0,2},{1,5},{2,0},{3,7},{4,6},{5,1},{6,4},{7,3},{8,10},{9,13},{10,... | collective-permute-start | bytes 786440 | tf_op jit(solution)/shard_map/ppermute | solution.py:403
  43.3 6.0 %collective-permute-start.6 = (f32[72,512]{1,0:T(8,128)S(1)}, f32[72,512]{1,0:T(8,128)S(1)}, u32[]{:S(2)}, u32[]{:S(2)}) collective-permute-start(f32[72,512]{1,0:T(8,128)S(1)} %pad_maximum_fusion.3), channel_id=1, source_target_pairs={{0,4},{1,3},{2,6},{3,1},{4,0},{5,7},{6,2},{7,5},{8,12},{9,11},{10,... | collective-permute-start | bytes 442376 | tf_op jit(solution)/shard_map/ppermute | solution.py:403
  46.1 6.1 %collective-permute-start.11 = (f32[64,512]{1,0:T(8,128)S(1)}, f32[64,512]{1,0:T(8,128)S(1)}, u32[]{:S(2)}, u32[]{:S(2)}) collective-permute-start(f32[64,512]{1,0:T(8,128)S(1)} %get-tuple-element.40), channel_id=1, source_target_pairs={{0,4},{1,3},{2,6},{3,1},{4,0},{5,7},{6,2},{7,5},{8,12},{9,11},{10,... | collective-permute-start | bytes 393224 | tf_op jit(solution)/shard_map/ppermute | solution.py:403
  49.3 5.9 %collective-permute-start.7 = (f32[40,512]{1,0:T(8,128)S(1)}, f32[40,512]{1,0:T(8,128)S(1)}, u32[]{:S(2)}, u32[]{:S(2)}) collective-permute-start(f32[40,512]{1,0:T(8,128)S(1)} %pad_maximum_fusion.6), channel_id=1, source_target_pairs={{0,8},{1,9},{2,10},{3,11},{4,12},{5,13},{6,14},{7,15},{8,0},{9,1},... | collective-permute-start | bytes 245768 | tf_op jit(solution)/shard_map/ppermute | solution.py:403
  52.2 6.2 %collective-permute-start.12 = (f32[32,512]{1,0:T(8,128)S(1)}, f32[32,512]{1,0:T(8,128)S(1)}, u32[]{:S(2)}, u32[]{:S(2)}) collective-permute-start(f32[32,512]{1,0:T(8,128)S(1)} %slice_add_fusion.8), channel_id=1, source_target_pairs={{0,8},{1,9},{2,10},{3,11},{4,12},{5,13},{6,14},{7,15},{8,0},{9,1},... | collective-permute-start | bytes 196616 | tf_op jit(solution)/shard_map/ppermute | solution.py:403
  55.3 10.2 %collective-permute-start.8 = (f32[40,512]{1,0:T(8,128)S(1)}, f32[40,512]{1,0:T(8,128)S(1)}, u32[]{:S(2)}, u32[]{:S(2)}) collective-permute-start(f32[40,512]{1,0:T(8,128)S(1)} %pad_maximum_fusion.7), channel_id=1, source_target_pairs={{0,16},{1,17},{2,18},{3,19},{4,20},{5,21},{6,22},{7,23},{8,24},{9,... | collective-permute-start | bytes 245768 | tf_op jit(solution)/shard_map/ppermute | solution.py:412
  58.5 5.3 %collective-permute-start.13 = (f32[32,512]{1,0:T(8,128)S(1)}, f32[32,512]{1,0:T(8,128)S(1)}, u32[]{:S(2)}, u32[]{:S(2)}) collective-permute-start(f32[32,512]{1,0:T(8,128)S(1)} %fusion), channel_id=1, source_target_pairs={{0,16},{1,17},{2,18},{3,19},{4,20},{5,21},{6,22},{7,23},{8,24},{9,... | collective-permute-start | bytes 196616 | tf_op jit(solution)/shard_map/ppermute | solution.py:412
  63.7 4.3 %collective-permute-start.14 = (f32[32,512]{1,0:T(8,128)S(1)}, f32[32,512]{1,0:T(8,128)S(1)}, u32[]{:S(2)}, u32[]{:S(2)}) collective-permute-start(f32[32,512]{1,0:T(8,128)S(1)} %add.272), channel_id=1, source_target_pairs={{0,8},{1,9},{2,10},{3,11},{4,12},{5,13},{6,14},{7,15},{8,0},{9,1},... | collective-permute-start | bytes 196616 | tf_op jit(solution)/shard_map/ppermute | solution.py:417
  65.6 4.3 %collective-permute-start.19 = (f32[32,512]{1,0:T(8,128)S(1)}, f32[32,512]{1,0:T(8,128)S(1)}, u32[]{:S(2)}, u32[]{:S(2)}) collective-permute-start(f32[32,512]{1,0:T(8,128)S(1)} %slice.154), channel_id=1, source_target_pairs={{0,8},{1,9},{2,10},{3,11},{4,12},{5,13},{6,14},{7,15},{8,0},{9,1},... | collective-permute-start | bytes 196616 | tf_op jit(solution)/shard_map/ppermute | solution.py:417
  68.1 6.4 %collective-permute-start.15 = (f32[64,512]{1,0:T(8,128)S(1)}, f32[64,512]{1,0:T(8,128)S(1)}, u32[]{:S(2)}, u32[]{:S(2)}) collective-permute-start(f32[64,512]{1,0:T(8,128)S(1)} %pad_maximum_fusion.4), channel_id=1, source_target_pairs={{0,4},{1,3},{2,6},{3,1},{4,0},{5,7},{6,2},{7,5},{8,12},{9,11},{10,... | collective-permute-start | bytes 393224 | tf_op jit(solution)/shard_map/ppermute | solution.py:418
  69.9 7.4 %collective-permute-start.20 = (f32[64,512]{1,0:T(8,128)S(1)}, f32[64,512]{1,0:T(8,128)S(1)}, u32[]{:S(2)}, u32[]{:S(2)}) collective-permute-start(f32[64,512]{1,0:T(8,128)S(1)} %pad_maximum_fusion.5), channel_id=1, source_target_pairs={{0,4},{1,3},{2,6},{3,1},{4,0},{5,7},{6,2},{7,5},{8,12},{9,11},{10,... | collective-permute-start | bytes 393224 | tf_op jit(solution)/shard_map/ppermute | solution.py:418
  74.5 6.6 %collective-permute-start.16 = (f32[128,512]{1,0:T(8,128)S(1)}, f32[128,512]{1,0:T(8,128)S(1)}, u32[]{:S(2)}, u32[]{:S(2)}) collective-permute-start(f32[128,512]{1,0:T(8,128)S(1)} %pad_maximum_fusion.1.refs_0_), channel_id=1, source_target_pairs={{0,2},{1,5},{2,0},{3,7},{4,6},{5,1},{6,4},{7,3},{8,10},{9,13},{10,... | collective-permute-start | bytes 786440 | tf_op jit(solution)/shard_map/ppermute | solution.py:419
  77.3 6.6 %collective-permute-start.21 = (f32[128,512]{1,0:T(8,128)S(1)}, f32[128,512]{1,0:T(8,128)S(1)}, u32[]{:S(2)}, u32[]{:S(2)}) collective-permute-start(f32[128,512]{1,0:T(8,128)S(1)} %pad_maximum_fusion.2.refs_4_), channel_id=1, source_target_pairs={{0,2},{1,5},{2,0},{3,7},{4,6},{5,1},{6,4},{7,3},{8,10},{9,13},{10,... | collective-permute-start | bytes 786440 | tf_op jit(solution)/shard_map/ppermute | solution.py:419
  79.6 4.4 %collective-permute-start.17 = (f32[128,512]{1,0:T(8,128)S(1)}, f32[128,512]{1,0:T(8,128)S(1)}, u32[]{:S(2)}, u32[]{:S(2)}) collective-permute-start(f32[128,512]{1,0:T(8,128)S(1)} %pad_maximum_fusion.1.refs_0_), channel_id=1, source_target_pairs={{0,1},{1,0},{2,3},{3,2},{4,5},{5,4},{6,7},{7,6},{8,9},{9,8},{10,11... | collective-permute-start | bytes 786440 | tf_op jit(solution)/shard_map/ppermute | solution.py:420
  79.6 4.4 %collective-permute-start.22 = (f32[128,512]{1,0:T(8,128)S(1)}, f32[128,512]{1,0:T(8,128)S(1)}, u32[]{:S(2)}, u32[]{:S(2)}) collective-permute-start(f32[128,512]{1,0:T(8,128)S(1)} %pad_maximum_fusion.2.refs_4_), channel_id=1, source_target_pairs={{0,1},{1,0},{2,3},{3,2},{4,5},{5,4},{6,7},{7,6},{8,9},{9,8},{10,11... | collective-permute-start | bytes 786440 | tf_op jit(solution)/shard_map/ppermute | solution.py:420
  81.1 2.8 %collective-permute-start.18 = (f32[128,512]{1,0:T(8,128)S(1)}, f32[128,512]{1,0:T(8,128)S(1)}, u32[]{:S(2)}, u32[]{:S(2)}) collective-permute-start(f32[128,512]{1,0:T(8,128)S(1)} %collective-permute-done.16.refs_1_), channel_id=1, source_target_pairs={{0,1},{1,0},{2,3},{3,2},{4,5},{5,4},{6,7},{7,6},{8,9},{9,8},{10,11... | collective-permute-start | bytes 786440 | tf_op jit(solution)/shard_map/ppermute | solution.py:420
  83.9 1.5 %collective-permute-start.23 = (f32[128,512]{1,0:T(8,128)S(1)}, f32[128,512]{1,0:T(8,128)S(1)}, u32[]{:S(2)}, u32[]{:S(2)}) collective-permute-start(f32[128,512]{1,0:T(8,128)S(1)} %collective-permute-done.21.refs_5_), channel_id=1, source_target_pairs={{0,1},{1,0},{2,3},{3,2},{4,5},{5,4},{6,7},{7,6},{8,9},{9,8},{10,11... | collective-permute-start | bytes 786440 | tf_op jit(solution)/shard_map/ppermute | solution.py:420

commit v3 on v2

--- a/solution.py
+++ b/solution.py
@@ -71,7 +71,7 @@
 
 def interior_kernel(chunks, order, height, coefs, patterns_hbm, *refs):
     totals, refs = refs[: len(chunks)], refs[len(chunks) :]
-    energy, near_rows, edge_cols, row_patterns, col_patterns, *refs = refs
+    energy, near_rows, edge_cols, sent_cols, row_patterns, col_patterns, *refs = refs
     patterns, flat, first, second, sem = refs
     cells, lanes = coefs.shape[1:]
     days = height.shape[0] // cells
@@ -159,20 +159,24 @@
                 velocity[here, place : place + lanes] = moved[rows, lanes:]
         return gathered, total
 
-    def two_groups(velocity, pair, carry):
+    def two_groups(velocity, pair):
         zero = jnp.zeros((TILE, lanes), F32)
         gathered, one = some_days(velocity, pair * 2, [zero, zero])
         gathered, two = some_days(velocity, pair * 2 + 1, gathered)
         energy[...] += one + two
-        here = pl.ds(pl.multiple_of(pair * lanes, lanes), lanes)
-        for side in range(2):
-            edge_cols[side * TILE : (side + 1) * TILE, here] = gathered[side]
-        return carry
+        edge_cols[:, pair * lanes : (pair + 1) * lanes] = jnp.concatenate(gathered)
 
     def work_out(velocity):
-        lax.fori_loop(
-            0, days // group_days, functools.partial(two_groups, velocity), 0, unroll=True
-        )
+        pairs = days // group_days
+        for pair in range(pairs):
+            two_groups(velocity, pair)
+        middle = (lane % 4 == 1) | (lane % 4 == 2)
+        for pair in range(0, pairs, 2):
+            for side in range(0, cells, TILE):
+                here = edge_cols[side : side + TILE, pair * lanes : (pair + 1) * lanes]
+                there = edge_cols[side : side + TILE, (pair + 1) * lanes : (pair + 2) * lanes]
+                both = jnp.where(middle, here, pltpu.roll(there, 2, 1))
+                sent_cols[side : side + TILE, pair // 2 * lanes : (pair // 2 + 1) * lanes] = both
         for side, cell in enumerate((1, cells - 2)):
             near_rows[side] = height[pl.ds(cell, days, stride=cells), :]
 
@@ -219,6 +223,7 @@
             like(TILE, lanes),
             like(2, days, lanes),
             like(cells, 4 * days),
+            like(cells, 2 * days),
             like(modes, 2 * lanes, dtype=BF16),
             like(modes, 2 * cells, dtype=BF16),
         ],
@@ -233,6 +238,7 @@
             pl.BlockSpec((TILE, lanes), lambda s: (0, 0)),
             pl.BlockSpec((2, day, lanes), lambda s: (0, now(s), 0)),
             pl.BlockSpec((cells, 4 * day), lambda s: (0, now(s))),
+            pl.BlockSpec((cells, 2 * day), lambda s: (0, now(s))),
             pl.BlockSpec((modes, 2 * lanes), lambda s: (0, 0)),
             pl.BlockSpec((modes, 2 * cells), lambda s: (0, 0)),
         ],
@@ -262,8 +268,12 @@
     added = lax.dot_general(row_patterns[...], rows, NT, preferred_element_type=F32)
     four = lax.broadcasted_iota(jnp.int32, (cells, 4 * days), 1) % 4
     even = place[0] % 2 == 0
-    west = jnp.where(even, other[...], paired[...])
-    east = jnp.where(even, paired[...], other[...])
+    spread = []
+    for one, two in ((other, paired), (paired, other)):
+        halo = jnp.where(even, one[...], two[...])
+        blocks = [halo[:, at : at + lanes] for at in range(0, 2 * days, lanes)]
+        spread.append([a for b in blocks for a in (b, pltpu.roll(b, lanes - 2, 1))])
+    west, east = (jnp.concatenate(a, axis=1) for a in spread)
     left = (edge_cols[...] - pltpu.roll(west, 2, 1)) * coefs[0, :, 0:1]
     right = (east - pltpu.roll(edge_cols[...], 2, 1)) * coefs[0, :, lanes - 1 : lanes]
     both = jnp.where(four == 3, left, jnp.where(four == 2, right, 0.0))
@@ -304,7 +314,6 @@
     cells, lanes = coefs.shape[1:]
     half = modes // 2
     whole = lambda a: pl.BlockSpec(a.shape, lambda s: (0,) * a.ndim)
-    cols = pl.BlockSpec((cells, 4 * size), lambda s: (0, at))
     outs = [like(half, size), like(half + TILE * last, size)]
     if not last:
         outs.append(like(TILE, lanes))
@@ -318,9 +327,9 @@
             pl.BlockSpec((size, lanes), lambda s: (at, 0)),
             pl.BlockSpec((size, lanes), lambda s: (at, 0)),
             pl.BlockSpec((2, size, lanes), lambda s: (0, at, 0)),
-            cols,
-            cols,
-            cols,
+            pl.BlockSpec((cells, 2 * size), lambda s: (0, at)),
+            pl.BlockSpec((cells, 2 * size), lambda s: (0, at)),
+            pl.BlockSpec((cells, 4 * size), lambda s: (0, at)),
             whole(coefs),
             whole(row_patterns),
             whole(col_patterns),
@@ -382,42 +391,53 @@
 
 
 def steps_of(devices):
-    flips = [(1, 1), (2, 4), (4, 2)] + [(b, b) for b in (8 << i for i in range(30)) if b < devices]
+    flips = [(1, 1), (2, 8), (4, 2), (8, 4)] + [(b, b) for b in (16 << i for i in range(30)) if b < devices]
     return [[(i, i ^ flip[i & 1]) for i in range(devices)] for flip in flips]
 
 
 def block_order(index):
-    core, first, second, third = (index >> bit & 1 for bit in range(SCATTERS))
+    core, chip = index & 1, (index >> 1) & 7
     order = []
     for position in range(SPLIT):
         near, here, there, far = (position >> bit & 1 for bit in reversed(range(SCATTERS)))
         owner = core ^ near
-        a = jnp.where(owner == 0, first ^ here, first ^ there)
-        b = jnp.where(owner == 0, second ^ there, second ^ here)
-        order.append(owner * 8 + a * 4 + b * 2 + (third ^ far))
+        flips = jnp.where(owner == 0, here + there * 2 + far * 4, there + far * 2 + here * 4)
+        order.append(owner * 8 + (chip ^ flips))
     return jnp.stack(order).astype(jnp.int32)
 
 
-def reduced(keep, send, steps):
+def exchanges(keep, send, steps):
     for step in range(SCATTERS):
-        got = lax.ppermute(send, BOTH, steps[step])
+        got = yield send, steps[step]
         half = keep.shape[0]
         quarter = half // 2 if step < SCATTERS - 1 else 0
         parts = [keep[quarter:] + got[quarter:half]]
         if got.shape[0] > half:
-            parts.append(send[-TILE:] + got[half:])
+            parts.append(send[half:] + got[half:])
         send = jnp.concatenate(parts, axis=0)
         keep = keep[:quarter] + got[:quarter]
     for step in steps[SCATTERS:]:
-        send = send + lax.ppermute(send, BOTH, step)
-    return send
-
-
-def gathered(own, steps):
-    pair = jnp.concatenate([own, lax.ppermute(own, BOTH, steps[3])], axis=0)
-    four = jnp.concatenate([pair, lax.ppermute(pair, BOTH, steps[2])], axis=0)
-    other = lax.ppermute(four, BOTH, steps[1])
-    return [four, other, lax.ppermute(four, BOTH, steps[0]), lax.ppermute(other, BOTH, steps[0])]
+        send = send + (yield send, step)
+    own, extra = send[:half], send[half:]
+    pair = jnp.concatenate([own, (yield own, steps[3])], axis=0)
+    four = jnp.concatenate([pair, (yield pair, steps[2])], axis=0)
+    other = yield four, steps[1]
+    first = yield four, steps[0]
+    second = yield other, steps[0]
+    return [four, other, first, second], extra
+
+
+def side_by_side(chains):
+    results = [None] * len(chains)
+    got = [None] * len(chains)
+    while None in results:
+        for i, chain in enumerate(chains):
+            try:
+                send, step = chain.send(got[i])
+                got[i] = lax.ppermute(send, BOTH, step)
+            except StopIteration as end:
+                results[i] = end.value
+    return results
 
 
 def on_device(height, land_sea, patterns):
@@ -443,27 +463,25 @@
     coefs = jnp.stack([coef_east * ocean, coef_north * ocean])
     place = jnp.stack([lat_place, lon_place]).astype(jnp.int32)
     order = block_order(lon_place * lat_devices + lat_place)
-    *totals, energy, near_rows, edge_cols, row_patterns, col_patterns = interior(
+    *totals, energy, near_rows, edge_cols, sent_cols, row_patterns, col_patterns = interior(
         chunks, order, height, coefs, patterns
     )
     pairs = [[(i, i ^ 1) for i in range(lat_devices)]]
     pairs.append([(i, ((i + 1) ^ 1) - 1) for i in range(1, lat_devices - 1)])
-    paired, other = (lax.ppermute(edge_cols, "lat", pair) for pair in pairs)
-
-    parts = []
+    paired, other = (lax.ppermute(sent_cols, "lat", pair) for pair in pairs)
+
+    chains = []
     for i, chunk in enumerate(chunks):
         last = i == len(chunks) - 1
         keep, send, *more = edge(
             chunk, last, place, totals[i], before, after, near_rows, paired, other, edge_cols,
             coefs, row_patterns, col_patterns, energy,
         )
-        own = reduced(keep, send, steps)
-        if last:
-            block = mode_count // SPLIT
-            own, energy = own[:block], own[block:, :LANES]
-        else:
-            energy = more[0]
-        parts.extend(gathered(own, steps))
+        chains.append(exchanges(keep, send, steps))
+        energy = more[0] if more else energy
+    results = side_by_side(chains)
+    parts = [part for found, _ in results for part in found]
+    energy = results[-1][1][:, :LANES]
     cells_total = 2.0 * days * lon_cells * lon_devices * total_rows
     return covariance(
         cells_total, chunks, mode_count // lat_devices, place, order, energy, parts

time: 88.5 us -> 87 us (0.983)
  starting transfers between devices: 41 us -> 39.5 us
    ppermute x22, starting transfers between devices: 34.8 us -> 33.3 us  [the longest x20 29.5 us: side_by_side(): got[i] = lax.ppermute(send, BOTH, step)]
  transfers between devices with their start and end apart: 24 -> 24, of which waited for: 12 -> 13; matrix products, arithmetic and copies ran while one was open for 1% -> 1% of each run, Pallas kernels for 18% -> 18%
where the time goes in v3:
time: 87 us; the launch traced here: 86.6 us
  starting transfers between devices  39.5 us (45%)
  Pallas kernels  23.6 us (27%)
  waiting for transfers between devices  22.4 us (26%)
    ppermute x20, starting transfers between devices, side_by_side(): got[i] = lax.ppermute(send, BOTH, step)  29.5 us
    ppermute x20, waiting for transfers between devices, side_by_side(): got[i] = lax.ppermute(send, BOTH, step)  21.1 us
    pallas_call x1, Pallas kernels, interior(): pl.pallas_call(functools.partial(interior_kernel, chunks), grid=(blocks +...  15.9 us
    ppermute x1, starting transfers between devices, on_device(): before = lax.ppermute(last, 'lon', up)  4.9 us
    ppermute x2, starting transfers between devices, on_device(): paired, other = (lax.ppermute(sent_cols, 'lat', pair) for pair in pairs)  3.76 us
    pallas_call x1, Pallas kernels, covariance(): pl.pallas_call(functools.partial(covariance_kernel, cells_total, chunks),...  2.86 us
    pallas_call x2, Pallas kernels, edge(): pl.pallas_call(functools.partial(edge_kernel, last), grid=(1,), out_shape...  2.62 us
    pallas_call x1, Pallas kernels, edge_rows(): pl.pallas_call(edge_rows_kernel, out_shape=[like(days, lanes)] * 2, in_sp...  2.23 us
  transfers between devices with their start and end apart: 24, of which 13 were waited for; matrix products, arithmetic and copies ran while one was open for 1% of the time, Pallas kernels for 18%

profile of v3, /device:TPU:0, one launch (start us, length us, event | category | flops | bytes accessed | tf_op | source)
XLA Modules:
  0.0 86.6 jit_solution(1101664739543429206)
XLA Ops:
  0.0 0.0 copy-start
  0.0 2.2 %shard_map.38 = (f32[1024,128]{1,0:T(8,128)}, f32[1024,128]{1,0:T(8,128)}) custom-call(f32[1024,16,128]{2,1,0:T(8,128)} %height.1), custom_call_target="tpu_custom_call" | custom-call | tf_op jit(solution)/shard_map/pallas_call | solution.py:63
  2.2 4.9 %collective-permute-start = (f32[1024,128]{1,0:T(8,128)}, f32[1024,128]{1,0:T(8,128)S(1)}, u32[]{:S(2)}, u32[]{:S(2)}) collective-permute-start(f32[1024,128]{1,0:T(8,128)} %get-tuple-element.21), channel_id=1, source_target_pairs={{0,4},{4,8},{8,12},{12,16},{16,20},{20,24},{24,28},{1,5},{5,9},{9,... | collective-permute-start | bytes 1572872 | tf_op jit(solution)/shard_map/ppermute | solution.py:457
  7.2 1.3 %collective-permute-start.1 = (f32[1024,128]{1,0:T(8,128)}, f32[1024,128]{1,0:T(8,128)S(1)}, u32[]{:S(2)}, u32[]{:S(2)}) collective-permute-start(f32[1024,128]{1,0:T(8,128)} %get-tuple-element.22), channel_id=1, source_target_pairs={{4,0},{8,4},{12,8},{16,12},{20,16},{24,20},{28,24},{5,1},{9,5},{13... | collective-permute-start | bytes 1572872 | tf_op jit(solution)/shard_map/ppermute | solution.py:458
  8.5 0.1 multiply_divide_fusion
  8.5 0.0 copy-done
  8.6 0.1 stack.88.order
  8.7 15.9 %shard_map.37 = (f32[512,512]{1,0:T(8,128)S(1)}, f32[512,512]{1,0:T(8,128)S(1)}, f32[8,128]{1,0:T(8,128)S(1)}, f32[2,1024,128]{2,1,0:T(8,128)S(1)}, f32[16,4096]...) custom-call(s32[16]{0:T(128)S(1)} %stack.88.order, ...), custom_call_target="tpu_custom_call" | custom-call | flops 4026531840 | bytes 14680064 | tf_op jit(solution)/shard_map/pallas_call | solution.py:218
  24.6 0.8 collective-permute-start.3
  25.5 2.9 %collective-permute-start.2 = (f32[16,2048]{1,0:T(8,128)S(1)}, f32[16,2048]{1,0:T(8,128)S(1)}, u32[]{:S(2)}, u32[]{:S(2)}) collective-permute-start(f32[16,2048]{1,0:T(8,128)S(1)} %get-tuple-element.24), channel_id=1, source_target_pairs={{0,1},{1,0},{2,3},{3,2},{4,5},{5,4},{6,7},{7,6},{8,9},{9,8},{10,11... | collective-permute-start | bytes 393224 | tf_op jit(solution)/shard_map/ppermute | solution.py:471
  28.4 0.1 pad_add_fusion.place
  28.5 0.0 collective-permute-done.3.other
  28.5 0.9 %collective-permute-done.2.paired = f32[16,2048]{1,0:T(8,128)S(1)} collective-permute-done((f32[16,2048]{1,0:T(8,128)S(1)}, f32[16,2048]{1,0:T(8,128)S(1)}, u32[]{:S(2)}, u32[]{:S(2)}) %collective-permute-start.2) | collective-permute-done | bytes 131104 | tf_op jit(solution)/shard_map/ppermute | solution.py:471
  29.4 0.4 collective-permute-done.before
  29.8 0.0 collective-permute-done.1.after
  29.8 1.3 %shard_map.39 = (f32[256,512]{1,0:T(8,128)S(1)}, f32[256,512]{1,0:T(8,128)S(1)}, f32[8,128]{1,0:T(8,128)S(1)}) custom-call(s32[2]{0:T(128)S(1)} %pad_add_fusion.place, f32[512,512]{1,0:T(8,128)S(1)} %get-tuple-element.28.totals, f32[1024,128]{1,0:T(8,128)S(1)} %collective-permute-done.before, f32[1024,128]{1,0:T(8,128)S(1)} %collective-permute-done.1.after, ...), custom_call_target="tpu_custom_call" | custom-call | tf_op jit(solution)/shard_map/pallas_call | solution.py:320
  31.2 1.3 %shard_map.40 = (f32[256,512]{1,0:T(8,128)S(1)}, f32[264,512]{1,0:T(8,128)S(1)}) custom-call(s32[2]{0:T(128)S(1)} %pad_add_fusion.place, f32[512,512]{1,0:T(8,128)S(1)} %get-tuple-element.20.totals, f32[1024,128]{1,0:T(8,128)S(1)} %collective-permute-done.before, f32[1024,128]{1,0:T(8,128)S(1)} %collective-permute-done.1.after, ...), custom_call_target="tpu_custom_call" | custom-call | tf_op jit(solution)/shard_map/pallas_call | solution.py:320
  32.5 1.0 %collective-permute-start.4 = (f32[264,512]{1,0:T(8,128)S(1)}, f32[264,512]{1,0:T(8,128)S(1)}, u32[]{:S(2)}, u32[]{:S(2)}) collective-permute-start(f32[264,512]{1,0:T(8,128)S(1)} %get-tuple-element.32), channel_id=1, source_target_pairs={{0,1},{1,0},{2,3},{3,2},{4,5},{5,4},{6,7},{7,6},{8,9},{9,8},{10,11... | collective-permute-start | bytes 1622024 | tf_op jit(solution)/shard_map/ppermute | solution.py:437
  33.5 0.1 collective-permute-start.9
  33.6 1.5 %collective-permute-done.4 = f32[264,512]{1,0:T(8,128)S(1)} collective-permute-done((f32[264,512]{1,0:T(8,128)S(1)}, f32[264,512]{1,0:T(8,128)S(1)}, u32[]{:S(2)}, u32[]{:S(2)}) %collective-permute-start.4) | collective-permute-done | bytes 540704 | tf_op jit(solution)/shard_map/ppermute | solution.py:437
  35.1 0.1 slice_add_fusion.3
  35.2 2.1 %collective-permute-start.5 = (f32[136,512]{1,0:T(8,128)S(1)}, f32[136,512]{1,0:T(8,128)S(1)}, u32[]{:S(2)}, u32[]{:S(2)}) collective-permute-start(f32[136,512]{1,0:T(8,128)S(1)} %pad_maximum_fusion), channel_id=1, source_target_pairs={{0,2},{1,9},{2,0},{3,11},{4,6},{5,13},{6,4},{7,15},{8,10},{9,1},{1... | collective-permute-start | bytes 835592 | tf_op jit(solution)/shard_map/ppermute | solution.py:437
  37.2 0.0 collective-permute-done.9
  37.3 0.1 slice_add_fusion.1
  37.3 0.6 collective-permute-start.10
  38.0 3.8 %collective-permute-done.5 = f32[136,512]{1,0:T(8,128)S(1)} collective-permute-done((f32[136,512]{1,0:T(8,128)S(1)}, f32[136,512]{1,0:T(8,128)S(1)}, u32[]{:S(2)}, u32[]{:S(2)}) %collective-permute-start.5) | collective-permute-done | bytes 278560 | tf_op jit(solution)/shard_map/ppermute | solution.py:437
  41.9 2.7 %collective-permute-start.6 = (f32[72,512]{1,0:T(8,128)S(1)}, f32[72,512]{1,0:T(8,128)S(1)}, u32[]{:S(2)}, u32[]{:S(2)}) collective-permute-start(f32[72,512]{1,0:T(8,128)S(1)} %pad_maximum_fusion.3), channel_id=1, source_target_pairs={{0,4},{1,3},{2,6},{3,1},{4,0},{5,7},{6,2},{7,5},{8,12},{9,11},{10,... | collective-permute-start | bytes 442376 | tf_op jit(solution)/shard_map/ppermute | solution.py:437
  44.6 0.0 collective-permute-done.10
  44.7 3.2 %collective-permute-start.11 = (f32[64,512]{1,0:T(8,128)S(1)}, f32[64,512]{1,0:T(8,128)S(1)}, u32[]{:S(2)}, u32[]{:S(2)}) collective-permute-start(f32[64,512]{1,0:T(8,128)S(1)} %get-tuple-element.42), channel_id=1, source_target_pairs={{0,4},{1,3},{2,6},{3,1},{4,0},{5,7},{6,2},{7,5},{8,12},{9,11},{10,... | collective-permute-start | bytes 393224 | tf_op jit(solution)/shard_map/ppermute | solution.py:437
  47.8 0.0 collective-permute-done.6
  47.9 2.9 %collective-permute-start.7 = (f32[40,512]{1,0:T(8,128)S(1)}, f32[40,512]{1,0:T(8,128)S(1)}, u32[]{:S(2)}, u32[]{:S(2)}) collective-permute-start(f32[40,512]{1,0:T(8,128)S(1)} %pad_maximum_fusion.6), channel_id=1, source_target_pairs={{0,8},{1,5},{2,10},{3,7},{4,12},{5,1},{6,14},{7,3},{8,0},{9,13},{1... | collective-permute-start | bytes 245768 | tf_op jit(solution)/shard_map/ppermute | solution.py:437
  50.8 0.7 collective-permute-done.11
  51.5 3.5 %collective-permute-start.12 = (f32[32,512]{1,0:T(8,128)S(1)}, f32[32,512]{1,0:T(8,128)S(1)}, u32[]{:S(2)}, u32[]{:S(2)}) collective-permute-start(f32[32,512]{1,0:T(8,128)S(1)} %slice_add_fusion.8), channel_id=1, source_target_pairs={{0,8},{1,5},{2,10},{3,7},{4,12},{5,1},{6,14},{7,3},{8,0},{9,13},{1... | collective-permute-start | bytes 196616 | tf_op jit(solution)/shard_map/ppermute | solution.py:437
  55.0 0.0 collective-permute-done.7
  55.0 2.6 %collective-permute-start.8 = (f32[40,512]{1,0:T(8,128)S(1)}, f32[40,512]{1,0:T(8,128)S(1)}, u32[]{:S(2)}, u32[]{:S(2)}) collective-permute-start(f32[40,512]{1,0:T(8,128)S(1)} %pad_maximum_fusion.7), channel_id=1, source_target_pairs={{0,16},{1,17},{2,18},{3,19},{4,20},{5,21},{6,22},{7,23},{8,24},{9,... | collective-permute-start | bytes 245768 | tf_op jit(solution)/shard_map/ppermute | solution.py:437
  57.7 0.3 collective-permute-done.12
  58.0 2.3 %collective-permute-start.13 = (f32[32,512]{1,0:T(8,128)S(1)}, f32[32,512]{1,0:T(8,128)S(1)}, u32[]{:S(2)}, u32[]{:S(2)}) collective-permute-start(f32[32,512]{1,0:T(8,128)S(1)} %fusion), channel_id=1, source_target_pairs={{0,16},{1,17},{2,18},{3,19},{4,20},{5,21},{6,22},{7,23},{8,24},{9,... | collective-permute-start | bytes 196616 | tf_op jit(solution)/shard_map/ppermute | solution.py:437
  60.3 2.9 %collective-permute-done.13 = f32[32,512]{1,0:T(8,128)S(1)} collective-permute-done((f32[32,512]{1,0:T(8,128)S(1)}, f32[32,512]{1,0:T(8,128)S(1)}, u32[]{:S(2)}, u32[]{:S(2)}) %collective-permute-start.13) | collective-permute-done | bytes 65568 | tf_op jit(solution)/shard_map/ppermute | solution.py:437
  63.3 1.9 %collective-permute-start.14 = (f32[32,512]{1,0:T(8,128)S(1)}, f32[32,512]{1,0:T(8,128)S(1)}, u32[]{:S(2)}, u32[]{:S(2)}) collective-permute-start(f32[32,512]{1,0:T(8,128)S(1)} %add.192), channel_id=1, source_target_pairs={{0,8},{1,5},{2,10},{3,7},{4,12},{5,1},{6,14},{7,3},{8,0},{9,13},{1... | collective-permute-start | bytes 196616 | tf_op jit(solution)/shard_map/ppermute | solution.py:437
  65.2 0.0 collective-permute-done.8
  65.2 0.3 collective-permute-start.19
  65.5 2.1 %collective-permute-done.14 = f32[32,512]{1,0:T(8,128)S(1)} collective-permute-done((f32[32,512]{1,0:T(8,128)S(1)}, f32[32,512]{1,0:T(8,128)S(1)}, u32[]{:S(2)}, u32[]{:S(2)}) %collective-permute-start.14) | collective-permute-done | bytes 65568 | tf_op jit(solution)/shard_map/ppermute | solution.py:437
  67.6 0.8 collective-permute-start.15
  68.4 1.1 %collective-permute-done.19 = f32[32,512]{1,0:T(8,128)S(1)} collective-permute-done((f32[32,512]{1,0:T(8,128)S(1)}, f32[32,512]{1,0:T(8,128)S(1)}, u32[]{:S(2)}, u32[]{:S(2)}) %collective-permute-start.19) | collective-permute-done | bytes 65568 | tf_op jit(solution)/shard_map/ppermute | solution.py:437
  69.5 0.7 collective-permute-start.20
  70.2 2.4 %collective-permute-done.15 = f32[64,512]{1,0:T(8,128)S(1)} collective-permute-done((f32[64,512]{1,0:T(8,128)S(1)}, f32[64,512]{1,0:T(8,128)S(1)}, u32[]{:S(2)}, u32[]{:S(2)}) %collective-permute-start.15) | collective-permute-done | bytes 131104 | tf_op jit(solution)/shard_map/ppermute | solution.py:437
  72.7 2.3 %collective-permute-start.16 = (f32[128,512]{1,0:T(8,128)S(1)}, f32[128,512]{1,0:T(8,128)S(1)}, u32[]{:S(2)}, u32[]{:S(2)}) collective-permute-start(f32[128,512]{1,0:T(8,128)S(1)} %pad_maximum_fusion.1.refs_0_), channel_id=1, source_target_pairs={{0,2},{1,9},{2,0},{3,11},{4,6},{5,13},{6,4},{7,15},{8,10},{9,1},{1... | collective-permute-start | bytes 786440 | tf_op jit(solution)/shard_map/ppermute | solution.py:437
  75.0 0.0 collective-permute-done.20
  75.0 2.1 %collective-permute-start.21 = (f32[128,512]{1,0:T(8,128)S(1)}, f32[128,512]{1,0:T(8,128)S(1)}, u32[]{:S(2)}, u32[]{:S(2)}) collective-permute-start(f32[128,512]{1,0:T(8,128)S(1)} %pad_maximum_fusion.2.refs_4_), channel_id=1, source_target_pairs={{0,2},{1,9},{2,0},{3,11},{4,6},{5,13},{6,4},{7,15},{8,10},{9,1},{1... | collective-permute-start | bytes 786440 | tf_op jit(solution)/shard_map/ppermute | solution.py:437
  77.1 0.0 collective-permute-start.17
  77.1 0.5 collective-permute-start.22
  77.6 1.7 %collective-permute-done.16.refs_1_ = f32[128,512]{1,0:T(8,128)S(1)} collective-permute-done((f32[128,512]{1,0:T(8,128)S(1)}, f32[128,512]{1,0:T(8,128)S(1)}, u32[]{:S(2)}, u32[]{:S(2)}) %collective-permute-start.16) | collective-permute-done | bytes 262176 | tf_op jit(solution)/shard_map/ppermute | solution.py:437
  79.4 0.0 collective-permute-start.18
  79.4 2.8 %collective-permute-done.21.refs_5_ = f32[128,512]{1,0:T(8,128)S(1)} collective-permute-done((f32[128,512]{1,0:T(8,128)S(1)}, f32[128,512]{1,0:T(8,128)S(1)}, u32[]{:S(2)}, u32[]{:S(2)}) %collective-permute-start.21) | collective-permute-done | bytes 262176 | tf_op jit(solution)/shard_map/ppermute | solution.py:437
  82.2 0.0 collective-permute-start.23
  82.2 0.0 collective-permute-done.17.refs_2_
  82.2 0.0 collective-permute-done.22.refs_6_
  82.2 0.0 collective-permute-done.18.refs_3_
  82.2 1.5 %collective-permute-done.23.refs_7_ = f32[128,512]{1,0:T(8,128)S(1)} collective-permute-done((f32[128,512]{1,0:T(8,128)S(1)}, f32[128,512]{1,0:T(8,128)S(1)}, u32[]{:S(2)}, u32[]{:S(2)}) %collective-permute-start.23) | collective-permute-done | bytes 262176 | tf_op jit(solution)/shard_map/ppermute | solution.py:437
  83.7 2.9 %shard_map.41 = f32[1,128,512]{2,1,0:T(8,128)} custom-call(s32[2]{0:T(128)S(1)} %pad_add_fusion.place, s32[16]{0:T(128)S(1)} %stack.88.order, f32[8,128]{1,0:T(8,128)S(1)} %slice.145.energy, f32[128,512]{1,0:T(8,128)S(1)} %pad_maximum_fusion.1.refs_0_, f32[128,512]{1,0:T(8,128)S(1)} %collective-permute-done.16.refs_1_, ...), custom_call_target="tpu_custom_call" | custom-call | tf_op jit(solution)/shard_map/pallas_call | solution.py:379
  (24 shorter events, 0.3 us)
Async XLA Ops:
  0.0 8.5 %copy-start = (s32[16,128]{1,0:T(8,128)S(1)}, s32[16,128]{1,0:T(8,128)}, u32[]{:S(2)}) copy-start(s32[16,128]{1,0:T(8,128)} %param.4) | copy-start | bytes 24580
  2.2 27.6 %collective-permute-start = (f32[1024,128]{1,0:T(8,128)}, f32[1024,128]{1,0:T(8,128)S(1)}, u32[]{:S(2)}, u32[]{:S(2)}) collective-permute-start(f32[1024,128]{1,0:T(8,128)} %get-tuple-element.21), channel_id=1, source_target_pairs={{0,4},{4,8},{8,12},{12,16},{16,20},{20,24},{24,28},{1,5},{5,9},{9,... | collective-permute-start | bytes 1572872 | tf_op jit(solution)/shard_map/ppermute | solution.py:457
  7.2 22.7 %collective-permute-start.1 = (f32[1024,128]{1,0:T(8,128)}, f32[1024,128]{1,0:T(8,128)S(1)}, u32[]{:S(2)}, u32[]{:S(2)}) collective-permute-start(f32[1024,128]{1,0:T(8,128)} %get-tuple-element.22), channel_id=1, source_target_pairs={{4,0},{8,4},{12,8},{16,12},{20,16},{24,20},{28,24},{5,1},{9,5},{13... | collective-permute-start | bytes 1572872 | tf_op jit(solution)/shard_map/ppermute | solution.py:458
  24.6 3.8 %collective-permute-start.3 = (f32[16,2048]{1,0:T(8,128)S(1)}, f32[16,2048]{1,0:T(8,128)S(1)}, u32[]{:S(2)}, u32[]{:S(2)}) collective-permute-start(f32[16,2048]{1,0:T(8,128)S(1)} %get-tuple-element.24), channel_id=1, source_target_pairs={{1,2},{2,1},{5,6},{6,5},{9,10},{10,9},{13,14},{14,13},{17,18},{18,... | collective-permute-start | bytes 393224 | tf_op jit(solution)/shard_map/ppermute | solution.py:471
  25.5 3.9 %collective-permute-start.2 = (f32[16,2048]{1,0:T(8,128)S(1)}, f32[16,2048]{1,0:T(8,128)S(1)}, u32[]{:S(2)}, u32[]{:S(2)}) collective-permute-start(f32[16,2048]{1,0:T(8,128)S(1)} %get-tuple-element.24), channel_id=1, source_target_pairs={{0,1},{1,0},{2,3},{3,2},{4,5},{5,4},{6,7},{7,6},{8,9},{9,8},{10,11... | collective-permute-start | bytes 393224 | tf_op jit(solution)/shard_map/ppermute | solution.py:471
  32.5 2.6 %collective-permute-start.4 = (f32[264,512]{1,0:T(8,128)S(1)}, f32[264,512]{1,0:T(8,128)S(1)}, u32[]{:S(2)}, u32[]{:S(2)}) collective-permute-start(f32[264,512]{1,0:T(8,128)S(1)} %get-tuple-element.32), channel_id=1, source_target_pairs={{0,1},{1,0},{2,3},{3,2},{4,5},{5,4},{6,7},{7,6},{8,9},{9,8},{10,11... | collective-permute-start | bytes 1622024 | tf_op jit(solution)/shard_map/ppermute | solution.py:437
  33.5 3.7 %collective-permute-start.9 = (f32[256,512]{1,0:T(8,128)S(1)}, f32[256,512]{1,0:T(8,128)S(1)}, u32[]{:S(2)}, u32[]{:S(2)}) collective-permute-start(f32[256,512]{1,0:T(8,128)S(1)} %get-tuple-element.34), channel_id=1, source_target_pairs={{0,1},{1,0},{2,3},{3,2},{4,5},{5,4},{6,7},{7,6},{8,9},{9,8},{10,11... | collective-permute-start | bytes 1572872 | tf_op jit(solution)/shard_map/ppermute | solution.py:437
  35.2 6.6 %collective-permute-start.5 = (f32[136,512]{1,0:T(8,128)S(1)}, f32[136,512]{1,0:T(8,128)S(1)}, u32[]{:S(2)}, u32[]{:S(2)}) collective-permute-start(f32[136,512]{1,0:T(8,128)S(1)} %pad_maximum_fusion), channel_id=1, source_target_pairs={{0,2},{1,9},{2,0},{3,11},{4,6},{5,13},{6,4},{7,15},{8,10},{9,1},{1... | collective-permute-start | bytes 835592 | tf_op jit(solution)/shard_map/ppermute | solution.py:437
  37.3 7.3 %collective-permute-start.10 = (f32[128,512]{1,0:T(8,128)S(1)}, f32[128,512]{1,0:T(8,128)S(1)}, u32[]{:S(2)}, u32[]{:S(2)}) collective-permute-start(f32[128,512]{1,0:T(8,128)S(1)} %get-tuple-element.38), channel_id=1, source_target_pairs={{0,2},{1,9},{2,0},{3,11},{4,6},{5,13},{6,4},{7,15},{8,10},{9,1},{1... | collective-permute-start | bytes 786440 | tf_op jit(solution)/shard_map/ppermute | solution.py:437
  41.9 6.0 %collective-permute-start.6 = (f32[72,512]{1,0:T(8,128)S(1)}, f32[72,512]{1,0:T(8,128)S(1)}, u32[]{:S(2)}, u32[]{:S(2)}) collective-permute-start(f32[72,512]{1,0:T(8,128)S(1)} %pad_maximum_fusion.3), channel_id=1, source_target_pairs={{0,4},{1,3},{2,6},{3,1},{4,0},{5,7},{6,2},{7,5},{8,12},{9,11},{10,... | collective-permute-start | bytes 442376 | tf_op jit(solution)/shard_map/ppermute | solution.py:437
  44.7 6.8 %collective-permute-start.11 = (f32[64,512]{1,0:T(8,128)S(1)}, f32[64,512]{1,0:T(8,128)S(1)}, u32[]{:S(2)}, u32[]{:S(2)}) collective-permute-start(f32[64,512]{1,0:T(8,128)S(1)} %get-tuple-element.42), channel_id=1, source_target_pairs={{0,4},{1,3},{2,6},{3,1},{4,0},{5,7},{6,2},{7,5},{8,12},{9,11},{10,... | collective-permute-start | bytes 393224 | tf_op jit(solution)/shard_map/ppermute | solution.py:437
  47.9 7.1 %collective-permute-start.7 = (f32[40,512]{1,0:T(8,128)S(1)}, f32[40,512]{1,0:T(8,128)S(1)}, u32[]{:S(2)}, u32[]{:S(2)}) collective-permute-start(f32[40,512]{1,0:T(8,128)S(1)} %pad_maximum_fusion.6), channel_id=1, source_target_pairs={{0,8},{1,5},{2,10},{3,7},{4,12},{5,1},{6,14},{7,3},{8,0},{9,13},{1... | collective-permute-start | bytes 245768 | tf_op jit(solution)/shard_map/ppermute | solution.py:437
  51.5 6.5 %collective-permute-start.12 = (f32[32,512]{1,0:T(8,128)S(1)}, f32[32,512]{1,0:T(8,128)S(1)}, u32[]{:S(2)}, u32[]{:S(2)}) collective-permute-start(f32[32,512]{1,0:T(8,128)S(1)} %slice_add_fusion.8), channel_id=1, source_target_pairs={{0,8},{1,5},{2,10},{3,7},{4,12},{5,1},{6,14},{7,3},{8,0},{9,13},{1... | collective-permute-start | bytes 196616 | tf_op jit(solution)/shard_map/ppermute | solution.py:437
  55.0 10.2 %collective-permute-start.8 = (f32[40,512]{1,0:T(8,128)S(1)}, f32[40,512]{1,0:T(8,128)S(1)}, u32[]{:S(2)}, u32[]{:S(2)}) collective-permute-start(f32[40,512]{1,0:T(8,128)S(1)} %pad_maximum_fusion.7), channel_id=1, source_target_pairs={{0,16},{1,17},{2,18},{3,19},{4,20},{5,21},{6,22},{7,23},{8,24},{9,... | collective-permute-start | bytes 245768 | tf_op jit(solution)/shard_map/ppermute | solution.py:437
  58.0 5.2 %collective-permute-start.13 = (f32[32,512]{1,0:T(8,128)S(1)}, f32[32,512]{1,0:T(8,128)S(1)}, u32[]{:S(2)}, u32[]{:S(2)}) collective-permute-start(f32[32,512]{1,0:T(8,128)S(1)} %fusion), channel_id=1, source_target_pairs={{0,16},{1,17},{2,18},{3,19},{4,20},{5,21},{6,22},{7,23},{8,24},{9,... | collective-permute-start | bytes 196616 | tf_op jit(solution)/shard_map/ppermute | solution.py:437
  63.3 4.3 %collective-permute-start.14 = (f32[32,512]{1,0:T(8,128)S(1)}, f32[32,512]{1,0:T(8,128)S(1)}, u32[]{:S(2)}, u32[]{:S(2)}) collective-permute-start(f32[32,512]{1,0:T(8,128)S(1)} %add.192), channel_id=1, source_target_pairs={{0,8},{1,5},{2,10},{3,7},{4,12},{5,1},{6,14},{7,3},{8,0},{9,13},{1... | collective-permute-start | bytes 196616 | tf_op jit(solution)/shard_map/ppermute | solution.py:437
  65.2 4.3 %collective-permute-start.19 = (f32[32,512]{1,0:T(8,128)S(1)}, f32[32,512]{1,0:T(8,128)S(1)}, u32[]{:S(2)}, u32[]{:S(2)}) collective-permute-start(f32[32,512]{1,0:T(8,128)S(1)} %slice.156), channel_id=1, source_target_pairs={{0,8},{1,5},{2,10},{3,7},{4,12},{5,1},{6,14},{7,3},{8,0},{9,13},{1... | collective-permute-start | bytes 196616 | tf_op jit(solution)/shard_map/ppermute | solution.py:437
  67.6 5.0 %collective-permute-start.15 = (f32[64,512]{1,0:T(8,128)S(1)}, f32[64,512]{1,0:T(8,128)S(1)}, u32[]{:S(2)}, u32[]{:S(2)}) collective-permute-start(f32[64,512]{1,0:T(8,128)S(1)} %pad_maximum_fusion.4), channel_id=1, source_target_pairs={{0,4},{1,3},{2,6},{3,1},{4,0},{5,7},{6,2},{7,5},{8,12},{9,11},{10,... | collective-permute-start | bytes 393224 | tf_op jit(solution)/shard_map/ppermute | solution.py:437
  69.5 5.5 %collective-permute-start.20 = (f32[64,512]{1,0:T(8,128)S(1)}, f32[64,512]{1,0:T(8,128)S(1)}, u32[]{:S(2)}, u32[]{:S(2)}) collective-permute-start(f32[64,512]{1,0:T(8,128)S(1)} %pad_maximum_fusion.5), channel_id=1, source_target_pairs={{0,4},{1,3},{2,6},{3,1},{4,0},{5,7},{6,2},{7,5},{8,12},{9,11},{10,... | collective-permute-start | bytes 393224 | tf_op jit(solution)/shard_map/ppermute | solution.py:437
  72.7 6.7 %collective-permute-start.16 = (f32[128,512]{1,0:T(8,128)S(1)}, f32[128,512]{1,0:T(8,128)S(1)}, u32[]{:S(2)}, u32[]{:S(2)}) collective-permute-start(f32[128,512]{1,0:T(8,128)S(1)} %pad_maximum_fusion.1.refs_0_), channel_id=1, source_target_pairs={{0,2},{1,9},{2,0},{3,11},{4,6},{5,13},{6,4},{7,15},{8,10},{9,1},{1... | collective-permute-start | bytes 786440 | tf_op jit(solution)/shard_map/ppermute | solution.py:437
  75.0 7.1 %collective-permute-start.21 = (f32[128,512]{1,0:T(8,128)S(1)}, f32[128,512]{1,0:T(8,128)S(1)}, u32[]{:S(2)}, u32[]{:S(2)}) collective-permute-start(f32[128,512]{1,0:T(8,128)S(1)} %pad_maximum_fusion.2.refs_4_), channel_id=1, source_target_pairs={{0,2},{1,9},{2,0},{3,11},{4,6},{5,13},{6,4},{7,15},{8,10},{9,1},{1... | collective-permute-start | bytes 786440 | tf_op jit(solution)/shard_map/ppermute | solution.py:437
  77.1 5.0 %collective-permute-start.17 = (f32[128,512]{1,0:T(8,128)S(1)}, f32[128,512]{1,0:T(8,128)S(1)}, u32[]{:S(2)}, u32[]{:S(2)}) collective-permute-start(f32[128,512]{1,0:T(8,128)S(1)} %pad_maximum_fusion.1.refs_0_), channel_id=1, source_target_pairs={{0,1},{1,0},{2,3},{3,2},{4,5},{5,4},{6,7},{7,6},{8,9},{9,8},{10,11... | collective-permute-start | bytes 786440 | tf_op jit(solution)/shard_map/ppermute | solution.py:437
  77.1 5.1 %collective-permute-start.22 = (f32[128,512]{1,0:T(8,128)S(1)}, f32[128,512]{1,0:T(8,128)S(1)}, u32[]{:S(2)}, u32[]{:S(2)}) collective-permute-start(f32[128,512]{1,0:T(8,128)S(1)} %pad_maximum_fusion.2.refs_4_), channel_id=1, source_target_pairs={{0,1},{1,0},{2,3},{3,2},{4,5},{5,4},{6,7},{7,6},{8,9},{9,8},{10,11... | collective-permute-start | bytes 786440 | tf_op jit(solution)/shard_map/ppermute | solution.py:437
  79.4 2.8 %collective-permute-start.18 = (f32[128,512]{1,0:T(8,128)S(1)}, f32[128,512]{1,0:T(8,128)S(1)}, u32[]{:S(2)}, u32[]{:S(2)}) collective-permute-start(f32[128,512]{1,0:T(8,128)S(1)} %collective-permute-done.16.refs_1_), channel_id=1, source_target_pairs={{0,1},{1,0},{2,3},{3,2},{4,5},{5,4},{6,7},{7,6},{8,9},{9,8},{10,11... | collective-permute-start | bytes 786440 | tf_op jit(solution)/shard_map/ppermute | solution.py:437
  82.2 1.5 %collective-permute-start.23 = (f32[128,512]{1,0:T(8,128)S(1)}, f32[128,512]{1,0:T(8,128)S(1)}, u32[]{:S(2)}, u32[]{:S(2)}) collective-permute-start(f32[128,512]{1,0:T(8,128)S(1)} %collective-permute-done.21.refs_5_), channel_id=1, source_target_pairs={{0,1},{1,0},{2,3},{3,2},{4,5},{5,4},{6,7},{7,6},{8,9},{9,8},{10,11... | collective-permute-start | bytes 786440 | tf_op jit(solution)/shard_map/ppermute | solution.py:437

commit v4 on v3

--- a/solution.py
+++ b/solution.py
@@ -367,7 +367,8 @@
     mine_high = mine.astype(BF16)
     mine_low = (mine - mine_high.astype(F32)).astype(BF16)
     dot = lambda a, b: lax.dot_general(a, b, NT, preferred_element_type=F32)
-    product = dot(mine_low, high[...]) + dot(mine_high, low[...]) + dot(mine_high, high[...])
+    both = dot(jnp.concatenate([mine_high, mine_low], axis=0), high[...])
+    product = both[rows:] + dot(mine_high, low[...]) + both[:rows]
     total = jnp.sum(energy[...], axis=(0, 1), keepdims=True)
     spread = total / cells_total + 1e-06
     out[0] = product / (spread * (days - lag).astype(F32))
@@ -468,7 +469,7 @@
     )
     pairs = [[(i, i ^ 1) for i in range(lat_devices)]]
     pairs.append([(i, ((i + 1) ^ 1) - 1) for i in range(1, lat_devices - 1)])
-    paired, other = (lax.ppermute(sent_cols, "lat", pair) for pair in pairs)
+    other, paired = (lax.ppermute(sent_cols, "lat", pair) for pair in reversed(pairs))
 
     chains = []
     for i, chunk in enumerate(chunks):

time: 87 us -> 86.7 us (level)
  no operation moved by 1% of the time
where the time goes in v4:
time: 86.7 us; the launch traced here: 86.2 us
  starting transfers between devices  39.5 us (46%)
  Pallas kernels  23.3 us (27%)
  waiting for transfers between devices  22.4 us (26%)
    ppermute x20, starting transfers between devices, side_by_side(): got[i] = lax.ppermute(send, BOTH, step)  29.5 us
    ppermute x20, waiting for transfers between devices, side_by_side(): got[i] = lax.ppermute(send, BOTH, step)  21.1 us
    pallas_call x1, Pallas kernels, interior(): pl.pallas_call(functools.partial(interior_kernel, chunks), grid=(blocks +...  15.9 us
    ppermute x1, starting transfers between devices, on_device(): before = lax.ppermute(last, 'lon', up)  4.9 us
    ppermute x2, starting transfers between devices, on_device(): lax.ppermute(sent_cols, 'lat', pair)  3.76 us
    pallas_call x2, Pallas kernels, edge(): pl.pallas_call(functools.partial(edge_kernel, last), grid=(1,), out_shape...  2.62 us
    pallas_call x1, Pallas kernels, covariance(): pl.pallas_call(functools.partial(covariance_kernel, cells_total, chunks),...  2.52 us
    pallas_call x1, Pallas kernels, edge_rows(): pl.pallas_call(edge_rows_kernel, out_shape=[like(days, lanes)] * 2, in_sp...  2.23 us
  transfers between devices with their start and end apart: 24, of which 13 were waited for; matrix products, arithmetic and copies ran while one was open for 1% of the time, Pallas kernels for 18%

profile of v4, /device:TPU:0, one launch (start us, length us, event | category | flops | bytes accessed | tf_op | source)
XLA Modules:
  0.0 86.2 jit_solution(17960899587884679391)
XLA Ops:
  0.0 0.0 copy-start
  0.0 2.2 %shard_map.38 = (f32[1024,128]{1,0:T(8,128)}, f32[1024,128]{1,0:T(8,128)}) custom-call(f32[1024,16,128]{2,1,0:T(8,128)} %height.1), custom_call_target="tpu_custom_call" | custom-call | tf_op jit(solution)/shard_map/pallas_call | solution.py:63
  2.2 4.9 %collective-permute-start = (f32[1024,128]{1,0:T(8,128)}, f32[1024,128]{1,0:T(8,128)S(1)}, u32[]{:S(2)}, u32[]{:S(2)}) collective-permute-start(f32[1024,128]{1,0:T(8,128)} %get-tuple-element.21), channel_id=1, source_target_pairs={{0,4},{4,8},{8,12},{12,16},{16,20},{20,24},{24,28},{1,5},{5,9},{9,... | collective-permute-start | bytes 1572872 | tf_op jit(solution)/shard_map/ppermute | solution.py:458
  7.2 1.3 %collective-permute-start.1 = (f32[1024,128]{1,0:T(8,128)}, f32[1024,128]{1,0:T(8,128)S(1)}, u32[]{:S(2)}, u32[]{:S(2)}) collective-permute-start(f32[1024,128]{1,0:T(8,128)} %get-tuple-element.22), channel_id=1, source_target_pairs={{4,0},{8,4},{12,8},{16,12},{20,16},{24,20},{28,24},{5,1},{9,5},{13... | collective-permute-start | bytes 1572872 | tf_op jit(solution)/shard_map/ppermute | solution.py:459
  8.5 0.1 multiply_divide_fusion
  8.5 0.0 copy-done
  8.6 0.1 stack.88.order
  8.7 15.9 %shard_map.37 = (f32[512,512]{1,0:T(8,128)S(1)}, f32[512,512]{1,0:T(8,128)S(1)}, f32[8,128]{1,0:T(8,128)S(1)}, f32[2,1024,128]{2,1,0:T(8,128)S(1)}, f32[16,4096]...) custom-call(s32[16]{0:T(128)S(1)} %stack.88.order, ...), custom_call_target="tpu_custom_call" | custom-call | flops 4026531840 | bytes 14680064 | tf_op jit(solution)/shard_map/pallas_call | solution.py:218
  24.6 0.8 collective-permute-start.3
  25.5 2.9 %collective-permute-start.2 = (f32[16,2048]{1,0:T(8,128)S(1)}, f32[16,2048]{1,0:T(8,128)S(1)}, u32[]{:S(2)}, u32[]{:S(2)}) collective-permute-start(f32[16,2048]{1,0:T(8,128)S(1)} %get-tuple-element.24), channel_id=1, source_target_pairs={{0,1},{1,0},{2,3},{3,2},{4,5},{5,4},{6,7},{7,6},{8,9},{9,8},{10,11... | collective-permute-start | bytes 393224 | tf_op jit(solution)/shard_map/ppermute | solution.py:472
  28.4 0.1 pad_add_fusion.place
  28.5 0.0 collective-permute-done.3.other
  28.5 0.9 %collective-permute-done.2.paired = f32[16,2048]{1,0:T(8,128)S(1)} collective-permute-done((f32[16,2048]{1,0:T(8,128)S(1)}, f32[16,2048]{1,0:T(8,128)S(1)}, u32[]{:S(2)}, u32[]{:S(2)}) %collective-permute-start.2) | collective-permute-done | bytes 131104 | tf_op jit(solution)/shard_map/ppermute | solution.py:472
  29.4 0.4 collective-permute-done.before
  29.8 0.0 collective-permute-done.1.after
  29.8 1.3 %shard_map.39 = (f32[256,512]{1,0:T(8,128)S(1)}, f32[256,512]{1,0:T(8,128)S(1)}, f32[8,128]{1,0:T(8,128)S(1)}) custom-call(s32[2]{0:T(128)S(1)} %pad_add_fusion.place, f32[512,512]{1,0:T(8,128)S(1)} %get-tuple-element.28.totals, f32[1024,128]{1,0:T(8,128)S(1)} %collective-permute-done.before, f32[1024,128]{1,0:T(8,128)S(1)} %collective-permute-done.1.after, ...), custom_call_target="tpu_custom_call" | custom-call | tf_op jit(solution)/shard_map/pallas_call | solution.py:320
  31.2 1.3 %shard_map.40 = (f32[256,512]{1,0:T(8,128)S(1)}, f32[264,512]{1,0:T(8,128)S(1)}) custom-call(s32[2]{0:T(128)S(1)} %pad_add_fusion.place, f32[512,512]{1,0:T(8,128)S(1)} %get-tuple-element.20.totals, f32[1024,128]{1,0:T(8,128)S(1)} %collective-permute-done.before, f32[1024,128]{1,0:T(8,128)S(1)} %collective-permute-done.1.after, ...), custom_call_target="tpu_custom_call" | custom-call | tf_op jit(solution)/shard_map/pallas_call | solution.py:320
  32.5 1.0 %collective-permute-start.4 = (f32[264,512]{1,0:T(8,128)S(1)}, f32[264,512]{1,0:T(8,128)S(1)}, u32[]{:S(2)}, u32[]{:S(2)}) collective-permute-start(f32[264,512]{1,0:T(8,128)S(1)} %get-tuple-element.32), channel_id=1, source_target_pairs={{0,1},{1,0},{2,3},{3,2},{4,5},{5,4},{6,7},{7,6},{8,9},{9,8},{10,11... | collective-permute-start | bytes 1622024 | tf_op jit(solution)/shard_map/ppermute | solution.py:438
  33.5 0.1 collective-permute-start.9
  33.6 1.5 %collective-permute-done.4 = f32[264,512]{1,0:T(8,128)S(1)} collective-permute-done((f32[264,512]{1,0:T(8,128)S(1)}, f32[264,512]{1,0:T(8,128)S(1)}, u32[]{:S(2)}, u32[]{:S(2)}) %collective-permute-start.4) | collective-permute-done | bytes 540704 | tf_op jit(solution)/shard_map/ppermute | solution.py:438
  35.1 0.1 slice_add_fusion.3
  35.2 2.1 %collective-permute-start.5 = (f32[136,512]{1,0:T(8,128)S(1)}, f32[136,512]{1,0:T(8,128)S(1)}, u32[]{:S(2)}, u32[]{:S(2)}) collective-permute-start(f32[136,512]{1,0:T(8,128)S(1)} %pad_maximum_fusion), channel_id=1, source_target_pairs={{0,2},{1,9},{2,0},{3,11},{4,6},{5,13},{6,4},{7,15},{8,10},{9,1},{1... | collective-permute-start | bytes 835592 | tf_op jit(solution)/shard_map/ppermute | solution.py:438
  37.2 0.0 collective-permute-done.9
  37.3 0.1 slice_add_fusion.1
  37.3 0.6 collective-permute-start.10
  38.0 3.8 %collective-permute-done.5 = f32[136,512]{1,0:T(8,128)S(1)} collective-permute-done((f32[136,512]{1,0:T(8,128)S(1)}, f32[136,512]{1,0:T(8,128)S(1)}, u32[]{:S(2)}, u32[]{:S(2)}) %collective-permute-start.5) | collective-permute-done | bytes 278560 | tf_op jit(solution)/shard_map/ppermute | solution.py:438
  41.9 2.7 %collective-permute-start.6 = (f32[72,512]{1,0:T(8,128)S(1)}, f32[72,512]{1,0:T(8,128)S(1)}, u32[]{:S(2)}, u32[]{:S(2)}) collective-permute-start(f32[72,512]{1,0:T(8,128)S(1)} %pad_maximum_fusion.3), channel_id=1, source_target_pairs={{0,4},{1,3},{2,6},{3,1},{4,0},{5,7},{6,2},{7,5},{8,12},{9,11},{10,... | collective-permute-start | bytes 442376 | tf_op jit(solution)/shard_map/ppermute | solution.py:438
  44.6 0.0 collective-permute-done.10
  44.7 3.2 %collective-permute-start.11 = (f32[64,512]{1,0:T(8,128)S(1)}, f32[64,512]{1,0:T(8,128)S(1)}, u32[]{:S(2)}, u32[]{:S(2)}) collective-permute-start(f32[64,512]{1,0:T(8,128)S(1)} %get-tuple-element.42), channel_id=1, source_target_pairs={{0,4},{1,3},{2,6},{3,1},{4,0},{5,7},{6,2},{7,5},{8,12},{9,11},{10,... | collective-permute-start | bytes 393224 | tf_op jit(solution)/shard_map/ppermute | solution.py:438
  47.8 0.0 collective-permute-done.6
  47.9 2.9 %collective-permute-start.7 = (f32[40,512]{1,0:T(8,128)S(1)}, f32[40,512]{1,0:T(8,128)S(1)}, u32[]{:S(2)}, u32[]{:S(2)}) collective-permute-start(f32[40,512]{1,0:T(8,128)S(1)} %pad_maximum_fusion.6), channel_id=1, source_target_pairs={{0,8},{1,5},{2,10},{3,7},{4,12},{5,1},{6,14},{7,3},{8,0},{9,13},{1... | collective-permute-start | bytes 245768 | tf_op jit(solution)/shard_map/ppermute | solution.py:438
  50.8 0.7 collective-permute-done.11
  51.5 3.5 %collective-permute-start.12 = (f32[32,512]{1,0:T(8,128)S(1)}, f32[32,512]{1,0:T(8,128)S(1)}, u32[]{:S(2)}, u32[]{:S(2)}) collective-permute-start(f32[32,512]{1,0:T(8,128)S(1)} %slice_add_fusion.8), channel_id=1, source_target_pairs={{0,8},{1,5},{2,10},{3,7},{4,12},{5,1},{6,14},{7,3},{8,0},{9,13},{1... | collective-permute-start | bytes 196616 | tf_op jit(solution)/shard_map/ppermute | solution.py:438
  55.0 0.0 collective-permute-done.7
  55.0 2.6 %collective-permute-start.8 = (f32[40,512]{1,0:T(8,128)S(1)}, f32[40,512]{1,0:T(8,128)S(1)}, u32[]{:S(2)}, u32[]{:S(2)}) collective-permute-start(f32[40,512]{1,0:T(8,128)S(1)} %pad_maximum_fusion.7), channel_id=1, source_target_pairs={{0,16},{1,17},{2,18},{3,19},{4,20},{5,21},{6,22},{7,23},{8,24},{9,... | collective-permute-start | bytes 245768 | tf_op jit(solution)/shard_map/ppermute | solution.py:438
  57.7 0.3 collective-permute-done.12
  58.0 2.3 %collective-permute-start.13 = (f32[32,512]{1,0:T(8,128)S(1)}, f32[32,512]{1,0:T(8,128)S(1)}, u32[]{:S(2)}, u32[]{:S(2)}) collective-permute-start(f32[32,512]{1,0:T(8,128)S(1)} %fusion), channel_id=1, source_target_pairs={{0,16},{1,17},{2,18},{3,19},{4,20},{5,21},{6,22},{7,23},{8,24},{9,... | collective-permute-start | bytes 196616 | tf_op jit(solution)/shard_map/ppermute | solution.py:438
  60.3 2.9 %collective-permute-done.13 = f32[32,512]{1,0:T(8,128)S(1)} collective-permute-done((f32[32,512]{1,0:T(8,128)S(1)}, f32[32,512]{1,0:T(8,128)S(1)}, u32[]{:S(2)}, u32[]{:S(2)}) %collective-permute-start.13) | collective-permute-done | bytes 65568 | tf_op jit(solution)/shard_map/ppermute | solution.py:438
  63.3 1.9 %collective-permute-start.14 = (f32[32,512]{1,0:T(8,128)S(1)}, f32[32,512]{1,0:T(8,128)S(1)}, u32[]{:S(2)}, u32[]{:S(2)}) collective-permute-start(f32[32,512]{1,0:T(8,128)S(1)} %add.192), channel_id=1, source_target_pairs={{0,8},{1,5},{2,10},{3,7},{4,12},{5,1},{6,14},{7,3},{8,0},{9,13},{1... | collective-permute-start | bytes 196616 | tf_op jit(solution)/shard_map/ppermute | solution.py:438
  65.2 0.0 collective-permute-done.8
  65.2 0.3 collective-permute-start.19
  65.5 2.1 %collective-permute-done.14 = f32[32,512]{1,0:T(8,128)S(1)} collective-permute-done((f32[32,512]{1,0:T(8,128)S(1)}, f32[32,512]{1,0:T(8,128)S(1)}, u32[]{:S(2)}, u32[]{:S(2)}) %collective-permute-start.14) | collective-permute-done | bytes 65568 | tf_op jit(solution)/shard_map/ppermute | solution.py:438
  67.6 0.8 collective-permute-start.15
  68.4 1.1 %collective-permute-done.19 = f32[32,512]{1,0:T(8,128)S(1)} collective-permute-done((f32[32,512]{1,0:T(8,128)S(1)}, f32[32,512]{1,0:T(8,128)S(1)}, u32[]{:S(2)}, u32[]{:S(2)}) %collective-permute-start.19) | collective-permute-done | bytes 65568 | tf_op jit(solution)/shard_map/ppermute | solution.py:438
  69.5 0.7 collective-permute-start.20
  70.2 2.4 %collective-permute-done.15 = f32[64,512]{1,0:T(8,128)S(1)} collective-permute-done((f32[64,512]{1,0:T(8,128)S(1)}, f32[64,512]{1,0:T(8,128)S(1)}, u32[]{:S(2)}, u32[]{:S(2)}) %collective-permute-start.15) | collective-permute-done | bytes 131104 | tf_op jit(solution)/shard_map/ppermute | solution.py:438
  72.7 2.3 %collective-permute-start.16 = (f32[128,512]{1,0:T(8,128)S(1)}, f32[128,512]{1,0:T(8,128)S(1)}, u32[]{:S(2)}, u32[]{:S(2)}) collective-permute-start(f32[128,512]{1,0:T(8,128)S(1)} %pad_maximum_fusion.1.refs_0_), channel_id=1, source_target_pairs={{0,2},{1,9},{2,0},{3,11},{4,6},{5,13},{6,4},{7,15},{8,10},{9,1},{1... | collective-permute-start | bytes 786440 | tf_op jit(solution)/shard_map/ppermute | solution.py:438
  75.0 0.0 collective-permute-done.20
  75.0 2.1 %collective-permute-start.21 = (f32[128,512]{1,0:T(8,128)S(1)}, f32[128,512]{1,0:T(8,128)S(1)}, u32[]{:S(2)}, u32[]{:S(2)}) collective-permute-start(f32[128,512]{1,0:T(8,128)S(1)} %pad_maximum_fusion.2.refs_4_), channel_id=1, source_target_pairs={{0,2},{1,9},{2,0},{3,11},{4,6},{5,13},{6,4},{7,15},{8,10},{9,1},{1... | collective-permute-start | bytes 786440 | tf_op jit(solution)/shard_map/ppermute | solution.py:438
  77.1 0.0 collective-permute-start.17
  77.1 0.5 collective-permute-start.22
  77.6 1.7 %collective-permute-done.16.refs_1_ = f32[128,512]{1,0:T(8,128)S(1)} collective-permute-done((f32[128,512]{1,0:T(8,128)S(1)}, f32[128,512]{1,0:T(8,128)S(1)}, u32[]{:S(2)}, u32[]{:S(2)}) %collective-permute-start.16) | collective-permute-done | bytes 262176 | tf_op jit(solution)/shard_map/ppermute | solution.py:438
  79.4 0.0 collective-permute-start.18
  79.4 2.8 %collective-permute-done.21.refs_5_ = f32[128,512]{1,0:T(8,128)S(1)} collective-permute-done((f32[128,512]{1,0:T(8,128)S(1)}, f32[128,512]{1,0:T(8,128)S(1)}, u32[]{:S(2)}, u32[]{:S(2)}) %collective-permute-start.21) | collective-permute-done | bytes 262176 | tf_op jit(solution)/shard_map/ppermute | solution.py:438
  82.2 0.0 collective-permute-start.23
  82.2 0.0 collective-permute-done.17.refs_2_
  82.2 0.0 collective-permute-done.22.refs_6_
  82.2 0.0 collective-permute-done.18.refs_3_
  82.2 1.5 %collective-permute-done.23.refs_7_ = f32[128,512]{1,0:T(8,128)S(1)} collective-permute-done((f32[128,512]{1,0:T(8,128)S(1)}, f32[128,512]{1,0:T(8,128)S(1)}, u32[]{:S(2)}, u32[]{:S(2)}) %collective-permute-start.23) | collective-permute-done | bytes 262176 | tf_op jit(solution)/shard_map/ppermute | solution.py:438
  83.7 2.5 %shard_map.41 = f32[1,128,512]{2,1,0:T(8,128)} custom-call(s32[2]{0:T(128)S(1)} %pad_add_fusion.place, s32[16]{0:T(128)S(1)} %stack.88.order, f32[8,128]{1,0:T(8,128)S(1)} %slice.145.energy, f32[128,512]{1,0:T(8,128)S(1)} %pad_maximum_fusion.1.refs_0_, f32[128,512]{1,0:T(8,128)S(1)} %collective-permute-done.16.refs_1_, ...), custom_call_target="tpu_custom_call" | custom-call | tf_op jit(solution)/shard_map/pallas_call | solution.py:380
  (24 shorter events, 0.3 us)
Async XLA Ops:
  0.0 8.5 %copy-start = (s32[16,128]{1,0:T(8,128)S(1)}, s32[16,128]{1,0:T(8,128)}, u32[]{:S(2)}) copy-start(s32[16,128]{1,0:T(8,128)} %param.4) | copy-start | bytes 24580
  2.2 27.6 %collective-permute-start = (f32[1024,128]{1,0:T(8,128)}, f32[1024,128]{1,0:T(8,128)S(1)}, u32[]{:S(2)}, u32[]{:S(2)}) collective-permute-start(f32[1024,128]{1,0:T(8,128)} %get-tuple-element.21), channel_id=1, source_target_pairs={{0,4},{4,8},{8,12},{12,16},{16,20},{20,24},{24,28},{1,5},{5,9},{9,... | collective-permute-start | bytes 1572872 | tf_op jit(solution)/shard_map/ppermute | solution.py:458
  7.2 22.7 %collective-permute-start.1 = (f32[1024,128]{1,0:T(8,128)}, f32[1024,128]{1,0:T(8,128)S(1)}, u32[]{:S(2)}, u32[]{:S(2)}) collective-permute-start(f32[1024,128]{1,0:T(8,128)} %get-tuple-element.22), channel_id=1, source_target_pairs={{4,0},{8,4},{12,8},{16,12},{20,16},{24,20},{28,24},{5,1},{9,5},{13... | collective-permute-start | bytes 1572872 | tf_op jit(solution)/shard_map/ppermute | solution.py:459
  24.6 3.8 %collective-permute-start.3 = (f32[16,2048]{1,0:T(8,128)S(1)}, f32[16,2048]{1,0:T(8,128)S(1)}, u32[]{:S(2)}, u32[]{:S(2)}) collective-permute-start(f32[16,2048]{1,0:T(8,128)S(1)} %get-tuple-element.24), channel_id=1, source_target_pairs={{1,2},{2,1},{5,6},{6,5},{9,10},{10,9},{13,14},{14,13},{17,18},{18,... | collective-permute-start | bytes 393224 | tf_op jit(solution)/shard_map/ppermute | solution.py:472
  25.5 3.9 %collective-permute-start.2 = (f32[16,2048]{1,0:T(8,128)S(1)}, f32[16,2048]{1,0:T(8,128)S(1)}, u32[]{:S(2)}, u32[]{:S(2)}) collective-permute-start(f32[16,2048]{1,0:T(8,128)S(1)} %get-tuple-element.24), channel_id=1, source_target_pairs={{0,1},{1,0},{2,3},{3,2},{4,5},{5,4},{6,7},{7,6},{8,9},{9,8},{10,11... | collective-permute-start | bytes 393224 | tf_op jit(solution)/shard_map/ppermute | solution.py:472
  32.5 2.6 %collective-permute-start.4 = (f32[264,512]{1,0:T(8,128)S(1)}, f32[264,512]{1,0:T(8,128)S(1)}, u32[]{:S(2)}, u32[]{:S(2)}) collective-permute-start(f32[264,512]{1,0:T(8,128)S(1)} %get-tuple-element.32), channel_id=1, source_target_pairs={{0,1},{1,0},{2,3},{3,2},{4,5},{5,4},{6,7},{7,6},{8,9},{9,8},{10,11... | collective-permute-start | bytes 1622024 | tf_op jit(solution)/shard_map/ppermute | solution.py:438
  33.5 3.7 %collective-permute-start.9 = (f32[256,512]{1,0:T(8,128)S(1)}, f32[256,512]{1,0:T(8,128)S(1)}, u32[]{:S(2)}, u32[]{:S(2)}) collective-permute-start(f32[256,512]{1,0:T(8,128)S(1)} %get-tuple-element.34), channel_id=1, source_target_pairs={{0,1},{1,0},{2,3},{3,2},{4,5},{5,4},{6,7},{7,6},{8,9},{9,8},{10,11... | collective-permute-start | bytes 1572872 | tf_op jit(solution)/shard_map/ppermute | solution.py:438
  35.2 6.6 %collective-permute-start.5 = (f32[136,512]{1,0:T(8,128)S(1)}, f32[136,512]{1,0:T(8,128)S(1)}, u32[]{:S(2)}, u32[]{:S(2)}) collective-permute-start(f32[136,512]{1,0:T(8,128)S(1)} %pad_maximum_fusion), channel_id=1, source_target_pairs={{0,2},{1,9},{2,0},{3,11},{4,6},{5,13},{6,4},{7,15},{8,10},{9,1},{1... | collective-permute-start | bytes 835592 | tf_op jit(solution)/shard_map/ppermute | solution.py:438
  37.3 7.3 %collective-permute-start.10 = (f32[128,512]{1,0:T(8,128)S(1)}, f32[128,512]{1,0:T(8,128)S(1)}, u32[]{:S(2)}, u32[]{:S(2)}) collective-permute-start(f32[128,512]{1,0:T(8,128)S(1)} %get-tuple-element.38), channel_id=1, source_target_pairs={{0,2},{1,9},{2,0},{3,11},{4,6},{5,13},{6,4},{7,15},{8,10},{9,1},{1... | collective-permute-start | bytes 786440 | tf_op jit(solution)/shard_map/ppermute | solution.py:438
  41.9 6.0 %collective-permute-start.6 = (f32[72,512]{1,0:T(8,128)S(1)}, f32[72,512]{1,0:T(8,128)S(1)}, u32[]{:S(2)}, u32[]{:S(2)}) collective-permute-start(f32[72,512]{1,0:T(8,128)S(1)} %pad_maximum_fusion.3), channel_id=1, source_target_pairs={{0,4},{1,3},{2,6},{3,1},{4,0},{5,7},{6,2},{7,5},{8,12},{9,11},{10,... | collective-permute-start | bytes 442376 | tf_op jit(solution)/shard_map/ppermute | solution.py:438
  44.7 6.8 %collective-permute-start.11 = (f32[64,512]{1,0:T(8,128)S(1)}, f32[64,512]{1,0:T(8,128)S(1)}, u32[]{:S(2)}, u32[]{:S(2)}) collective-permute-start(f32[64,512]{1,0:T(8,128)S(1)} %get-tuple-element.42), channel_id=1, source_target_pairs={{0,4},{1,3},{2,6},{3,1},{4,0},{5,7},{6,2},{7,5},{8,12},{9,11},{10,... | collective-permute-start | bytes 393224 | tf_op jit(solution)/shard_map/ppermute | solution.py:438
  47.9 7.1 %collective-permute-start.7 = (f32[40,512]{1,0:T(8,128)S(1)}, f32[40,512]{1,0:T(8,128)S(1)}, u32[]{:S(2)}, u32[]{:S(2)}) collective-permute-start(f32[40,512]{1,0:T(8,128)S(1)} %pad_maximum_fusion.6), channel_id=1, source_target_pairs={{0,8},{1,5},{2,10},{3,7},{4,12},{5,1},{6,14},{7,3},{8,0},{9,13},{1... | collective-permute-start | bytes 245768 | tf_op jit(solution)/shard_map/ppermute | solution.py:438
  51.5 6.5 %collective-permute-start.12 = (f32[32,512]{1,0:T(8,128)S(1)}, f32[32,512]{1,0:T(8,128)S(1)}, u32[]{:S(2)}, u32[]{:S(2)}) collective-permute-start(f32[32,512]{1,0:T(8,128)S(1)} %slice_add_fusion.8), channel_id=1, source_target_pairs={{0,8},{1,5},{2,10},{3,7},{4,12},{5,1},{6,14},{7,3},{8,0},{9,13},{1... | collective-permute-start | bytes 196616 | tf_op jit(solution)/shard_map/ppermute | solution.py:438
  55.0 10.2 %collective-permute-start.8 = (f32[40,512]{1,0:T(8,128)S(1)}, f32[40,512]{1,0:T(8,128)S(1)}, u32[]{:S(2)}, u32[]{:S(2)}) collective-permute-start(f32[40,512]{1,0:T(8,128)S(1)} %pad_maximum_fusion.7), channel_id=1, source_target_pairs={{0,16},{1,17},{2,18},{3,19},{4,20},{5,21},{6,22},{7,23},{8,24},{9,... | collective-permute-start | bytes 245768 | tf_op jit(solution)/shard_map/ppermute | solution.py:438
  58.0 5.2 %collective-permute-start.13 = (f32[32,512]{1,0:T(8,128)S(1)}, f32[32,512]{1,0:T(8,128)S(1)}, u32[]{:S(2)}, u32[]{:S(2)}) collective-permute-start(f32[32,512]{1,0:T(8,128)S(1)} %fusion), channel_id=1, source_target_pairs={{0,16},{1,17},{2,18},{3,19},{4,20},{5,21},{6,22},{7,23},{8,24},{9,... | collective-permute-start | bytes 196616 | tf_op jit(solution)/shard_map/ppermute | solution.py:438
  63.3 4.3 %collective-permute-start.14 = (f32[32,512]{1,0:T(8,128)S(1)}, f32[32,512]{1,0:T(8,128)S(1)}, u32[]{:S(2)}, u32[]{:S(2)}) collective-permute-start(f32[32,512]{1,0:T(8,128)S(1)} %add.192), channel_id=1, source_target_pairs={{0,8},{1,5},{2,10},{3,7},{4,12},{5,1},{6,14},{7,3},{8,0},{9,13},{1... | collective-permute-start | bytes 196616 | tf_op jit(solution)/shard_map/ppermute | solution.py:438
  65.2 4.3 %collective-permute-start.19 = (f32[32,512]{1,0:T(8,128)S(1)}, f32[32,512]{1,0:T(8,128)S(1)}, u32[]{:S(2)}, u32[]{:S(2)}) collective-permute-start(f32[32,512]{1,0:T(8,128)S(1)} %slice.156), channel_id=1, source_target_pairs={{0,8},{1,5},{2,10},{3,7},{4,12},{5,1},{6,14},{7,3},{8,0},{9,13},{1... | collective-permute-start | bytes 196616 | tf_op jit(solution)/shard_map/ppermute | solution.py:438
  67.6 5.0 %collective-permute-start.15 = (f32[64,512]{1,0:T(8,128)S(1)}, f32[64,512]{1,0:T(8,128)S(1)}, u32[]{:S(2)}, u32[]{:S(2)}) collective-permute-start(f32[64,512]{1,0:T(8,128)S(1)} %pad_maximum_fusion.4), channel_id=1, source_target_pairs={{0,4},{1,3},{2,6},{3,1},{4,0},{5,7},{6,2},{7,5},{8,12},{9,11},{10,... | collective-permute-start | bytes 393224 | tf_op jit(solution)/shard_map/ppermute | solution.py:438
  69.5 5.5 %collective-permute-start.20 = (f32[64,512]{1,0:T(8,128)S(1)}, f32[64,512]{1,0:T(8,128)S(1)}, u32[]{:S(2)}, u32[]{:S(2)}) collective-permute-start(f32[64,512]{1,0:T(8,128)S(1)} %pad_maximum_fusion.5), channel_id=1, source_target_pairs={{0,4},{1,3},{2,6},{3,1},{4,0},{5,7},{6,2},{7,5},{8,12},{9,11},{10,... | collective-permute-start | bytes 393224 | tf_op jit(solution)/shard_map/ppermute | solution.py:438
  72.7 6.7 %collective-permute-start.16 = (f32[128,512]{1,0:T(8,128)S(1)}, f32[128,512]{1,0:T(8,128)S(1)}, u32[]{:S(2)}, u32[]{:S(2)}) collective-permute-start(f32[128,512]{1,0:T(8,128)S(1)} %pad_maximum_fusion.1.refs_0_), channel_id=1, source_target_pairs={{0,2},{1,9},{2,0},{3,11},{4,6},{5,13},{6,4},{7,15},{8,10},{9,1},{1... | collective-permute-start | bytes 786440 | tf_op jit(solution)/shard_map/ppermute | solution.py:438
  75.0 7.1 %collective-permute-start.21 = (f32[128,512]{1,0:T(8,128)S(1)}, f32[128,512]{1,0:T(8,128)S(1)}, u32[]{:S(2)}, u32[]{:S(2)}) collective-permute-start(f32[128,512]{1,0:T(8,128)S(1)} %pad_maximum_fusion.2.refs_4_), channel_id=1, source_target_pairs={{0,2},{1,9},{2,0},{3,11},{4,6},{5,13},{6,4},{7,15},{8,10},{9,1},{1... | collective-permute-start | bytes 786440 | tf_op jit(solution)/shard_map/ppermute | solution.py:438
  77.1 5.0 %collective-permute-start.17 = (f32[128,512]{1,0:T(8,128)S(1)}, f32[128,512]{1,0:T(8,128)S(1)}, u32[]{:S(2)}, u32[]{:S(2)}) collective-permute-start(f32[128,512]{1,0:T(8,128)S(1)} %pad_maximum_fusion.1.refs_0_), channel_id=1, source_target_pairs={{0,1},{1,0},{2,3},{3,2},{4,5},{5,4},{6,7},{7,6},{8,9},{9,8},{10,11... | collective-permute-start | bytes 786440 | tf_op jit(solution)/shard_map/ppermute | solution.py:438
  77.1 5.1 %collective-permute-start.22 = (f32[128,512]{1,0:T(8,128)S(1)}, f32[128,512]{1,0:T(8,128)S(1)}, u32[]{:S(2)}, u32[]{:S(2)}) collective-permute-start(f32[128,512]{1,0:T(8,128)S(1)} %pad_maximum_fusion.2.refs_4_), channel_id=1, source_target_pairs={{0,1},{1,0},{2,3},{3,2},{4,5},{5,4},{6,7},{7,6},{8,9},{9,8},{10,11... | collective-permute-start | bytes 786440 | tf_op jit(solution)/shard_map/ppermute | solution.py:438
  79.4 2.8 %collective-permute-start.18 = (f32[128,512]{1,0:T(8,128)S(1)}, f32[128,512]{1,0:T(8,128)S(1)}, u32[]{:S(2)}, u32[]{:S(2)}) collective-permute-start(f32[128,512]{1,0:T(8,128)S(1)} %collective-permute-done.16.refs_1_), channel_id=1, source_target_pairs={{0,1},{1,0},{2,3},{3,2},{4,5},{5,4},{6,7},{7,6},{8,9},{9,8},{10,11... | collective-permute-start | bytes 786440 | tf_op jit(solution)/shard_map/ppermute | solution.py:438
  82.2 1.5 %collective-permute-start.23 = (f32[128,512]{1,0:T(8,128)S(1)}, f32[128,512]{1,0:T(8,128)S(1)}, u32[]{:S(2)}, u32[]{:S(2)}) collective-permute-start(f32[128,512]{1,0:T(8,128)S(1)} %collective-permute-done.21.refs_5_), channel_id=1, source_target_pairs={{0,1},{1,0},{2,3},{3,2},{4,5},{5,4},{6,7},{7,6},{8,9},{9,8},{10,11... | collective-permute-start | bytes 786440 | tf_op jit(solution)/shard_map/ppermute | solution.py:438

commit v5 on v3

--- a/solution.py
+++ b/solution.py
@@ -256,16 +256,25 @@
     )(order, height.reshape(days * cells, lanes), coefs, patterns)
 
 
-def edge_kernel(
-    last, place, totals, before, after, near_rows, paired, other, edge_cols, coefs, row_patterns,
-    col_patterns, energy, keep, send, *more,
+def with_edges(chunk, totals, rows, cols, row_patterns, col_patterns):
+    days = pl.ds(*chunk)
+    added = lax.dot_general(row_patterns[...], rows[days, :], NT, preferred_element_type=F32)
+    added = added + lax.dot_general(
+        col_patterns[...], cols[:, days], NN, preferred_element_type=F32
+    )
+    return totals[...] + added
+
+
+def send_kernel(
+    chunks, place, before, after, near_rows, paired, other, edge_cols, coefs, row_patterns,
+    col_patterns, energy, *refs,
 ):
+    totals, (rows, cols, *sends) = refs[: len(chunks)], refs[len(chunks) :]
     cells, lanes = coefs.shape[1:]
-    days = totals.shape[1]
+    days = before.shape[0]
     low = (near_rows[0] - before[...]) * coefs[1, 0:1, :]
     high = (after[...] - near_rows[1]) * coefs[1, cells - 1 : cells, :]
-    rows = jnp.concatenate([low.astype(BF16), high.astype(BF16)], axis=1)
-    added = lax.dot_general(row_patterns[...], rows, NT, preferred_element_type=F32)
+    rows[...] = jnp.concatenate([low.astype(BF16), high.astype(BF16)], axis=1)
     four = lax.broadcasted_iota(jnp.int32, (cells, 4 * days), 1) % 4
     even = place[0] % 2 == 0
     spread = []
@@ -283,62 +292,66 @@
     place, column = (lax.broadcasted_iota(jnp.int32, (wide, 2 * lanes), d) for d in (0, 1))
     pick = (place == 4 * (column % lanes) + 3 - column // lanes).astype(BF16)
     sides = lax.dot_general(packed, pick, NN, preferred_element_type=F32).astype(BF16)
-    cols = jnp.concatenate(
+    cols[...] = jnp.concatenate(
         [
             jnp.concatenate([sides[at : at + cells, :lanes], sides[at : at + cells, lanes:]], axis=0)
             for at in range(0, sides.shape[0], cells)
         ],
         axis=1,
     )
-    added = added + lax.dot_general(col_patterns[...], cols, NN, preferred_element_type=F32)
-    summed = totals[...] + added
-    half = keep.shape[0]
-    keep[...] = summed[:half]
-    send[:half, :] = summed[half:]
+    half = totals[0].shape[0]
+    for chunk, total, send in zip(chunks, totals, sends):
+        send[:half, :] = with_edges(chunk, total, rows, cols, row_patterns, col_patterns)
     squares = energy[...] + (low * low + high * high).reshape(-1, TILE, lanes).sum(axis=0)
     across = both * both
     for at in range(0, 4 * days, lanes):
         squares = squares + across[:, at : at + lanes].reshape(-1, TILE, lanes).sum(axis=0)
-    if last:
-        send[half:, :] = jnp.zeros((TILE, send.shape[1]), F32)
-        send[half:, :lanes] = squares
-    else:
-        more[0][...] = squares
-
-
-def edge(chunk, last, place, totals, before, after, near_rows, paired, other, edge_cols, coefs,
+    sends[-1][half:, :] = jnp.zeros((TILE, sends[-1].shape[1]), F32)
+    sends[-1][half:, :lanes] = squares
+
+
+def keep_kernel(chunks, rows, cols, row_patterns, col_patterns, *refs):
+    totals, keeps = refs[: len(chunks)], refs[len(chunks) :]
+    for chunk, total, keep in zip(chunks, totals, keeps):
+        keep[...] = with_edges(chunk, total, rows, cols, row_patterns, col_patterns)
+
+
+def half_specs(arrays, part):
+    return [pl.BlockSpec((a.shape[0] // 2, a.shape[1]), lambda s: (part, 0)) for a in arrays]
+
+
+def edge(chunks, place, totals, before, after, near_rows, paired, other, edge_cols, coefs,
          row_patterns, col_patterns, energy):
-    start, size = chunk
-    at = start // size
-    modes = totals.shape[0]
+    half = totals[0].shape[0] // 2
     cells, lanes = coefs.shape[1:]
-    half = modes // 2
+    days = before.shape[0]
     whole = lambda a: pl.BlockSpec(a.shape, lambda s: (0,) * a.ndim)
-    outs = [like(half, size), like(half + TILE * last, size)]
-    if not last:
-        outs.append(like(TILE, lanes))
-    return pl.pallas_call(
-        functools.partial(edge_kernel, last),
+    outs = [like(days, 2 * lanes, dtype=BF16), like(2 * cells, days, dtype=BF16)]
+    outs += [like(half + TILE * (i == len(chunks) - 1), size) for i, (_, size) in enumerate(chunks)]
+    wholes = (before, after, near_rows, paired, other, edge_cols, coefs)
+    patterns = (row_patterns, col_patterns)
+    rows, cols, *sends = pl.pallas_call(
+        functools.partial(send_kernel, chunks),
         grid=(1,),
         out_shape=outs,
-        in_specs=[
-            SMEM,
-            whole(totals),
-            pl.BlockSpec((size, lanes), lambda s: (at, 0)),
-            pl.BlockSpec((size, lanes), lambda s: (at, 0)),
-            pl.BlockSpec((2, size, lanes), lambda s: (0, at, 0)),
-            pl.BlockSpec((cells, 2 * size), lambda s: (0, at)),
-            pl.BlockSpec((cells, 2 * size), lambda s: (0, at)),
-            pl.BlockSpec((cells, 4 * size), lambda s: (0, at)),
-            whole(coefs),
-            whole(row_patterns),
-            whole(col_patterns),
-            whole(energy),
-        ],
+        in_specs=[SMEM]
+        + [whole(a) for a in wholes]
+        + half_specs(patterns, 1)
+        + [whole(energy)]
+        + half_specs(totals, 1),
         out_specs=[whole(a) for a in outs],
         compiler_params=params(),
-    )(place, totals, before, after, near_rows, paired, other, edge_cols, coefs, row_patterns,
-      col_patterns, energy)
+    )(place, *wholes, *patterns, energy, *totals)
+    keeps = [like(half, size) for _, size in chunks]
+    keeps = pl.pallas_call(
+        functools.partial(keep_kernel, chunks),
+        grid=(1,),
+        out_shape=keeps,
+        in_specs=[whole(rows), whole(cols)] + half_specs(patterns, 0) + half_specs(totals, 0),
+        out_specs=[whole(a) for a in keeps],
+        compiler_params=params(),
+    )(rows, cols, *patterns, *totals)
+    return keeps, sends
 
 
 def covariance_kernel(cells_total, chunks, place, order, energy, *refs):
@@ -470,15 +483,11 @@
     pairs.append([(i, ((i + 1) ^ 1) - 1) for i in range(1, lat_devices - 1)])
     paired, other = (lax.ppermute(sent_cols, "lat", pair) for pair in pairs)
 
-    chains = []
-    for i, chunk in enumerate(chunks):
-        last = i == len(chunks) - 1
-        keep, send, *more = edge(
-            chunk, last, place, totals[i], before, after, near_rows, paired, other, edge_cols,
-            coefs, row_patterns, col_patterns, energy,
-        )
-        chains.append(exchanges(keep, send, steps))
-        energy = more[0] if more else energy
+    keeps, sends = edge(
+        chunks, place, totals, before, after, near_rows, paired, other, edge_cols, coefs,
+        row_patterns, col_patterns, energy,
+    )
+    chains = [exchanges(keep, send, steps) for keep, send in zip(keeps, sends)]
     results = side_by_side(chains)
     parts = [part for found, _ in results for part in found]
     energy = results[-1][1][:, :LANES]

time: 87 us -> 86 us (0.989)
  transfers between devices with their start and end apart: 24 -> 24, of which waited for: 13 -> 13; matrix products, arithmetic and copies ran while one was open for 1% -> 1% of each run, Pallas kernels for 18% -> 19%
where the time goes in v5:
time: 86 us; the launch traced here: 85.6 us
  starting transfers between devices  39.5 us (46%)
  Pallas kernels  23 us (27%)
  waiting for transfers between devices  22 us (26%)
    ppermute x20, starting transfers between devices, side_by_side(): got[i] = lax.ppermute(send, BOTH, step)  29.5 us
    ppermute x20, waiting for transfers between devices, side_by_side(): got[i] = lax.ppermute(send, BOTH, step)  20.7 us
    pallas_call x1, Pallas kernels, interior(): pl.pallas_call(functools.partial(interior_kernel, chunks), grid=(blocks +...  15.9 us
    ppermute x1, starting transfers between devices, on_device(): before = lax.ppermute(last, 'lon', up)  4.9 us
    ppermute x2, starting transfers between devices, on_device(): paired, other = (lax.ppermute(sent_cols, 'lat', pair) for pair in pairs)  3.76 us
    pallas_call x1, Pallas kernels, covariance(): pl.pallas_call(functools.partial(covariance_kernel, cells_total, chunks),...  2.86 us
    pallas_call x1, Pallas kernels, edge_rows(): pl.pallas_call(edge_rows_kernel, out_shape=[like(days, lanes)] * 2, in_sp...  2.23 us
  transfers between devices with their start and end apart: 24, of which 13 were waited for; matrix products, arithmetic and copies ran while one was open for 1% of the time, Pallas kernels for 19%

profile of v5, /device:TPU:0, one launch (start us, length us, event | category | flops | bytes accessed | tf_op | source)
XLA Modules:
  0.0 85.6 jit_solution(5799747686305661862)
XLA Ops:
  0.0 0.0 copy-start
  0.0 2.2 %shard_map.37 = (f32[1024,128]{1,0:T(8,128)}, f32[1024,128]{1,0:T(8,128)}) custom-call(f32[1024,16,128]{2,1,0:T(8,128)} %height.1), custom_call_target="tpu_custom_call" | custom-call | tf_op jit(solution)/shard_map/pallas_call | solution.py:63
  2.2 4.9 %collective-permute-start = (f32[1024,128]{1,0:T(8,128)}, f32[1024,128]{1,0:T(8,128)S(1)}, u32[]{:S(2)}, u32[]{:S(2)}) collective-permute-start(f32[1024,128]{1,0:T(8,128)} %get-tuple-element.21), channel_id=1, source_target_pairs={{0,4},{4,8},{8,12},{12,16},{16,20},{20,24},{24,28},{1,5},{5,9},{9,... | collective-permute-start | bytes 1572872 | tf_op jit(solution)/shard_map/ppermute | solution.py:470
  7.2 1.3 %collective-permute-start.1 = (f32[1024,128]{1,0:T(8,128)}, f32[1024,128]{1,0:T(8,128)S(1)}, u32[]{:S(2)}, u32[]{:S(2)}) collective-permute-start(f32[1024,128]{1,0:T(8,128)} %get-tuple-element.22), channel_id=1, source_target_pairs={{4,0},{8,4},{12,8},{16,12},{20,16},{24,20},{28,24},{5,1},{9,5},{13... | collective-permute-start | bytes 1572872 | tf_op jit(solution)/shard_map/ppermute | solution.py:471
  8.5 0.1 multiply_divide_fusion
  8.5 0.0 copy-done
  8.6 0.1 stack.88.order
  8.7 15.9 %shard_map.38 = (f32[512,512]{1,0:T(8,128)S(1)}, f32[512,512]{1,0:T(8,128)S(1)}, f32[8,128]{1,0:T(8,128)S(1)}, f32[2,1024,128]{2,1,0:T(8,128)S(1)}, f32[16,4096]...) custom-call(s32[16]{0:T(128)S(1)} %stack.88.order, ...), custom_call_target="tpu_custom_call" | custom-call | flops 4026531840 | bytes 14680064 | tf_op jit(solution)/shard_map/pallas_call | solution.py:218
  24.6 0.8 collective-permute-start.3
  25.5 2.9 %collective-permute-start.2 = (f32[16,2048]{1,0:T(8,128)S(1)}, f32[16,2048]{1,0:T(8,128)S(1)}, u32[]{:S(2)}, u32[]{:S(2)}) collective-permute-start(f32[16,2048]{1,0:T(8,128)S(1)} %get-tuple-element.24), channel_id=1, source_target_pairs={{0,1},{1,0},{2,3},{3,2},{4,5},{5,4},{6,7},{7,6},{8,9},{9,8},{10,11... | collective-permute-start | bytes 393224 | tf_op jit(solution)/shard_map/ppermute | solution.py:484
  28.4 0.1 pad_add_fusion.place
  28.5 0.0 collective-permute-done.3.other
  28.5 0.9 %collective-permute-done.2.paired = f32[16,2048]{1,0:T(8,128)S(1)} collective-permute-done((f32[16,2048]{1,0:T(8,128)S(1)}, f32[16,2048]{1,0:T(8,128)S(1)}, u32[]{:S(2)}, u32[]{:S(2)}) %collective-permute-start.2) | collective-permute-done | bytes 131104 | tf_op jit(solution)/shard_map/ppermute | solution.py:484
  29.4 0.4 collective-permute-done.before
  29.8 0.0 collective-permute-done.1.after
  29.8 1.6 %shard_map.39 = (bf16[1024,256]{1,0:T(8,128)(2,1)S(1)}, bf16[32,1024]{1,0:T(8,128)(2,1)S(1)}, f32[256,512]{1,0:T(8,128)S(1)}, f32[264,512]{1,0:T(8,128)S(1)}) custom-call(s32[2]{0:T(128)S(1)} %pad_add_fusion.place, f32[1024,128]{1,0:T(8,128)S(1)} %collective-permute-done.before, f32[1024,128]{1,0:T(8,128)S(1)} %collective-permute-done.1.after, ...), custom_call_target="tpu_custom_call" | custom-call | tf_op jit(solution)/shard_map/pallas_call | solution.py:333
  31.5 1.0 %collective-permute-start.4 = (f32[264,512]{1,0:T(8,128)S(1)}, f32[264,512]{1,0:T(8,128)S(1)}, u32[]{:S(2)}, u32[]{:S(2)}) collective-permute-start(f32[264,512]{1,0:T(8,128)S(1)} %get-tuple-element.34), channel_id=1, source_target_pairs={{0,1},{1,0},{2,3},{3,2},{4,5},{5,4},{6,7},{7,6},{8,9},{9,8},{10,11... | collective-permute-start | bytes 1622024 | tf_op jit(solution)/shard_map/ppermute | solution.py:450
  32.5 0.1 collective-permute-start.9
  32.6 0.4 shard_map.40
  33.0 1.1 %collective-permute-done.4 = f32[264,512]{1,0:T(8,128)S(1)} collective-permute-done((f32[264,512]{1,0:T(8,128)S(1)}, f32[264,512]{1,0:T(8,128)S(1)}, u32[]{:S(2)}, u32[]{:S(2)}) %collective-permute-start.4) | collective-permute-done | bytes 540704 | tf_op jit(solution)/shard_map/ppermute | solution.py:450
  34.1 0.1 slice_add_fusion.3
  34.2 2.1 %collective-permute-start.5 = (f32[136,512]{1,0:T(8,128)S(1)}, f32[136,512]{1,0:T(8,128)S(1)}, u32[]{:S(2)}, u32[]{:S(2)}) collective-permute-start(f32[136,512]{1,0:T(8,128)S(1)} %pad_maximum_fusion), channel_id=1, source_target_pairs={{0,2},{1,9},{2,0},{3,11},{4,6},{5,13},{6,4},{7,15},{8,10},{9,1},{1... | collective-permute-start | bytes 835592 | tf_op jit(solution)/shard_map/ppermute | solution.py:450
  36.2 0.0 collective-permute-done.9
  36.2 0.1 slice_add_fusion.1
  36.3 0.6 collective-permute-start.10
  37.0 3.8 %collective-permute-done.5 = f32[136,512]{1,0:T(8,128)S(1)} collective-permute-done((f32[136,512]{1,0:T(8,128)S(1)}, f32[136,512]{1,0:T(8,128)S(1)}, u32[]{:S(2)}, u32[]{:S(2)}) %collective-permute-start.5) | collective-permute-done | bytes 278560 | tf_op jit(solution)/shard_map/ppermute | solution.py:450
  40.9 2.7 %collective-permute-start.6 = (f32[72,512]{1,0:T(8,128)S(1)}, f32[72,512]{1,0:T(8,128)S(1)}, u32[]{:S(2)}, u32[]{:S(2)}) collective-permute-start(f32[72,512]{1,0:T(8,128)S(1)} %pad_maximum_fusion.3), channel_id=1, source_target_pairs={{0,4},{1,3},{2,6},{3,1},{4,0},{5,7},{6,2},{7,5},{8,12},{9,11},{10,... | collective-permute-start | bytes 442376 | tf_op jit(solution)/shard_map/ppermute | solution.py:450
  43.6 0.0 collective-permute-done.10
  43.7 3.2 %collective-permute-start.11 = (f32[64,512]{1,0:T(8,128)S(1)}, f32[64,512]{1,0:T(8,128)S(1)}, u32[]{:S(2)}, u32[]{:S(2)}) collective-permute-start(f32[64,512]{1,0:T(8,128)S(1)} %get-tuple-element.44), channel_id=1, source_target_pairs={{0,4},{1,3},{2,6},{3,1},{4,0},{5,7},{6,2},{7,5},{8,12},{9,11},{10,... | collective-permute-start | bytes 393224 | tf_op jit(solution)/shard_map/ppermute | solution.py:450
  46.8 0.0 collective-permute-done.6
  46.9 2.9 %collective-permute-start.7 = (f32[40,512]{1,0:T(8,128)S(1)}, f32[40,512]{1,0:T(8,128)S(1)}, u32[]{:S(2)}, u32[]{:S(2)}) collective-permute-start(f32[40,512]{1,0:T(8,128)S(1)} %pad_maximum_fusion.6), channel_id=1, source_target_pairs={{0,8},{1,5},{2,10},{3,7},{4,12},{5,1},{6,14},{7,3},{8,0},{9,13},{1... | collective-permute-start | bytes 245768 | tf_op jit(solution)/shard_map/ppermute | solution.py:450
  49.8 0.7 collective-permute-done.11
  50.5 3.5 %collective-permute-start.12 = (f32[32,512]{1,0:T(8,128)S(1)}, f32[32,512]{1,0:T(8,128)S(1)}, u32[]{:S(2)}, u32[]{:S(2)}) collective-permute-start(f32[32,512]{1,0:T(8,128)S(1)} %slice_add_fusion.8), channel_id=1, source_target_pairs={{0,8},{1,5},{2,10},{3,7},{4,12},{5,1},{6,14},{7,3},{8,0},{9,13},{1... | collective-permute-start | bytes 196616 | tf_op jit(solution)/shard_map/ppermute | solution.py:450
  54.0 0.0 collective-permute-done.7
  54.0 2.6 %collective-permute-start.8 = (f32[40,512]{1,0:T(8,128)S(1)}, f32[40,512]{1,0:T(8,128)S(1)}, u32[]{:S(2)}, u32[]{:S(2)}) collective-permute-start(f32[40,512]{1,0:T(8,128)S(1)} %pad_maximum_fusion.7), channel_id=1, source_target_pairs={{0,16},{1,17},{2,18},{3,19},{4,20},{5,21},{6,22},{7,23},{8,24},{9,... | collective-permute-start | bytes 245768 | tf_op jit(solution)/shard_map/ppermute | solution.py:450
  56.7 0.4 collective-permute-done.12
  57.0 2.3 %collective-permute-start.13 = (f32[32,512]{1,0:T(8,128)S(1)}, f32[32,512]{1,0:T(8,128)S(1)}, u32[]{:S(2)}, u32[]{:S(2)}) collective-permute-start(f32[32,512]{1,0:T(8,128)S(1)} %fusion), channel_id=1, source_target_pairs={{0,16},{1,17},{2,18},{3,19},{4,20},{5,21},{6,22},{7,23},{8,24},{9,... | collective-permute-start | bytes 196616 | tf_op jit(solution)/shard_map/ppermute | solution.py:450
  59.3 2.9 %collective-permute-done.13 = f32[32,512]{1,0:T(8,128)S(1)} collective-permute-done((f32[32,512]{1,0:T(8,128)S(1)}, f32[32,512]{1,0:T(8,128)S(1)}, u32[]{:S(2)}, u32[]{:S(2)}) %collective-permute-start.13) | collective-permute-done | bytes 65568 | tf_op jit(solution)/shard_map/ppermute | solution.py:450
  62.3 1.9 %collective-permute-start.14 = (f32[32,512]{1,0:T(8,128)S(1)}, f32[32,512]{1,0:T(8,128)S(1)}, u32[]{:S(2)}, u32[]{:S(2)}) collective-permute-start(f32[32,512]{1,0:T(8,128)S(1)} %add.192), channel_id=1, source_target_pairs={{0,8},{1,5},{2,10},{3,7},{4,12},{5,1},{6,14},{7,3},{8,0},{9,13},{1... | collective-permute-start | bytes 196616 | tf_op jit(solution)/shard_map/ppermute | solution.py:450
  64.2 0.0 collective-permute-done.8
  64.2 0.3 collective-permute-start.19
  64.5 2.1 %collective-permute-done.14 = f32[32,512]{1,0:T(8,128)S(1)} collective-permute-done((f32[32,512]{1,0:T(8,128)S(1)}, f32[32,512]{1,0:T(8,128)S(1)}, u32[]{:S(2)}, u32[]{:S(2)}) %collective-permute-start.14) | collective-permute-done | bytes 65568 | tf_op jit(solution)/shard_map/ppermute | solution.py:450
  66.6 0.8 collective-permute-start.15
  67.4 1.1 %collective-permute-done.19 = f32[32,512]{1,0:T(8,128)S(1)} collective-permute-done((f32[32,512]{1,0:T(8,128)S(1)}, f32[32,512]{1,0:T(8,128)S(1)}, u32[]{:S(2)}, u32[]{:S(2)}) %collective-permute-start.19) | collective-permute-done | bytes 65568 | tf_op jit(solution)/shard_map/ppermute | solution.py:450
  68.5 0.7 collective-permute-start.20
  69.2 2.4 %collective-permute-done.15 = f32[64,512]{1,0:T(8,128)S(1)} collective-permute-done((f32[64,512]{1,0:T(8,128)S(1)}, f32[64,512]{1,0:T(8,128)S(1)}, u32[]{:S(2)}, u32[]{:S(2)}) %collective-permute-start.15) | collective-permute-done | bytes 131104 | tf_op jit(solution)/shard_map/ppermute | solution.py:450
  71.7 2.3 %collective-permute-start.16 = (f32[128,512]{1,0:T(8,128)S(1)}, f32[128,512]{1,0:T(8,128)S(1)}, u32[]{:S(2)}, u32[]{:S(2)}) collective-permute-start(f32[128,512]{1,0:T(8,128)S(1)} %pad_maximum_fusion.1.refs_0_), channel_id=1, source_target_pairs={{0,2},{1,9},{2,0},{3,11},{4,6},{5,13},{6,4},{7,15},{8,10},{9,1},{1... | collective-permute-start | bytes 786440 | tf_op jit(solution)/shard_map/ppermute | solution.py:450
  74.0 0.0 collective-permute-done.20
  74.0 2.1 %collective-permute-start.21 = (f32[128,512]{1,0:T(8,128)S(1)}, f32[128,512]{1,0:T(8,128)S(1)}, u32[]{:S(2)}, u32[]{:S(2)}) collective-permute-start(f32[128,512]{1,0:T(8,128)S(1)} %pad_maximum_fusion.2.refs_4_), channel_id=1, source_target_pairs={{0,2},{1,9},{2,0},{3,11},{4,6},{5,13},{6,4},{7,15},{8,10},{9,1},{1... | collective-permute-start | bytes 786440 | tf_op jit(solution)/shard_map/ppermute | solution.py:450
  76.1 0.0 collective-permute-start.17
  76.1 0.5 collective-permute-start.22
  76.6 1.7 %collective-permute-done.16.refs_1_ = f32[128,512]{1,0:T(8,128)S(1)} collective-permute-done((f32[128,512]{1,0:T(8,128)S(1)}, f32[128,512]{1,0:T(8,128)S(1)}, u32[]{:S(2)}, u32[]{:S(2)}) %collective-permute-start.16) | collective-permute-done | bytes 262176 | tf_op jit(solution)/shard_map/ppermute | solution.py:450
  78.4 0.0 collective-permute-start.18
  78.4 2.8 %collective-permute-done.21.refs_5_ = f32[128,512]{1,0:T(8,128)S(1)} collective-permute-done((f32[128,512]{1,0:T(8,128)S(1)}, f32[128,512]{1,0:T(8,128)S(1)}, u32[]{:S(2)}, u32[]{:S(2)}) %collective-permute-start.21) | collective-permute-done | bytes 262176 | tf_op jit(solution)/shard_map/ppermute | solution.py:450
  81.2 0.0 collective-permute-start.23
  81.2 0.0 collective-permute-done.17.refs_2_
  81.2 0.0 collective-permute-done.22.refs_6_
  81.2 0.0 collective-permute-done.18.refs_3_
  81.2 1.5 %collective-permute-done.23.refs_7_ = f32[128,512]{1,0:T(8,128)S(1)} collective-permute-done((f32[128,512]{1,0:T(8,128)S(1)}, f32[128,512]{1,0:T(8,128)S(1)}, u32[]{:S(2)}, u32[]{:S(2)}) %collective-permute-start.23) | collective-permute-done | bytes 262176 | tf_op jit(solution)/shard_map/ppermute | solution.py:450
  82.7 2.9 %shard_map.41 = f32[1,128,512]{2,1,0:T(8,128)} custom-call(s32[2]{0:T(128)S(1)} %pad_add_fusion.place, s32[16]{0:T(128)S(1)} %stack.88.order, f32[8,128]{1,0:T(8,128)S(1)} %slice.145.energy, f32[128,512]{1,0:T(8,128)S(1)} %pad_maximum_fusion.1.refs_0_, f32[128,512]{1,0:T(8,128)S(1)} %collective-permute-done.16.refs_1_, ...), custom_call_target="tpu_custom_call" | custom-call | tf_op jit(solution)/shard_map/pallas_call | solution.py:392
  (24 shorter events, 0.3 us)
Async XLA Ops:
  0.0 8.5 %copy-start = (s32[16,128]{1,0:T(8,128)S(1)}, s32[16,128]{1,0:T(8,128)}, u32[]{:S(2)}) copy-start(s32[16,128]{1,0:T(8,128)} %param.4) | copy-start | bytes 24580
  2.2 27.6 %collective-permute-start = (f32[1024,128]{1,0:T(8,128)}, f32[1024,128]{1,0:T(8,128)S(1)}, u32[]{:S(2)}, u32[]{:S(2)}) collective-permute-start(f32[1024,128]{1,0:T(8,128)} %get-tuple-element.21), channel_id=1, source_target_pairs={{0,4},{4,8},{8,12},{12,16},{16,20},{20,24},{24,28},{1,5},{5,9},{9,... | collective-permute-start | bytes 1572872 | tf_op jit(solution)/shard_map/ppermute | solution.py:470
  7.2 22.7 %collective-permute-start.1 = (f32[1024,128]{1,0:T(8,128)}, f32[1024,128]{1,0:T(8,128)S(1)}, u32[]{:S(2)}, u32[]{:S(2)}) collective-permute-start(f32[1024,128]{1,0:T(8,128)} %get-tuple-element.22), channel_id=1, source_target_pairs={{4,0},{8,4},{12,8},{16,12},{20,16},{24,20},{28,24},{5,1},{9,5},{13... | collective-permute-start | bytes 1572872 | tf_op jit(solution)/shard_map/ppermute | solution.py:471
  24.6 3.8 %collective-permute-start.3 = (f32[16,2048]{1,0:T(8,128)S(1)}, f32[16,2048]{1,0:T(8,128)S(1)}, u32[]{:S(2)}, u32[]{:S(2)}) collective-permute-start(f32[16,2048]{1,0:T(8,128)S(1)} %get-tuple-element.24), channel_id=1, source_target_pairs={{1,2},{2,1},{5,6},{6,5},{9,10},{10,9},{13,14},{14,13},{17,18},{18,... | collective-permute-start | bytes 393224 | tf_op jit(solution)/shard_map/ppermute | solution.py:484
  25.5 3.9 %collective-permute-start.2 = (f32[16,2048]{1,0:T(8,128)S(1)}, f32[16,2048]{1,0:T(8,128)S(1)}, u32[]{:S(2)}, u32[]{:S(2)}) collective-permute-start(f32[16,2048]{1,0:T(8,128)S(1)} %get-tuple-element.24), channel_id=1, source_target_pairs={{0,1},{1,0},{2,3},{3,2},{4,5},{5,4},{6,7},{7,6},{8,9},{9,8},{10,11... | collective-permute-start | bytes 393224 | tf_op jit(solution)/shard_map/ppermute | solution.py:484
  31.5 2.6 %collective-permute-start.4 = (f32[264,512]{1,0:T(8,128)S(1)}, f32[264,512]{1,0:T(8,128)S(1)}, u32[]{:S(2)}, u32[]{:S(2)}) collective-permute-start(f32[264,512]{1,0:T(8,128)S(1)} %get-tuple-element.34), channel_id=1, source_target_pairs={{0,1},{1,0},{2,3},{3,2},{4,5},{5,4},{6,7},{7,6},{8,9},{9,8},{10,11... | collective-permute-start | bytes 1622024 | tf_op jit(solution)/shard_map/ppermute | solution.py:450
  32.5 3.7 %collective-permute-start.9 = (f32[256,512]{1,0:T(8,128)S(1)}, f32[256,512]{1,0:T(8,128)S(1)}, u32[]{:S(2)}, u32[]{:S(2)}) collective-permute-start(f32[256,512]{1,0:T(8,128)S(1)} %get-tuple-element.36), channel_id=1, source_target_pairs={{0,1},{1,0},{2,3},{3,2},{4,5},{5,4},{6,7},{7,6},{8,9},{9,8},{10,11... | collective-permute-start | bytes 1572872 | tf_op jit(solution)/shard_map/ppermute | solution.py:450
  34.2 6.6 %collective-permute-start.5 = (f32[136,512]{1,0:T(8,128)S(1)}, f32[136,512]{1,0:T(8,128)S(1)}, u32[]{:S(2)}, u32[]{:S(2)}) collective-permute-start(f32[136,512]{1,0:T(8,128)S(1)} %pad_maximum_fusion), channel_id=1, source_target_pairs={{0,2},{1,9},{2,0},{3,11},{4,6},{5,13},{6,4},{7,15},{8,10},{9,1},{1... | collective-permute-start | bytes 835592 | tf_op jit(solution)/shard_map/ppermute | solution.py:450
  36.3 7.3 %collective-permute-start.10 = (f32[128,512]{1,0:T(8,128)S(1)}, f32[128,512]{1,0:T(8,128)S(1)}, u32[]{:S(2)}, u32[]{:S(2)}) collective-permute-start(f32[128,512]{1,0:T(8,128)S(1)} %get-tuple-element.40), channel_id=1, source_target_pairs={{0,2},{1,9},{2,0},{3,11},{4,6},{5,13},{6,4},{7,15},{8,10},{9,1},{1... | collective-permute-start | bytes 786440 | tf_op jit(solution)/shard_map/ppermute | solution.py:450
  40.9 6.0 %collective-permute-start.6 = (f32[72,512]{1,0:T(8,128)S(1)}, f32[72,512]{1,0:T(8,128)S(1)}, u32[]{:S(2)}, u32[]{:S(2)}) collective-permute-start(f32[72,512]{1,0:T(8,128)S(1)} %pad_maximum_fusion.3), channel_id=1, source_target_pairs={{0,4},{1,3},{2,6},{3,1},{4,0},{5,7},{6,2},{7,5},{8,12},{9,11},{10,... | collective-permute-start | bytes 442376 | tf_op jit(solution)/shard_map/ppermute | solution.py:450
  43.7 6.8 %collective-permute-start.11 = (f32[64,512]{1,0:T(8,128)S(1)}, f32[64,512]{1,0:T(8,128)S(1)}, u32[]{:S(2)}, u32[]{:S(2)}) collective-permute-start(f32[64,512]{1,0:T(8,128)S(1)} %get-tuple-element.44), channel_id=1, source_target_pairs={{0,4},{1,3},{2,6},{3,1},{4,0},{5,7},{6,2},{7,5},{8,12},{9,11},{10,... | collective-permute-start | bytes 393224 | tf_op jit(solution)/shard_map/ppermute | solution.py:450
  46.9 7.1 %collective-permute-start.7 = (f32[40,512]{1,0:T(8,128)S(1)}, f32[40,512]{1,0:T(8,128)S(1)}, u32[]{:S(2)}, u32[]{:S(2)}) collective-permute-start(f32[40,512]{1,0:T(8,128)S(1)} %pad_maximum_fusion.6), channel_id=1, source_target_pairs={{0,8},{1,5},{2,10},{3,7},{4,12},{5,1},{6,14},{7,3},{8,0},{9,13},{1... | collective-permute-start | bytes 245768 | tf_op jit(solution)/shard_map/ppermute | solution.py:450
  50.5 6.5 %collective-permute-start.12 = (f32[32,512]{1,0:T(8,128)S(1)}, f32[32,512]{1,0:T(8,128)S(1)}, u32[]{:S(2)}, u32[]{:S(2)}) collective-permute-start(f32[32,512]{1,0:T(8,128)S(1)} %slice_add_fusion.8), channel_id=1, source_target_pairs={{0,8},{1,5},{2,10},{3,7},{4,12},{5,1},{6,14},{7,3},{8,0},{9,13},{1... | collective-permute-start | bytes 196616 | tf_op jit(solution)/shard_map/ppermute | solution.py:450
  54.0 10.2 %collective-permute-start.8 = (f32[40,512]{1,0:T(8,128)S(1)}, f32[40,512]{1,0:T(8,128)S(1)}, u32[]{:S(2)}, u32[]{:S(2)}) collective-permute-start(f32[40,512]{1,0:T(8,128)S(1)} %pad_maximum_fusion.7), channel_id=1, source_target_pairs={{0,16},{1,17},{2,18},{3,19},{4,20},{5,21},{6,22},{7,23},{8,24},{9,... | collective-permute-start | bytes 245768 | tf_op jit(solution)/shard_map/ppermute | solution.py:450
  57.0 5.2 %collective-permute-start.13 = (f32[32,512]{1,0:T(8,128)S(1)}, f32[32,512]{1,0:T(8,128)S(1)}, u32[]{:S(2)}, u32[]{:S(2)}) collective-permute-start(f32[32,512]{1,0:T(8,128)S(1)} %fusion), channel_id=1, source_target_pairs={{0,16},{1,17},{2,18},{3,19},{4,20},{5,21},{6,22},{7,23},{8,24},{9,... | collective-permute-start | bytes 196616 | tf_op jit(solution)/shard_map/ppermute | solution.py:450
  62.3 4.3 %collective-permute-start.14 = (f32[32,512]{1,0:T(8,128)S(1)}, f32[32,512]{1,0:T(8,128)S(1)}, u32[]{:S(2)}, u32[]{:S(2)}) collective-permute-start(f32[32,512]{1,0:T(8,128)S(1)} %add.192), channel_id=1, source_target_pairs={{0,8},{1,5},{2,10},{3,7},{4,12},{5,1},{6,14},{7,3},{8,0},{9,13},{1... | collective-permute-start | bytes 196616 | tf_op jit(solution)/shard_map/ppermute | solution.py:450
  64.2 4.3 %collective-permute-start.19 = (f32[32,512]{1,0:T(8,128)S(1)}, f32[32,512]{1,0:T(8,128)S(1)}, u32[]{:S(2)}, u32[]{:S(2)}) collective-permute-start(f32[32,512]{1,0:T(8,128)S(1)} %slice.156), channel_id=1, source_target_pairs={{0,8},{1,5},{2,10},{3,7},{4,12},{5,1},{6,14},{7,3},{8,0},{9,13},{1... | collective-permute-start | bytes 196616 | tf_op jit(solution)/shard_map/ppermute | solution.py:450
  66.6 5.0 %collective-permute-start.15 = (f32[64,512]{1,0:T(8,128)S(1)}, f32[64,512]{1,0:T(8,128)S(1)}, u32[]{:S(2)}, u32[]{:S(2)}) collective-permute-start(f32[64,512]{1,0:T(8,128)S(1)} %pad_maximum_fusion.4), channel_id=1, source_target_pairs={{0,4},{1,3},{2,6},{3,1},{4,0},{5,7},{6,2},{7,5},{8,12},{9,11},{10,... | collective-permute-start | bytes 393224 | tf_op jit(solution)/shard_map/ppermute | solution.py:450
  68.5 5.5 %collective-permute-start.20 = (f32[64,512]{1,0:T(8,128)S(1)}, f32[64,512]{1,0:T(8,128)S(1)}, u32[]{:S(2)}, u32[]{:S(2)}) collective-permute-start(f32[64,512]{1,0:T(8,128)S(1)} %pad_maximum_fusion.5), channel_id=1, source_target_pairs={{0,4},{1,3},{2,6},{3,1},{4,0},{5,7},{6,2},{7,5},{8,12},{9,11},{10,... | collective-permute-start | bytes 393224 | tf_op jit(solution)/shard_map/ppermute | solution.py:450
  71.7 6.7 %collective-permute-start.16 = (f32[128,512]{1,0:T(8,128)S(1)}, f32[128,512]{1,0:T(8,128)S(1)}, u32[]{:S(2)}, u32[]{:S(2)}) collective-permute-start(f32[128,512]{1,0:T(8,128)S(1)} %pad_maximum_fusion.1.refs_0_), channel_id=1, source_target_pairs={{0,2},{1,9},{2,0},{3,11},{4,6},{5,13},{6,4},{7,15},{8,10},{9,1},{1... | collective-permute-start | bytes 786440 | tf_op jit(solution)/shard_map/ppermute | solution.py:450
  74.0 7.1 %collective-permute-start.21 = (f32[128,512]{1,0:T(8,128)S(1)}, f32[128,512]{1,0:T(8,128)S(1)}, u32[]{:S(2)}, u32[]{:S(2)}) collective-permute-start(f32[128,512]{1,0:T(8,128)S(1)} %pad_maximum_fusion.2.refs_4_), channel_id=1, source_target_pairs={{0,2},{1,9},{2,0},{3,11},{4,6},{5,13},{6,4},{7,15},{8,10},{9,1},{1... | collective-permute-start | bytes 786440 | tf_op jit(solution)/shard_map/ppermute | solution.py:450
  76.1 5.0 %collective-permute-start.17 = (f32[128,512]{1,0:T(8,128)S(1)}, f32[128,512]{1,0:T(8,128)S(1)}, u32[]{:S(2)}, u32[]{:S(2)}) collective-permute-start(f32[128,512]{1,0:T(8,128)S(1)} %pad_maximum_fusion.1.refs_0_), channel_id=1, source_target_pairs={{0,1},{1,0},{2,3},{3,2},{4,5},{5,4},{6,7},{7,6},{8,9},{9,8},{10,11... | collective-permute-start | bytes 786440 | tf_op jit(solution)/shard_map/ppermute | solution.py:450
  76.1 5.1 %collective-permute-start.22 = (f32[128,512]{1,0:T(8,128)S(1)}, f32[128,512]{1,0:T(8,128)S(1)}, u32[]{:S(2)}, u32[]{:S(2)}) collective-permute-start(f32[128,512]{1,0:T(8,128)S(1)} %pad_maximum_fusion.2.refs_4_), channel_id=1, source_target_pairs={{0,1},{1,0},{2,3},{3,2},{4,5},{5,4},{6,7},{7,6},{8,9},{9,8},{10,11... | collective-permute-start | bytes 786440 | tf_op jit(solution)/shard_map/ppermute | solution.py:450
  78.4 2.8 %collective-permute-start.18 = (f32[128,512]{1,0:T(8,128)S(1)}, f32[128,512]{1,0:T(8,128)S(1)}, u32[]{:S(2)}, u32[]{:S(2)}) collective-permute-start(f32[128,512]{1,0:T(8,128)S(1)} %collective-permute-done.16.refs_1_), channel_id=1, source_target_pairs={{0,1},{1,0},{2,3},{3,2},{4,5},{5,4},{6,7},{7,6},{8,9},{9,8},{10,11... | collective-permute-start | bytes 786440 | tf_op jit(solution)/shard_map/ppermute | solution.py:450
  81.2 1.5 %collective-permute-start.23 = (f32[128,512]{1,0:T(8,128)S(1)}, f32[128,512]{1,0:T(8,128)S(1)}, u32[]{:S(2)}, u32[]{:S(2)}) collective-permute-start(f32[128,512]{1,0:T(8,128)S(1)} %collective-permute-done.21.refs_5_), channel_id=1, source_target_pairs={{0,1},{1,0},{2,3},{3,2},{4,5},{5,4},{6,7},{7,6},{8,9},{9,8},{10,11... | collective-permute-start | bytes 786440 | tf_op jit(solution)/shard_map/ppermute | solution.py:450
